TPU v7x, 32 devices: a whole 2x2x4 slice. The times are simulated.
32 devices in a mesh: seq: 4 (over x, core), shard: 8 (over z, y).
Axes of the slice: x: 2, y: 2, z: 4, core: 2. Of those that a mesh axis runs over, the one named last changes fastest.
Arguments:
- tokens: bfloat16 [8, 1536, 768], P('shard', 'seq'), may hold values from -8 to 8
- route_residual: float32 [8, 1536, 8], P('shard', 'seq'), may hold values from -3 to 3
- doc_lengths: int32 [8, 8], P('shard'), may hold values from 1 to 1153, 1536 in all within a row
- routes: int32 [8, 1536, 2], P('shard', 'seq'), may hold values from 0 to 7, all different within a row
- priority: int32 [8, 1536], P('shard', 'seq'), may hold values from 0 to 1535, each once within a row
- grad_out: bfloat16 [8, 1536, 768], P('shard', 'seq'), may hold values from -6 to 6
- attend_in: float32 [3, 768, 768], P(None, 'shard'), may hold values from -0.21875 to 0.21875
- attend_in_first: float32 [3, 768, 768], P(None, 'shard'), may hold values from -640 to 640
- attend_in_second: float32 [3, 768, 768], P(None, 'shard'), may hold values from 12288 to 49152
- attend_out: float32 [768, 768], P('shard'), may hold values from -0.75 to 0.75
- attend_out_first: float32 [768, 768], P('shard'), may hold values from -128 to 128
- attend_out_second: float32 [768, 768], P('shard'), may hold values from 491.52 to 1966.08
- expert_up: float32 [4, 768, 4096], P(None, 'shard'), may hold values from -0.21875 to 0.21875
- expert_up_first: float32 [4, 768, 4096], P(None, 'shard'), may hold values from -64 to 64
- expert_up_second: float32 [4, 768, 4096], P(None, 'shard'), may hold values from 122.88 to 491.52
- expert_down: float32 [4, 2048, 768], P(None, 'shard'), may hold values from -0.125 to 0.125
- expert_down_first: float32 [4, 2048, 768], P(None, 'shard'), may hold values from -96 to 96
- expert_down_second: float32 [4, 2048, 768], P(None, 'shard'), may hold values from 276.48 to 1105.92
- router_mix: float32 [768, 12], P('shard'), may hold values from -0.109375 to 0.109375
- router_mix_first: float32 [768, 12], P('shard'), may hold values from -2048 to 2048
- router_mix_second: float32 [768, 12], P('shard'), may hold values from 110592 to 442368
- vectors: float32 [4, 768], P(None, 'shard'), may hold values from 0.5 to 1.5
- vectors_first: float32 [4, 768], P(None, 'shard'), may hold values from -640 to 640
- vectors_second: float32 [4, 768], P(None, 'shard'), may hold values from 12288 to 49152
Outputs:
- layer_out: bfloat16 [8, 1536, 768], P('shard', 'seq')
- grad_tokens: float32 [8, 1536, 768], P('shard', 'seq')
- grad_route_residual: float32 [8, 1536, 8], P('shard', 'seq')
- attend_in_new: float32 [3, 768, 768], P(None, 'shard')
- attend_in_first_new: float32 [3, 768, 768], P(None, 'shard')
- attend_in_second_new: float32 [3, 768, 768], P(None, 'shard')
- attend_out_new: float32 [768, 768], P('shard')
- attend_out_first_new: float32 [768, 768], P('shard')
- attend_out_second_new: float32 [768, 768], P('shard')
- expert_up_new: float32 [4, 768, 4096], P(None, 'shard')
- expert_up_first_new: float32 [4, 768, 4096], P(None, 'shard')
- expert_up_second_new: float32 [4, 768, 4096], P(None, 'shard')
- expert_down_new: float32 [4, 2048, 768], P(None, 'shard')
- expert_down_first_new: float32 [4, 2048, 768], P(None, 'shard')
- expert_down_second_new: float32 [4, 2048, 768], P(None, 'shard')
- router_mix_new: float32 [768, 12], P('shard')
- router_mix_first_new: float32 [768, 12], P('shard')
- router_mix_second_new: float32 [768, 12], P('shard')
- vectors_new: float32 [4, 768], P(None, 'shard')
- vectors_first_new: float32 [4, 768], P(None, 'shard')
- vectors_second_new: float32 [4, 768], P(None, 'shard')
Inputs may be any that keep to these rules, and one draw needn't show every extreme that they name: `doc_lengths`: each stream's lengths sum to 1536; the longest is exactly 1153. `routes`: a token's two experts differ. `priority`: each stream's row is a permutation.
All inputs are finite; a program needn't handle non-finite values.
Results may differ from a plain program's by a relative error of at most 0.012.
Values may be sent and summed in bfloat16 or wider, within the bound.
A program may use at most 192 MiB of HBM per device.

v0:
```python
import jax
import jax.numpy as jnp
from jax import lax
from jax.sharding import PartitionSpec as P

D = 768
HEADS = 12
HEAD_DIM = 64
FF = 2048
NFFN = 4
NEXP = 8
TOPK = 2
STEP = 5
CAP = 96


NORM_EPSILON = 1e-05
ROPE_BASE = 10000.0
NEGATIVE = -1e30
HIGHEST = lax.Precision.HIGHEST
MOMENT_DECAY = 0.5
ADAM_EPSILON = 1e-08
STEP_RATES = (0.04, 0.1, 0.04, 0.02, 0.02, 0.2)
STEP_DECAYS = (0.1, 0.1, 0.1, 0.1, 0.1, 0.0)


def norm_rows(values, gain_row):
    scale_rows = lax.rsqrt(jnp.mean(values * values, axis=-1, keepdims=True) + NORM_EPSILON)
    return (values * scale_rows * gain_row, scale_rows)


def norm_back(grad_rows, values, scale_rows, gain_row):
    normal_rows = values * scale_rows
    grad_gain = jnp.sum(grad_rows * normal_rows, axis=0)
    inner_term = grad_rows * gain_row
    grad_input = scale_rows * (
        inner_term - normal_rows * jnp.mean(inner_term * normal_rows, axis=-1, keepdims=True)
    )
    return (grad_input, grad_gain)


def doc_layout(lengths, token_ids):
    starts = jnp.cumsum(lengths) - lengths
    inside = starts[None, :] <= token_ids[:, None]
    segment = jnp.sum(inside.astype(jnp.int32), axis=1)
    doc_begin = jnp.max(jnp.where(inside, starts[None, :], 0), axis=1)
    return (segment, token_ids - doc_begin)


def rope_tables(positions):
    frequency = ROPE_BASE ** (-(jnp.arange(HEAD_DIM // 2, dtype=jnp.float32) * 2.0 / HEAD_DIM))
    angles = positions.astype(jnp.float32)[:, None] * frequency[None, :]
    return (jnp.cos(angles), jnp.sin(angles))


def rotate(values, cosine, sine_table, direction):
    shaped = values.reshape(values.shape[0], -1, HEAD_DIM)
    front_half = shaped[..., : HEAD_DIM // 2]
    back_half = shaped[..., HEAD_DIM // 2 :]
    cos_rows = cosine[:, None, :]
    sin_rows = direction * sine_table[:, None, :]
    turned = jnp.concatenate(
        [
            front_half * cos_rows - back_half * sin_rows,
            back_half * cos_rows + front_half * sin_rows,
        ],
        axis=-1,
    )
    return turned.reshape(values.shape)


def block_scores(query_rows, key_heads, segment, offset, block_rows):
    scores = jnp.einsum(
        "qhd,khd->hqk", query_rows, key_heads, preferred_element_type=jnp.float32
    ) * HEAD_DIM ** (-0.5)
    row_ids = offset + jnp.arange(block_rows, dtype=jnp.int32)
    col_ids = jnp.arange(key_heads.shape[0], dtype=jnp.int32)
    row_seg = lax.dynamic_slice_in_dim(segment, offset, block_rows, 0)
    allowed = (row_seg[:, None] == segment[None, :]) & (col_ids[None, :] <= row_ids[:, None])
    return jnp.where(allowed[None], scores, NEGATIVE)


def split_heads(heads_in, local_heads):
    stream_len = heads_in.shape[1]
    return (
        heads_in[0].reshape(stream_len, local_heads, HEAD_DIM),
        heads_in[1].reshape(stream_len, local_heads, HEAD_DIM),
        heads_in[2].reshape(stream_len, local_heads, HEAD_DIM),
    )


def attention_forward(heads_in, segment, local_heads):
    stream_len = heads_in.shape[1]
    block_rows = min(512, stream_len)
    query_heads, key_heads, value_heads = split_heads(heads_in, local_heads)

    def one_block(running, offset):
        query_rows = lax.dynamic_slice_in_dim(query_heads, offset, block_rows, 0)
        scores = block_scores(query_rows, key_heads, segment, offset, block_rows)
        row_max = jnp.max(scores, axis=2, keepdims=True)
        exponent = jnp.exp(scores - row_max)
        row_total = jnp.sum(exponent, axis=2, keepdims=True)
        probabilities = (exponent / row_total).astype(jnp.bfloat16)
        result = jnp.einsum(
            "hqk,khd->qhd", probabilities, value_heads, preferred_element_type=jnp.float32
        )
        return (running, (result.astype(jnp.bfloat16), (row_max + jnp.log(row_total))[..., 0]))

    offsets = jnp.arange(0, stream_len, block_rows, dtype=jnp.int32)
    unused, (outputs, log_totals) = lax.scan(one_block, jnp.int32(0), offsets)
    return (outputs.reshape(stream_len, local_heads * HEAD_DIM), log_totals)


def attention_backward(heads_in, grad_heads, log_totals, segment, local_heads):
    stream_len = heads_in.shape[1]
    block_rows = min(512, stream_len)
    query_heads, key_heads, value_heads = split_heads(heads_in, local_heads)
    grad_rows = grad_heads.reshape(stream_len, local_heads, HEAD_DIM)
    scale_value = HEAD_DIM ** (-0.5)

    def one_block(running, inputs):
        offset, block_log = inputs
        grad_keys, grad_values = running
        query_rows = lax.dynamic_slice_in_dim(query_heads, offset, block_rows, 0)
        scores = block_scores(query_rows, key_heads, segment, offset, block_rows)
        probabilities = jnp.exp(scores - block_log[:, :, None])
        grad_block = lax.dynamic_slice_in_dim(grad_rows, offset, block_rows, 0)
        grad_probs = jnp.einsum(
            "qhd,khd->hqk", grad_block, value_heads, preferred_element_type=jnp.float32
        )
        delta_rows = jnp.sum(probabilities * grad_probs, axis=2, keepdims=True)
        grad_scores = (probabilities * (grad_probs - delta_rows)).astype(jnp.bfloat16)
        grad_query = (
            jnp.einsum("hqk,khd->qhd", grad_scores, key_heads, preferred_element_type=jnp.float32)
            * scale_value
        )
        grad_keys = (
            grad_keys
            + jnp.einsum(
                "hqk,qhd->khd", grad_scores, query_rows, preferred_element_type=jnp.float32
            )
            * scale_value
        )
        grad_values = grad_values + jnp.einsum(
            "hqk,qhd->khd",
            probabilities.astype(jnp.bfloat16),
            grad_block,
            preferred_element_type=jnp.float32,
        )
        return ((grad_keys, grad_values), grad_query)

    offsets = jnp.arange(0, stream_len, block_rows, dtype=jnp.int32)
    zero_rows = jnp.zeros((stream_len, local_heads, HEAD_DIM), jnp.float32)
    (grad_keys, grad_values), grad_query = lax.scan(
        one_block, (zero_rows, zero_rows), (offsets, log_totals)
    )
    width = local_heads * HEAD_DIM
    return jnp.stack(
        [
            grad_query.reshape(stream_len, width),
            grad_keys.reshape(stream_len, width),
            grad_values.reshape(stream_len, width),
        ]
    ).astype(jnp.bfloat16)


def pair_values(route_ids, ffn_rows, hidden_val, coefficient, vector_rows):
    const_zero = (
        coefficient[:, 0, 0:1] * hidden_val + coefficient[:, 0, 1:2] * vector_rows[2][None, :]
    )
    const_one = (
        coefficient[:, 1, 0:1] * hidden_val + coefficient[:, 1, 1:2] * vector_rows[3][None, :]
    )
    outputs = []
    for pick_index in range(TOPK):
        expert_col = route_ids[:, pick_index][:, None]
        result = jnp.where(expert_col < NFFN, ffn_rows[pick_index], 0.0)
        result = jnp.where(expert_col == NFFN + 1, hidden_val, result)
        result = jnp.where(expert_col == NFFN + 2, const_zero, result)
        result = jnp.where(expert_col == NFFN + 3, const_one, result)
        outputs.append(result)
    return outputs


def adam_update(weight, grad, first, second, rate, decay):
    first_new = MOMENT_DECAY * first + (1.0 - MOMENT_DECAY) * grad
    second_new = MOMENT_DECAY * second + (1.0 - MOMENT_DECAY) * grad * grad
    correction = 1.0 - MOMENT_DECAY**STEP
    update = first_new / correction / (jnp.sqrt(second_new / correction) + ADAM_EPSILON)
    return (weight - rate * (update + decay * weight), first_new, second_new)


def local(
    tokens,
    route_residual,
    doc_lengths,
    routes,
    priority,
    grad_out,
    attend_in,
    attend_in_first,
    attend_in_second,
    attend_out,
    attend_out_first,
    attend_out_second,
    expert_up,
    expert_up_first,
    expert_up_second,
    expert_down,
    expert_down_first,
    expert_down_second,
    router_mix,
    router_mix_first,
    router_mix_second,
    vectors,
    vectors_first,
    vectors_second,
):
    local_tokens = tokens.shape[1]
    seq_count = lax.axis_size("seq")
    stream_len = local_tokens * seq_count
    local_heads = HEADS // seq_count
    stream_ids = jnp.arange(stream_len, dtype=jnp.int32)
    segment, stream_pos = doc_layout(doc_lengths[0], stream_ids)
    local_pos = lax.dynamic_slice_in_dim(
        stream_pos, lax.axis_index("seq") * local_tokens, local_tokens, 0
    )
    cosine, sine_table = rope_tables(local_pos)
    w_in, w_out, w_router, w_vectors = (
        lax.all_gather(attend_in.astype(jnp.bfloat16), "shard", axis=1, tiled=True),
        lax.all_gather(attend_out.astype(jnp.bfloat16), "shard", axis=0, tiled=True),
        lax.all_gather(router_mix.astype(jnp.bfloat16), "shard", axis=0, tiled=True),
        lax.all_gather(vectors.astype(jnp.bfloat16), "shard", axis=1, tiled=True),
    )
    w_up, w_down = (
        lax.all_gather(expert_up.astype(jnp.bfloat16), "shard", axis=1, tiled=True),
        lax.all_gather(expert_down.astype(jnp.bfloat16), "shard", axis=1, tiled=True),
    )
    vector_rows = w_vectors.astype(jnp.float32)
    residual_in = tokens[0].astype(jnp.float32)
    normed, scale_one = norm_rows(residual_in, vector_rows[0])
    normed_low = normed.astype(jnp.bfloat16)
    raw = jnp.einsum("td,cde->cte", normed_low, w_in, preferred_element_type=jnp.float32)
    turned = jnp.stack(
        [rotate(raw[0], cosine, sine_table, 1.0), rotate(raw[1], cosine, sine_table, 1.0), raw[2]]
    ).astype(jnp.bfloat16)
    heads_in = lax.all_to_all(turned, "seq", split_axis=2, concat_axis=1, tiled=True)
    attended_heads, log_totals = attention_forward(heads_in, segment, local_heads)
    attended = lax.all_to_all(attended_heads, "seq", split_axis=0, concat_axis=1, tiled=True)
    branch = jnp.dot(attended, w_out, preferred_element_type=jnp.float32)
    middle = residual_in + branch
    hidden, scale_two = norm_rows(middle, vector_rows[1])
    hidden_low = hidden.astype(jnp.bfloat16)
    hidden_val = hidden_low.astype(jnp.float32)
    logits = jnp.dot(hidden_low, w_router, preferred_element_type=jnp.float32)
    route_ids = routes[0]
    route_logits = logits[:, :NEXP] + route_residual[0]
    onehot = (route_ids[:, :, None] == jnp.arange(NEXP, dtype=jnp.int32)[None, None, :]).astype(
        jnp.float32
    )
    picked = jnp.sum(onehot * route_logits[:, None, :], axis=2)
    gate_weights = jax.nn.softmax(picked, axis=-1)
    coefficient = jax.nn.softmax(logits[:, NEXP:].reshape(local_tokens, 2, 2), axis=-1)
    expert_id = route_ids.T.reshape(-1)
    order_key = (
        jnp.arange(TOPK, dtype=jnp.int32)[:, None] * stream_len + priority[0][None, :]
    ).reshape(-1)
    earlier = (expert_id[:, None] == expert_id[None, :]) & (order_key[None, :] < order_key[:, None])
    slot_rank = jnp.sum(earlier.astype(jnp.int32), axis=1)
    kept_pair = (expert_id < NFFN) & (slot_rank < CAP)
    flat_slot = jnp.where(kept_pair, expert_id * CAP + slot_rank, -1)
    dispatch = (jnp.arange(NFFN * CAP, dtype=jnp.int32)[:, None] == flat_slot[None, :]).astype(
        jnp.float32
    )
    token_map = jnp.sum(dispatch.reshape(NFFN * CAP, TOPK, local_tokens), axis=1)
    buffer_rows = (
        jnp.dot(token_map.astype(jnp.bfloat16), hidden_low, preferred_element_type=jnp.float32)
        .astype(jnp.bfloat16)
        .reshape(NFFN, CAP, D)
    )
    up_proj = jnp.einsum("ecd,edf->ecf", buffer_rows, w_up, preferred_element_type=jnp.float32)
    gate_part = up_proj[..., :FF]
    lin_part = up_proj[..., FF:]
    silu_part = jax.nn.silu(gate_part)
    activated = (silu_part * lin_part).astype(jnp.bfloat16)
    down_work = jnp.einsum("ecf,efd->ecd", activated, w_down, preferred_element_type=jnp.float32)
    down_proj = down_work.reshape(NFFN * CAP, D)
    safe_slot = jnp.maximum(flat_slot, 0)
    ffn_rows = (
        jnp.take(down_proj, safe_slot, axis=0) * kept_pair[:, None].astype(jnp.float32)
    ).reshape(TOPK, local_tokens, D)
    values_list = pair_values(route_ids, ffn_rows, hidden_val, coefficient, vector_rows)
    mixture = gate_weights[:, 0:1] * values_list[0] + gate_weights[:, 1:2] * values_list[1]
    layer_out = (middle + mixture).astype(jnp.bfloat16)[None]
    w_in, w_out, w_router, w_vectors = (
        lax.all_gather(attend_in.astype(jnp.bfloat16), "shard", axis=1, tiled=True),
        lax.all_gather(attend_out.astype(jnp.bfloat16), "shard", axis=0, tiled=True),
        lax.all_gather(router_mix.astype(jnp.bfloat16), "shard", axis=0, tiled=True),
        lax.all_gather(vectors.astype(jnp.bfloat16), "shard", axis=1, tiled=True),
    )
    w_up, w_down = (
        lax.all_gather(expert_up.astype(jnp.bfloat16), "shard", axis=1, tiled=True),
        lax.all_gather(expert_down.astype(jnp.bfloat16), "shard", axis=1, tiled=True),
    )
    grad_top = grad_out[0].astype(jnp.float32)
    grad_gate = jnp.stack(
        [jnp.sum(grad_top * pair_value, axis=1) for pair_value in values_list], axis=1
    )
    grad_pick = gate_weights * (
        grad_gate - jnp.sum(gate_weights * grad_gate, axis=1, keepdims=True)
    )
    grad_route = jnp.sum(onehot * grad_pick[:, :, None], axis=1)
    copy_weight = jnp.sum(gate_weights * (route_ids == NFFN + 1).astype(jnp.float32), axis=1)
    grad_hidden = copy_weight[:, None] * grad_top
    grad_mix_list = []
    grad_vec_list = []
    for const_index in range(2):
        weight_const = jnp.sum(
            gate_weights * (route_ids == NFFN + 2 + const_index).astype(jnp.float32), axis=1
        )
        vec_row = vector_rows[2 + const_index]
        coef_row = coefficient[:, const_index]
        grad_hidden = grad_hidden + (weight_const * coef_row[:, 0])[:, None] * grad_top
        grad_coef = jnp.stack(
            [
                weight_const * jnp.sum(grad_top * hidden_val, axis=1),
                weight_const * jnp.sum(grad_top * vec_row[None, :], axis=1),
            ],
            axis=1,
        )
        grad_mix_list.append(
            coef_row * (grad_coef - jnp.sum(coef_row * grad_coef, axis=1, keepdims=True))
        )
        grad_vec_list.append(jnp.sum((weight_const * coef_row[:, 1])[:, None] * grad_top, axis=0))
    grad_logits = jnp.concatenate([grad_route, grad_mix_list[0], grad_mix_list[1]], axis=1)
    pair_grad = jnp.concatenate(
        [gate_weights[:, pick_index : pick_index + 1] * grad_top for pick_index in range(TOPK)],
        axis=0,
    )
    grad_down = (
        jnp.dot(dispatch, pair_grad, precision=HIGHEST).astype(jnp.bfloat16).reshape(NFFN, CAP, D)
    )
    grad_act = jnp.einsum("ecd,efd->ecf", grad_down, w_down, preferred_element_type=jnp.float32)
    sigma = jax.nn.sigmoid(gate_part)
    grad_up = jnp.concatenate(
        [grad_act * lin_part * sigma * (1.0 + gate_part * (1.0 - sigma)), grad_act * silu_part],
        axis=2,
    ).astype(jnp.bfloat16)
    grad_w_down = jnp.einsum(
        "ecf,ecd->efd", activated, grad_down, preferred_element_type=jnp.float32
    )
    grad_w_up = jnp.einsum("ecd,ecf->edf", buffer_rows, grad_up, preferred_element_type=jnp.float32)
    buffer_grad_work = jnp.einsum("ecf,edf->ecd", grad_up, w_up, preferred_element_type=jnp.float32)
    grad_buffer = buffer_grad_work.reshape(NFFN * CAP, D)
    grad_hidden = grad_hidden + jnp.einsum("st,sd->td", token_map, grad_buffer, precision=HIGHEST)
    grad_hidden = grad_hidden + jnp.einsum(
        "te,de->td", grad_logits, w_router.astype(jnp.float32), precision=HIGHEST
    )
    grad_w_router = jnp.einsum("td,te->de", hidden_val, grad_logits, precision=HIGHEST)
    grad_norm_two, grad_gain_two = norm_back(grad_hidden, middle, scale_two, vector_rows[1])
    grad_middle = grad_top + grad_norm_two
    grad_branch = grad_middle.astype(jnp.bfloat16)
    grad_w_out = jnp.einsum("td,te->de", attended, grad_branch, preferred_element_type=jnp.float32)
    grad_attended = jnp.einsum(
        "te,de->td", grad_branch, w_out, preferred_element_type=jnp.float32
    ).astype(jnp.bfloat16)
    grad_heads = lax.all_to_all(grad_attended, "seq", split_axis=1, concat_axis=0, tiled=True)
    grad_turned = attention_backward(heads_in, grad_heads, log_totals, segment, local_heads)
    grad_local = lax.all_to_all(grad_turned, "seq", split_axis=1, concat_axis=2, tiled=True).astype(
        jnp.float32
    )
    grad_raw = jnp.stack(
        [
            rotate(grad_local[0], cosine, sine_table, -1.0),
            rotate(grad_local[1], cosine, sine_table, -1.0),
            grad_local[2],
        ]
    ).astype(jnp.bfloat16)
    grad_w_in = jnp.einsum("td,cte->cde", normed_low, grad_raw, preferred_element_type=jnp.float32)
    grad_normed = jnp.einsum("cte,cde->td", grad_raw, w_in, preferred_element_type=jnp.float32)
    grad_norm_one, grad_gain_one = norm_back(grad_normed, residual_in, scale_one, vector_rows[0])
    grad_tokens = (grad_middle + grad_norm_one)[None]
    grad_vectors = jnp.stack([grad_gain_one, grad_gain_two, grad_vec_list[0], grad_vec_list[1]])
    small_shares = (
        lax.psum_scatter(grad_w_in, "shard", scatter_dimension=1, tiled=True),
        lax.psum_scatter(grad_w_out, "shard", scatter_dimension=0, tiled=True),
        lax.psum_scatter(grad_w_router, "shard", scatter_dimension=0, tiled=True),
        lax.psum_scatter(grad_vectors, "shard", scatter_dimension=1, tiled=True),
    )
    up_share, down_share = (
        lax.psum_scatter(grad_w_up, "shard", scatter_dimension=1, tiled=True),
        lax.psum_scatter(grad_w_down, "shard", scatter_dimension=1, tiled=True),
    )
    summed = lax.psum(
        (small_shares[0], small_shares[1], up_share, down_share, small_shares[2], small_shares[3]),
        "seq",
    )
    masters = (attend_in, attend_out, expert_up, expert_down, router_mix, vectors)
    firsts = (
        attend_in_first,
        attend_out_first,
        expert_up_first,
        expert_down_first,
        router_mix_first,
        vectors_first,
    )
    seconds = (
        attend_in_second,
        attend_out_second,
        expert_up_second,
        expert_down_second,
        router_mix_second,
        vectors_second,
    )
    results = []
    for kind_index in range(6):
        results.extend(
            adam_update(
                masters[kind_index],
                summed[kind_index],
                firsts[kind_index],
                seconds[kind_index],
                STEP_RATES[kind_index],
                STEP_DECAYS[kind_index],
            )
        )
    return (
        layer_out,
        grad_tokens,
        grad_route[None],
        results[0],
        results[1],
        results[2],
        results[3],
        results[4],
        results[5],
        results[6],
        results[7],
        results[8],
        results[9],
        results[10],
        results[11],
        results[12],
        results[13],
        results[14],
        results[15],
        results[16],
        results[17],
    )


def solution(mesh):
    placed = (
        P("shard", "seq", None),
        P("shard", "seq", None),
        P("shard", None),
        P("shard", "seq", None),
        P("shard", "seq"),
        P("shard", "seq", None),
        P(None, "shard", None),
        P(None, "shard", None),
        P(None, "shard", None),
        P("shard", None),
        P("shard", None),
        P("shard", None),
        P(None, "shard", None),
        P(None, "shard", None),
        P(None, "shard", None),
        P(None, "shard", None),
        P(None, "shard", None),
        P(None, "shard", None),
        P("shard", None),
        P("shard", None),
        P("shard", None),
        P(None, "shard"),
        P(None, "shard"),
        P(None, "shard"),
    )
    return jax.shard_map(
        local,
        mesh=mesh,
        in_specs=placed,
        out_specs=(
            P("shard", "seq", None),
            P("shard", "seq", None),
            P("shard", "seq", None),
            P(None, "shard", None),
            P(None, "shard", None),
            P(None, "shard", None),
            P("shard", None),
            P("shard", None),
            P("shard", None),
            P(None, "shard", None),
            P(None, "shard", None),
            P(None, "shard", None),
            P(None, "shard", None),
            P(None, "shard", None),
            P(None, "shard", None),
            P("shard", None),
            P("shard", None),
            P("shard", None),
            P(None, "shard"),
            P(None, "shard"),
            P(None, "shard"),
        ),
        check_vma=False,
    )
```

profile of v0, /device:TPU:0, one launch (start us, length us, event | category | flops | bytes accessed | tf_op | source)
XLA Modules:
  0.0 2805.1 jit_solution(4132626531344485833)
XLA Ops:
  10.1 4.9 convert_element_type.139
  18.2 22.5 all-gather
  43.0 35.8 %all-gather.7.cloned.1.call-done = bf16[3,768,768]{2,1,0:T(8,128)(2,1)} async-done(((bf16[3,96,768]{2,1,0:T(8,128)(2,1)}), bf16[3,768,768]{2,1,0:T(8,128)(2,1)}) %all-gather.7.cloned.1.call-update) | async-done | bytes 3538960 | tf_op jit(solution)/shard_map/all_gather | solution.py:230
  78.8 3.6 convolution_bitcast_fusion.1
  86.8 3.3 copy.192
  90.1 3.8 all-to-all-start
  93.9 30.9 %all-gather.1 = bf16[8,96,12]{1,2,0:T(8,128)(2,1)S(1)} all-gather(bf16[1,96,12]{1,2,0:T(8,128)(2,1)S(1)} %convert_bitcast_fusion), channel_id=1, replica_groups=mesh['seq'=4,'shard'=8] {'shard'}, dimensions={0}, use_global_device_ids=true | all-gather | bytes 20736 | tf_op jit(solution)/shard_map/all_gather | solution.py:232
  131.2 41.7 %while.27 = (s32[]{:T(128)}, bf16[3,512,3,64]{1,3,2,0:T(8,128)(2,1)S(1)}, f32[3,3,512]{2,1,0:T(4,128)}, s32[3]{0:T(128)}, s32[1536]{0:T(1024)S(1)}, /*index=5*/b...) while((s32[]{:T(128)}, ...), condition=%wide.region_7.8_spmd, body=%wide.region_4.7_spmd.sunk | while | flops 634747904 | bytes 33102008 | solution.py:110
  138.1 2.8 fusion.181
  140.9 3.6 fusion.182
  151.9 2.8 fusion.181
  154.7 3.6 fusion.182
  165.8 2.8 fusion.181
  168.6 3.6 fusion.182
  178.9 4.0 all-to-all-start.1
  185.1 7.2 all-to-all-done.1
  205.2 2.6 fusion.49
  208.3 394.3 %all-gather.11.cloned.1.call-done = bf16[4,768,4096]{2,1,0:T(8,128)(2,1)} async-done(((bf16[4,96,4096]{2,1,0:T(8,128)(2,1)}), bf16[4,768,4096]{2,1,0:T(8,128)(2,1)}) %all-gather.11.cloned.1.call-update) | async-done | bytes 25165840 | tf_op jit(solution)/shard_map/all_gather | solution.py:236
  602.6 15.0 fusion.123
  617.6 164.1 %all-gather.13.cloned.1.call-done = bf16[4,2048,768]{2,1,0:T(8,128)(2,1)} async-done(((bf16[4,256,768]{2,1,0:T(8,128)(2,1)}), bf16[4,2048,768]{2,1,0:T(8,128)(2,1)}) %all-gather.13.cloned.1.call-update) | async-done | bytes 12582928 | tf_op jit(solution)/shard_map/all_gather | solution.py:237
  781.7 14.8 multiply_convert_fusion.2
  796.4 7.1 fusion.124
  803.5 3.8 gather_fusion
  809.8 3.7 fusion.67
  815.4 13.9 fusion.43
  829.4 5.0 multiply_reduce_fusion.1
  838.5 4.3 all-to-all-start.2
  842.9 9.5 all-to-all-done.2
  857.2 107.2 %while.28 = (s32[]{:T(128)}, f32[1536,3,64]{0,2,1:T(8,128)S(1)}, f32[1536,3,64]{0,2,1:T(8,128)S(1)}, bf16[3,512,3,64]{1,3,2,0:T(8,128)(2,1)}, s32[3]{0:T(128)S(1...) while((s32[]{:T(128)}, f32[1536,3,64]{0,2,1:T(8,128)S(1)}, ...), condition=%wide.region_31.32_spmd.clone, body=%wide.region_29.31_spmd.clone.sunk | while | flops 1535114240 | bytes 136690128 | solution.py:154
  859.7 2.5 fusion.192
  864.6 7.7 multiply_reduce_fusion.8
  872.3 9.4 multiply_convert_fusion.6
  881.8 3.7 fusion.194
  885.5 5.1 fusion.195
  895.5 2.5 fusion.192
  900.3 7.7 multiply_reduce_fusion.8
  908.1 9.4 multiply_convert_fusion.6
  917.5 3.7 fusion.194
  921.2 5.1 fusion.195
  936.1 7.7 multiply_reduce_fusion.8
  943.8 9.4 multiply_convert_fusion.6
  953.2 3.6 fusion.194
  956.9 5.1 fusion.195
  968.2 4.1 copy.203
  972.3 40.5 %all_to_all.59 = bf16[3,1536,192]{2,0,1:T(4,128)(2,1)} all-to-all(bf16[3,1536,192]{2,0,1:T(4,128)(2,1)S(1)} %copy.203), channel_id=1, replica_groups=mesh['seq'=4,'shard'=8] {'seq'}, dimensions={1} | all-to-all | bytes 3538944 | tf_op jit(solution)/shard_map/all_to_all | solution.py:369
  1012.8 5.8 copy.214
  1028.0 5.0 convolution_bitcast_fusion
  1033.0 11.0 copy.215
  1044.0 8.3 copy.224
  1057.7 11.3 fusion.125
  1070.0 22.7 fusion.42
  1095.4 5.0 fusion.58
  1101.5 77.3 %reduce-scatter.19.cloned.1.call-done = f32[96,2304]{1,0:T(8,128)} async-done(((f32[768,2304]{1,0:T(8,128)}), f32[96,2304]{1,0:T(8,128)}) %reduce-scatter.19.cloned.1.call-update) | async-done | bytes 884752
  1181.5 70.0 %reduce-scatter.13.cloned.1.call-done = f32[96,768]{1,0:T(8,128)} async-done(((f32[768,768]{1,0:T(8,128)}), f32[96,768]{1,0:T(8,128)}) %reduce-scatter.13.cloned.1.call-update) | async-done | bytes 294928 | tf_op jit(solution)/shard_map/reduce_scatter | solution.py:386
  1251.4 407.3 %reduce-scatter.17.cloned.1.call-done = f32[4,256,768]{2,1,0:T(8,128)} async-done(((f32[4,2048,768]{2,1,0:T(8,128)}), f32[4,256,768]{2,1,0:T(8,128)}) %reduce-scatter.17.cloned.1.call-update) | async-done | bytes 3145744 | tf_op jit(solution)/shard_map/reduce_scatter | solution.py:392
  1658.7 793.3 %reduce-scatter.15.cloned.1.call-done = f32[4,96,4096]{2,1,0:T(8,128)} async-done(((f32[4,768,4096]{2,1,0:T(8,128)}), f32[4,96,4096]{2,1,0:T(8,128)}) %reduce-scatter.15.cloned.1.call-update) | async-done | bytes 6291472 | tf_op jit(solution)/shard_map/reduce_scatter | solution.py:391
  2452.0 64.4 %reduce-scatter.21.cloned.1.call-done = f32[96,12]{1,0:T(8,128)} async-done(((f32[768,12]{1,0:T(8,128)}), f32[96,12]{1,0:T(8,128)}) %reduce-scatter.21.cloned.1.call-update) | async-done | bytes 4624
  2517.3 2.9 fusion.57
  2520.2 60.2 %reduce-scatter.23.cloned.1.call-done = f32[96,4]{1,0:T(8,128)} async-done(((f32[768,4]{1,0:T(8,128)}), f32[96,4]{1,0:T(8,128)}) %reduce-scatter.23.cloned.1.call-update) | async-done | bytes 1552
  2581.3 10.3 all-reduce
  2592.9 180.0 %all-reduce.4.cloned.1.call-done = (f32[3,96,768]{2,1,0:T(8,128)}, f32[96,768]{1,0:T(8,128)}, f32[4,96,4096]{2,1,0:T(8,128)}, f32[4,256,768]{2,1,0:T(8,128)}) async-done(((f32[3,96,768]{2,1,0:T(8,128)}, f32[96,768]{1,0:T(8,128)}, f32[4,96,4096]{2,1,0:T(8,128)}, f32[4,256,768]{2,1,0:T(8,128)}), (f32[3,96,768]{2,1,0:T(8,128)}, f32[96,768]{1,0:T(8,128)}, f32[4,96,4096]{2,1,0:T(8,128)}, ...) | async-done | bytes 10616848 | tf_op jit(solution)/shard_map/psum | solution.py:394
  2773.0 4.1 multiply_subtract_fusion.2
  2778.1 13.4 multiply_subtract_fusion
  2791.5 6.8 multiply_subtract_fusion.1
  (447 shorter events, 117.9 us)
Async XLA Ops:
  7.2 71.6 %all-gather.7.cloned.1.call-start = ((), (), s32[]{:S(2)}) async-start(), calls=%async_computation.10 | async-start | bytes 3981312 | tf_op jit(solution)/shard_map/all_gather | solution.py:230
  9.3 175.8 %all-gather.9.cloned.1.call-start = ((), (), s32[]{:S(2)}) async-start(), calls=%async_computation.11 | async-start | bytes 1327104 | tf_op jit(solution)/shard_map/all_gather | solution.py:231
  10.0 592.6 %all-gather.11.cloned.1.call-start = ((), (), s32[]{:S(2)}) async-start(), calls=%async_computation.12 | async-start | bytes 28311552 | tf_op jit(solution)/shard_map/all_gather | solution.py:236
  15.0 25.8 copy-start.107
  15.1 766.6 %all-gather.13.cloned.1.call-start = ((), (), s32[]{:S(2)}) async-start(), calls=%async_computation.13 | async-start | bytes 14155776 | tf_op jit(solution)/shard_map/all_gather | solution.py:237
  18.2 23.7 copy-start.18
  41.9 40.5 %copy-start.80 = (f32[768]{0:T(1024)}, f32[768]{0:T(1024)S(1)}, u32[]{:S(2)}) copy-start(f32[768]{0:T(1024)S(1)} %get-tuple-element.283) | copy-start | bytes 9220
  41.9 153.5 %copy-start.47 = (f32[768]{0:T(1024)}, f32[768]{0:T(1024)S(1)}, u32[]{:S(2)}) copy-start(f32[768]{0:T(1024)S(1)} %get-tuple-element.282) | copy-start | bytes 9220
  42.1 40.3 %copy-start.89 = (f32[384]{0:T(512)}, f32[384]{0:T(512)S(1)}, u32[]{:S(2)}) copy-start(f32[384]{0:T(512)S(1)} %add_rsqrt_fusion.1) | copy-start | bytes 4612
  90.1 35.5 %copy-start.106 = (s32[1,384]{1,0:T(1,128)S(1)}, s32[1,384]{1,0:T(1,128)}, u32[]{:S(2)}) copy-start(s32[1,384]{1,0:T(1,128)} %param.32) | copy-start | bytes 4612
  90.1 35.6 %copy-start.43 = (s32[1,384,2]{1,2,0:T(2,128)S(1)}, s32[1,384,2]{1,2,0:T(2,128)}, u32[]{:S(2)}) copy-start(s32[1,384,2]{1,2,0:T(2,128)} %param.31) | copy-start | bytes 9220
  90.1 38.5 %all-to-all-start = ((bf16[3,384,768]{1,0,2:T(4,128)(2,1)}), bf16[3,384,768]{1,0,2:T(4,128)(2,1)S(1)}, u32[]{:S(2)}, u32[]{:S(2)}) async-start(bf16[3,384,768]{1,0,2:T(4,128)(2,1)} %copy.192), calls=%async_computation | async-start | bytes 4718592 | tf_op jit(solution)/shard_map/all_to_all | solution.py:247
  173.7 5.2 copy-start.3
  175.5 7.4 copy-start.79
  175.5 8.0 copy-start.82
  176.8 7.7 copy-start.52
  176.8 7.7 copy-start.54
  176.8 16.4 copy-start.19
  178.9 13.5 all-to-all-start.1
  195.3 9.6 copy-start.8
  196.0 11.8 copy-start.10
  200.2 5.0 copy-start.95
  208.3 409.3 %copy-start.1 = (bf16[384,768]{1,0:T(8,128)(2,1)}, bf16[384,768]{1,0:T(8,128)(2,1)S(1)}, u32[]{:S(2)}) copy-start(bf16[384,768]{1,0:T(8,128)(2,1)S(1)} %convolution_convert_fusion.1) | copy-start | bytes 1769476
  602.6 179.1 %copy-start.35 = (bf16[384,768]{1,0:T(8,128)(2,1)S(1)}, bf16[384,768]{1,0:T(8,128)(2,1)}, u32[]{:S(2)}) copy-start(bf16[384,768]{1,0:T(8,128)(2,1)} %fusion.49) | copy-start | bytes 1769476
  815.4 14.0 copy-start.14
  815.4 14.0 copy-start.49
  815.4 14.0 copy-start.57
  829.3 5.0 copy-start.15
  829.4 5.0 copy-start.16
  829.4 5.0 copy-start.71
  829.4 5.0 copy-start.73
  838.5 18.7 copy-start.108
  838.5 13.9 all-to-all-start.2
  842.8 336.0 %reduce-scatter.19.cloned.1.call-start = ((), (), s32[]{:S(2)}) async-start(), calls=%async_computation.17 | async-start | bytes 7962624
  862.2 10.1 copy-start
  881.7 8.8 slice-start
  885.4 5.1 slice-start.1
  885.4 5.1 copy-start.32
  898.0 10.1 copy-start
  917.5 8.8 slice-start
  921.2 5.1 slice-start.1
  921.2 5.1 copy-start.32
  933.7 10.0 copy-start
  953.2 8.7 slice-start
  956.9 5.1 slice-start.1
  956.9 5.1 copy-start.32
  1026.9 6.0 copy-start.29
  1028.0 5.0 copy-start.30
  1052.3 199.1 %reduce-scatter.13.cloned.1.call-start = ((), (), s32[]{:S(2)}) async-start(), calls=%async_computation.14 | async-start | bytes 2654208 | tf_op jit(solution)/shard_map/reduce_scatter | solution.py:386
  1055.9 602.7 %reduce-scatter.17.cloned.1.call-start = ((), (), s32[]{:S(2)}) async-start(), calls=%async_computation.16 | async-start | bytes 28311552 | tf_op jit(solution)/shard_map/reduce_scatter | solution.py:392
  1069.0 1383.0 %reduce-scatter.15.cloned.1.call-start = ((), (), s32[]{:S(2)}) async-start(), calls=%async_computation.15 | async-start | bytes 56623104 | tf_op jit(solution)/shard_map/reduce_scatter | solution.py:391
  1092.8 1423.6 %reduce-scatter.21.cloned.1.call-start = ((), (), s32[]{:S(2)}) async-start(), calls=%async_computation.18 | async-start | bytes 442368
  1095.4 1485.1 %reduce-scatter.23.cloned.1.call-start = ((), (), s32[]{:S(2)}) async-start(), calls=%async_computation.19 | async-start | bytes 442368
  1101.4 1671.5 %all-reduce.4.cloned.1.call-start = ((), (), s32[]{:S(2)}) async-start(), calls=%async_computation.20 | async-start | bytes 21233664 | tf_op jit(solution)/shard_map/psum | solution.py:394
  2517.2 74.4 %copy-start.94 = (f32[4,96]{1,0:T(4,128)S(1)}, f32[4,96]{1,0:T(4,128)}, u32[]{:S(2)}) copy-start(f32[4,96]{1,0:T(4,128)} %param.49) | copy-start | bytes 4612
  2517.2 74.4 %copy-start.104 = (f32[4,96]{1,0:T(4,128)S(1)}, f32[4,96]{1,0:T(4,128)}, u32[]{:S(2)}) copy-start(f32[4,96]{1,0:T(4,128)} %param.50) | copy-start | bytes 4612
  2517.3 74.4 %copy-start.105 = (f32[4,96]{1,0:T(4,128)S(1)}, f32[4,96]{1,0:T(4,128)}, u32[]{:S(2)}) copy-start(f32[4,96]{1,0:T(4,128)} %param.51) | copy-start | bytes 4612
  2517.3 75.0 %copy-start.61 = (f32[96,12]{0,1:T(8,128)S(1)}, f32[96,12]{0,1:T(8,128)}, u32[]{:S(2)}) copy-start(f32[96,12]{0,1:T(8,128)} %param.46) | copy-start | bytes 13828
  2517.3 75.0 %copy-start.91 = (f32[96,12]{0,1:T(8,128)S(1)}, f32[96,12]{0,1:T(8,128)}, u32[]{:S(2)}) copy-start(f32[96,12]{0,1:T(8,128)} %param.47) | copy-start | bytes 13828
  2517.3 75.0 %copy-start.92 = (f32[96,12]{0,1:T(8,128)S(1)}, f32[96,12]{0,1:T(8,128)}, u32[]{:S(2)}) copy-start(f32[96,12]{0,1:T(8,128)} %param.48) | copy-start | bytes 13828
  2517.3 260.8 %slice-start.2 = ((s8[6291456]{0:T(1024)(128)(4,1)}), s8[2097152]{0:T(1024)(128)(4,1)S(1)}, s32[]{:S(2)}) async-start(s8[6291456]{0:T(1024)(128)(4,1)} %bitcast.226), calls=%async_computation.23 | async-start | bytes 4194304
  2773.0 4.1 copy-start.39
  2773.0 5.2 slice-start.3
  2778.1 13.4 copy-start.7
  (76 other events, 159.3 us)
Sparse Core Ops, SparseCore 0:
  10.8 67.9 all-gather.6
  81.6 39.6 all-gather.8
  123.3 479.2 all-gather.10
  605.2 176.3 all-gather.12
  1052.5 126.2 reduce-scatter.18
  1183.1 68.2 reduce-scatter.12
  1255.8 402.8 reduce-scatter.16
  1663.0 788.8 reduce-scatter.14
  2455.8 60.5 reduce-scatter.20
  2520.1 60.3 reduce-scatter.22
  2583.9 189.0 all-reduce.3
where the time goes:
time: 2810 us
  waiting for transfers between devices  2260 us (80%)
  matrix products  193 us (7%)
  other arithmetic  111 us (4%)
  blocking collectives  104 us (4%)
  local copies, waits for them, and re-layouts  92.5 us (3%)
    reduce_scatter x1, waiting for transfers between devices, local(): lax.psum_scatter(grad_w_up, 'shard', scatter_dimension=1, tiled=True)  793 us
    reduce_scatter x1, waiting for transfers between devices, local(): lax.psum_scatter(grad_w_down, 'shard', scatter_dimension=1, tiled=True)  407 us
    all_gather x1, waiting for transfers between devices, local(): lax.all_gather(expert_up.astype(jnp.bfloat16), 'shard', axis=1, tiled=True)  394 us
    unnamed x14, waiting for transfers between devices  202 us
    psum x1, waiting for transfers between devices, local(): lax.psum((small_shares[0], small_shares[1], up_share, down_share, small_s...  180 us
    all_gather x1, waiting for transfers between devices, local(): lax.all_gather(expert_down.astype(jnp.bfloat16), 'shard', axis=1, tiled=T...  164 us
    reduce_scatter x1, waiting for transfers between devices, local(): lax.psum_scatter(grad_w_out, 'shard', scatter_dimension=0, tiled=True)  70 us
  transfers between devices with their start and end apart: 14, of which 12 were waited for; matrix products, arithmetic and copies ran while one was open for 5% of the time, Pallas kernels for 0%

commit v1 on v0

v1 whole, which is shorter than its diff:
```python
import functools

import jax
import jax.numpy as jnp
import numpy as np
from jax import lax
from jax.experimental import pallas as pl
from jax.experimental.pallas import tpu as pltpu
from jax.sharding import PartitionSpec as P

D = 768
HEADS = 12
HEAD_DIM = 64
FF = 2048
NFFN = 4
NEXP = 8
TOPK = 2
STEP = 5
CAP = 96
LINE = 4
OUTER = 8
LOCAL_HEADS = 3

NORM_EPSILON = 1e-05
ROPE_BASE = 10000.0
NEGATIVE = -1e30
MOMENT_DECAY = 0.5
ADAM_EPSILON = 1e-08
STEP_RATES = (0.04, 0.1, 0.04, 0.02, 0.02, 0.2)
STEP_DECAYS = (0.1, 0.1, 0.1, 0.1, 0.1, 0.0)
BF = jnp.bfloat16
F32 = jnp.float32
MESH = pl.DeviceIdType.MESH
VMEM_LIMIT = 48 * 2**20


def mm(left, right):
    return jnp.dot(left, right, preferred_element_type=F32)


def mm_nt(left, right):
    return lax.dot_general(left, right, (((1,), (1,)), ((), ())), preferred_element_type=F32)


def mm_tn(left, right):
    return lax.dot_general(left, right, (((0,), (0,)), ((), ())), preferred_element_type=F32)


class Place:
    def __init__(self, inner):
        q = lax.axis_index("seq")
        shard = lax.axis_index("shard")
        self.inner = inner
        self.rest = lax.rem(shard, inner) if inner > 1 else 0
        outer = lax.div(shard, inner) if inner > 1 else shard
        self.q = q
        self.x = lax.div(q, 2)
        self.c = lax.rem(q, 2)
        self.l = lax.div(outer, 2)
        self.y = lax.rem(outer, 2)
        self.own = outer

    def at(self, x=None, c=None, l=None, y=None):
        x = self.x if x is None else x
        c = self.c if c is None else c
        l = self.l if l is None else l
        y = self.y if y is None else y
        return (2 * x + c, (2 * l + y) * self.inner + self.rest)


def greet(me, devices, line):
    barrier = pltpu.get_barrier_semaphore()
    for device in devices:
        pl.semaphore_signal(barrier, inc=1, device_id=device, device_id_type=MESH)
    if not line:
        pl.semaphore_wait(barrier, len(devices))
        return

    @pl.when(me.l > 0)
    def _():
        pl.semaphore_signal(barrier, inc=1, device_id=me.at(l=me.l - 1), device_id_type=MESH)

    @pl.when(me.l < LINE - 1)
    def _():
        pl.semaphore_signal(barrier, inc=1, device_id=me.at(l=me.l + 1), device_id_type=MESH)

    near = jnp.minimum(me.l, 1) + jnp.minimum(LINE - 1 - me.l, 1)
    pl.semaphore_wait(barrier, len(devices) + near)


def remote(src, dst, send, recv, device):
    return pltpu.make_async_remote_copy(
        src_ref=src, dst_ref=dst, send_sem=send, recv_sem=recv, device_id=device, device_id_type=MESH
    )


def rope_constants(stream_len):
    frequency = ROPE_BASE ** (-(np.arange(HEAD_DIM // 2, dtype=np.float64) * 2.0 / HEAD_DIM))
    angles = np.arange(stream_len, dtype=np.float64)[:, None] * frequency[None, :]
    cosine = np.tile(np.cos(angles), (1, 4)).astype(np.float32)
    sine = np.tile(np.sin(angles), (1, 4)).astype(np.float32)
    turn = np.zeros((128, 128), np.float32)
    for j in range(128):
        if j % 64 < 32:
            turn[j + 32, j] = -1.0
        else:
            turn[j - 32, j] = 1.0
    return cosine, sine, turn


A_ROWS = 5 * 96
O_ROWS = 144
S_ROWS = 96
PACK = A_ROWS + O_ROWS + S_ROWS
TOK = 384
STREAM = 1536
ATT = 576


def forward_kernel(
    inner,
    tok, pack, up, dn, cos, sin, begin, turn,
    stream, packs, wo_all, wup, wdn, normed, qs, ks, vs, ohead, lse, attended, branch, wo,
    wq, wr, pk, got, ss, rs, ls,
):
    me = Place(inner)
    x, c, l, y, q, own = me.x, me.c, me.l, me.y, me.q, me.own
    nx, nc, ny = 1 - x, 1 - c, 1 - y

    S_TOK, S_PACK, S_WO, S_EX, S_ATT = 0, 3, 15, 18, 52
    R_TOK, R_PACK, R_WO, R_EX, R_ATT = 0, 3, 11, 14, 30

    keep = [
        pltpu.make_async_copy(up.at[y], wup.at[own], ls.at[0]),
        pltpu.make_async_copy(dn.at[y], wdn.at[own], ls.at[1]),
    ]
    for copy in keep:
        copy.start()
    greet(me, [me.at(c=nc), me.at(x=nx), me.at(x=nx, c=nc), me.at(y=ny)], True)

    def tok_copy(k, part, device):
        return remote(stream.at[part], stream.at[part], ss.at[S_TOK + k], rs.at[R_TOK + k], device)

    def pack_copy(kind, z, device):
        slot = 2 * z + y
        return remote(
            packs.at[slot], packs.at[slot], ss.at[S_PACK + 4 * kind + z], rs.at[R_PACK + slot], device
        )

    def pack_wait(slot):
        remote(packs.at[slot], packs.at[slot], ss.at[0], rs.at[R_PACK + slot], me.at(y=ny)).wait_recv()

    def ex_copies(kind, z, yy, device):
        slot = 2 * z + yy
        k = 2 * (8 * kind + slot)
        return [
            remote(ref.at[slot], ref.at[slot], ss.at[S_EX + k + n], rs.at[R_EX + 2 * slot + n], device)
            for n, ref in enumerate((wup, wdn))
        ]

    def ex_wait(slot):
        for n, ref in enumerate((wup, wdn)):
            remote(ref.at[slot], ref.at[slot], ss.at[0], rs.at[R_EX + 2 * slot + n], me.at(y=ny)).wait_recv()

    def ex_forward(z, yy, upward):
        if upward:
            @pl.when(l < LINE - 1)
            def _():
                for copy in ex_copies(0, z, yy, me.at(l=l + 1)):
                    copy.start()
        else:
            @pl.when(l > 0)
            def _():
                for copy in ex_copies(1, z, yy, me.at(l=l - 1)):
                    copy.start()

    stream[q] = tok[...]
    packs[own] = pack[...]
    tok_copy(1, q, me.at(x=nx)).start()
    tok_copy(0, q, me.at(c=nc)).start()

    def pack_up(z):
        @pl.when(l < LINE - 1)
        def _():
            pack_copy(0, z, me.at(l=l + 1)).start()

    def pack_down(z):
        @pl.when(l > 0)
        def _():
            pack_copy(1, z, me.at(l=l - 1)).start()

    def pack_over(z):
        pack_copy(2, z, me.at(y=ny)).start()

    pack_up(l)
    pack_down(l)
    pack_over(l)
    for step in range(1, LINE):
        @pl.when(l - step >= 0)
        def _():
            pack_wait(2 * (l - step) + y)
            pack_up(l - step)
            pack_over(l - step)

        @pl.when(l + step < LINE)
        def _():
            pack_wait(2 * (l + step) + y)
            pack_down(l + step)
            pack_over(l + step)

    for n, (src, ref) in enumerate(((up, wup), (dn, wdn))):
        remote(
            src.at[ny], ref.at[own], ss.at[S_EX + 32 + n], rs.at[R_EX + 2 * own + n], me.at(y=ny)
        ).start()
    for copy in keep:
        copy.wait()
    ex_forward(l, y, True)
    ex_forward(l, y, False)

    tok_copy(1, 2 * nx + c, me.at(x=nx)).wait_recv()
    tok_copy(2, 2 * nx + c, me.at(c=nc)).start()

    for z in range(LINE):
        pack_wait(2 * z + ny)

    wo_all[:, pl.ds(q * O_ROWS, O_ROWS), :] = packs[:, A_ROWS:A_ROWS + O_ROWS, :]

    def wo_copy(k, part, device):
        rows = pl.ds(part * O_ROWS, O_ROWS)
        return remote(
            wo_all.at[:, rows, :], wo_all.at[:, rows, :], ss.at[S_WO + k], rs.at[R_WO + k], device
        )

    wo_copy(1, q, me.at(x=nx)).start()
    wo_copy(0, q, me.at(c=nc)).start()

    for s in range(OUTER):
        for t in range(5):
            wq[t, 96 * s:96 * (s + 1), :] = packs[s, 96 * t:96 * (t + 1), :]
    for t in range(LOCAL_HEADS):
        wr[t] = mm(wq[t], turn[...]).astype(BF)
    gain = []
    for t in range(6):
        total = jnp.zeros((1, 128), F32)
        for s in range(OUTER):
            first = A_ROWS + O_ROWS + 16 * t
            total = total + packs[s, first:first + 16, :].astype(F32)[0:1]
        gain.append(total)
    gain = jnp.concatenate(gain, axis=1)

    tok_copy(0, 2 * x + nc, me.at(c=nc)).wait_recv()
    tok_copy(2, 2 * nx + nc, me.at(c=nc)).wait_recv()

    wo_copy(1, 2 * nx + c, me.at(x=nx)).wait_recv()
    wo_copy(2, 2 * nx + c, me.at(c=nc)).start()

    @pl.loop(0, 4)
    def _(part):
        values = stream[part].astype(F32)
        scale = lax.rsqrt(jnp.mean(values * values, axis=1, keepdims=True) + NORM_EPSILON)
        rows = pl.ds(pl.multiple_of(part * TOK, TOK), TOK)
        low = (values * scale * gain).astype(BF)
        normed[rows, :] = low
        cosine, sine = cos[rows, :], sin[rows, :]
        for h in range(LOCAL_HEADS):
            turned = mm(low, wq[h]) * cosine + mm(low, wr[h]) * sine
            qs[h, rows, :] = (turned[:, :64] * 0.125).astype(BF)
            ks[h, rows, :] = turned[:, 64:].astype(BF)
        both = mm(low, wq[3])
        vs[0, rows, :] = both[:, :64].astype(BF)
        vs[1, rows, :] = both[:, 64:].astype(BF)
        vs[2, rows, :] = mm(low, wq[4])[:, :64].astype(BF)

    def relay(step):
        @pl.when(l - step >= 0)
        def _():
            ex_wait(2 * (l - step) + y)
            ex_forward(l - step, y, True)
        @pl.when(l + step < LINE)
        def _():
            ex_wait(2 * (l + step) + y)
            ex_forward(l + step, y, False)
        @pl.when(l - step >= 0)
        def _():
            ex_wait(2 * (l - step) + ny)
            ex_forward(l - step, ny, True)
        @pl.when(l + step < LINE)
        def _():
            ex_wait(2 * (l + step) + ny)
            ex_forward(l + step, ny, False)

    ex_wait(2 * l + ny)
    ex_forward(l, ny, True)
    ex_forward(l, ny, False)

    block = 256

    def one_head(h):
        for b in range(STREAM // block):
            first, last = b * block, (b + 1) * block
            scores = mm_nt(qs[h, first:last, :], ks[h, 0:last, :])
            col = lax.broadcasted_iota(jnp.int32, (block, last), 1)
            row = lax.broadcasted_iota(jnp.int32, (block, last), 0) + first
            seen = (col >= begin[first:last, :]) & (col <= row)
            scores = jnp.where(seen, scores, NEGATIVE)
            top = jnp.max(scores, axis=1, keepdims=True)
            weight = jnp.exp(scores - top)
            total = jnp.sum(weight, axis=1, keepdims=True)
            result = mm(weight.astype(BF), vs[h, 0:last, :]) / total
            ohead[h, first:last, :] = result.astype(BF)
            logs = jnp.broadcast_to(top + jnp.log(total), (block, 128))
            lse[h, :, first:last] = jnp.transpose(logs)[0:8, :]

    pl.loop(0, 1)(one_head)
    relay(1)
    pl.loop(1, LOCAL_HEADS)(one_head)

    for part in range(4):
        rows = slice(part * TOK, (part + 1) * TOK)
        pk[part, 0:TOK, :] = jnp.concatenate([ohead[0, rows, :], ohead[1, rows, :]], axis=1)
        half = TOK // 2
        third = [ohead[2, part * TOK + k * half:part * TOK + (k + 1) * half, :] for k in range(2)]
        pk[part, TOK:ATT, :] = jnp.concatenate(third, axis=1)
    got[q] = pk[q]

    def att_copy(k, to, frm, device):
        return remote(pk.at[to], got.at[frm], ss.at[S_ATT + k], rs.at[R_ATT + k], device)

    others = [(2 * nx + c, me.at(x=nx)), (2 * nx + nc, me.at(x=nx, c=nc)), (2 * x + nc, me.at(c=nc))]
    for k, (other, device) in enumerate(others):
        att_copy(k, other, q, device).start()

    wo_copy(0, 2 * x + nc, me.at(c=nc)).wait_recv()
    wo_copy(2, 2 * nx + nc, me.at(c=nc)).wait_recv()
    for s in range(OUTER):
        for t in range(6):
            wo[96 * s:96 * (s + 1), 128 * t:128 * (t + 1)] = wo_all[s, 96 * t:96 * (t + 1), :]

    relay(2)
    for k, (other, device) in enumerate(others):
        att_copy(k, q, other, device).wait_recv()
    pieces = []
    for part in range(4):
        both = got[part, 0:TOK, :]
        half = TOK // 2
        low = got[part, TOK:ATT, :]
        pieces.append(both)
        pieces.append(jnp.concatenate([low[:, :64], low[:, 64:]], axis=0))
    whole = jnp.concatenate(pieces, axis=1)
    attended[...] = whole
    branch[...] = mm(whole, wo[...])

    relay(3)

    tok_copy(1, q, me.at(x=nx)).wait_send()
    tok_copy(0, q, me.at(c=nc)).wait_send()
    tok_copy(2, 2 * nx + c, me.at(c=nc)).wait_send()
    wo_copy(1, q, me.at(x=nx)).wait_send()
    wo_copy(0, q, me.at(c=nc)).wait_send()
    wo_copy(2, 2 * nx + c, me.at(c=nc)).wait_send()
    for k, (other, device) in enumerate(others):
        att_copy(k, other, q, device).wait_send()
    for n, (src, ref) in enumerate(((up, wup), (dn, wdn))):
        remote(
            src.at[ny], ref.at[own], ss.at[S_EX + 32 + n], rs.at[R_EX + 2 * own + n], me.at(y=ny)
        ).wait_send()
    for z in range(LINE):
        pack_copy(2, z, me.at(y=ny)).wait_send()

        @pl.when((l >= z) & (l < LINE - 1))
        def _():
            pack_copy(0, z, me.at(l=l + 1)).wait_send()
            for yy in range(2):
                for copy in ex_copies(0, z, yy, me.at(l=l + 1)):
                    copy.wait_send()

        @pl.when((l <= z) & (l > 0))
        def _():
            pack_copy(1, z, me.at(l=l - 1)).wait_send()
            for yy in range(2):
                for copy in ex_copies(1, z, yy, me.at(l=l - 1)):
                    copy.wait_send()


def forward_call(inner, tok, pack, up, dn, cos, sin, begin, turn):
    vm = pl.BlockSpec(memory_space=pltpu.VMEM)
    hbm = pl.BlockSpec(memory_space=pl.ANY)
    shapes = [
        ((4, TOK, D), BF, vm),
        ((OUTER, PACK, 128), BF, vm),
        ((OUTER, 576, 128), BF, vm),
        ((OUTER, 96, FF), BF, hbm),
        ((OUTER, 128, D), BF, hbm),
        ((STREAM, D), BF, vm),
        ((LOCAL_HEADS, STREAM, 64), BF, vm),
        ((LOCAL_HEADS, STREAM, 64), BF, vm),
        ((LOCAL_HEADS, STREAM, 64), BF, vm),
        ((LOCAL_HEADS, STREAM, 64), BF, vm),
        ((LOCAL_HEADS, 8, STREAM), F32, vm),
        ((TOK, D), BF, vm),
        ((TOK, D), F32, vm),
        ((D, D), BF, vm),
    ]
    return pl.pallas_call(
        functools.partial(forward_kernel, inner),
        out_shape=[jax.ShapeDtypeStruct(s, t) for s, t, _ in shapes],
        in_specs=[vm, vm, hbm, hbm, vm, vm, vm, vm],
        out_specs=[spec for _, _, spec in shapes],
        scratch_shapes=[
            pltpu.VMEM((5, D, 128), BF),
            pltpu.VMEM((3, D, 128), BF),
            pltpu.VMEM((4, ATT, 128), BF),
            pltpu.VMEM((4, ATT, 128), BF),
            pltpu.SemaphoreType.DMA((55,)),
            pltpu.SemaphoreType.DMA((33,)),
            pltpu.SemaphoreType.DMA((2,)),
        ],
        compiler_params=pltpu.CompilerParams(
            collective_id=0, has_side_effects=True, vmem_limit_bytes=VMEM_LIMIT
        ),
        name="gather_attend",
    )(tok, pack, up, dn, cos, sin, begin, turn)


def gather_inner(values, axis, inner):
    if inner == 1:
        return values
    count = lax.axis_size("shard")
    groups = [[o * inner + i for i in range(inner)] for o in range(count // inner)]
    return lax.all_gather(values, "shard", axis=axis, tiled=True, axis_index_groups=groups)


def pick(values, index, axis):
    return lax.dynamic_index_in_dim(values, index, axis, keepdims=False)


def pack_attention(w_in, w_out, w_router, w_vectors, q, outer):
    heads = pick(w_in.reshape(3, 96, 4, LOCAL_HEADS, 64), q, 2)
    tiles = [jnp.concatenate([heads[0, :, h], heads[1, :, h]], axis=1) for h in range(LOCAL_HEADS)]
    tiles.append(jnp.concatenate([heads[2, :, 0], heads[2, :, 1]], axis=1))
    tiles.append(jnp.pad(heads[2, :, 2], ((0, 0), (0, 64))))
    out_tiles = w_out.reshape(96, 6, 128).transpose(1, 0, 2).reshape(4, O_ROWS, 128)
    small = jnp.concatenate([w_vectors, w_router.T], axis=0)
    placed = lax.dynamic_update_slice(jnp.zeros((16, D), BF), small, (0, 96 * outer))
    small_tiles = placed.reshape(16, 6, 128).transpose(1, 0, 2).reshape(S_ROWS, 128)
    return jnp.concatenate(tiles + [pick(out_tiles, q, 0), small_tiles], axis=0)


def expert_pieces(w_up, w_down, x, c):
    ups = lax.dynamic_slice_in_dim(w_up, 2 * x, 2, 0).reshape(2, 96, 2, 8, 2, 128)
    ups = pick(ups, c, 4).reshape(2, 96, FF).astype(BF)
    downs = lax.dynamic_slice(w_down, (2 * x, 128 * c, 0), (2, 128, D)).astype(BF)
    return ups, downs


def expert_kernel(
    inner,
    bufh, bufg, wup, wdn,
    down_ret, gbuf_ret, gup, gdn,
    rowh, rowg, rowt, act, da, db, total, part_out, part_in, send, ss, rs,
):
    me = Place(inner)
    x, c, y = me.x, me.c, me.y
    nx, nc, ny = 1 - x, 1 - c, 1 - y
    mine = 2 * x + y
    chips = [(nx, y), (x, ny), (nx, ny)]
    greet(me, [me.at(c=nc)] + [me.at(x=cx, y=cy) for cx, cy in chips], False)
    base = 4 * c

    def out_copy(n, buf, row, k, cx, cy):
        return remote(
            buf.at[2 * cx + cy], row.at[base + mine], ss.at[16 * n + k], rs.at[16 * n + mine], me.at(x=cx, y=cy)
        )

    def in_wait(n, row, cx, cy):
        slot = 2 * cx + cy
        remote(
            row.at[base + slot], row.at[base + slot], ss.at[0], rs.at[16 * n + slot], me.at(x=cx, y=cy)
        ).wait_recv()

    def core_copy(n, row, first, k, slot):
        return remote(
            row.at[first + slot], row.at[first + slot], ss.at[16 * n + 3 + k], rs.at[16 * n + 4 + slot], me.at(c=nc)
        )

    for n, (buf, row) in enumerate(((bufh, rowh), (bufg, rowg))):
        for k, (cx, cy) in enumerate(chips):
            out_copy(n, buf, row, k, cx, cy).start()
        row[base + mine] = buf[mine]
        core_copy(n, row, base, 0, mine).start()

    def collect(n, row):
        for k, (cx, cy) in enumerate(chips):
            in_wait(n, row, cx, cy)
            core_copy(n, row, base, 1 + k, 2 * cx + cy).start()
        for slot in range(4):
            core_copy(n, row, 4 - base, 0, slot).wait_recv()

    collect(0, rowh)
    rows_h = rowh[...].reshape(8 * CAP, D)
    rowt[...] = jnp.transpose(rows_h.astype(F32)).astype(BF)
    total[...] = jnp.zeros_like(total)

    @pl.loop(0, 4)
    def _(j):
        gate_cols = pl.ds(pl.multiple_of(j * 256, 256), 256)
        lin_cols = pl.ds(pl.multiple_of(1024 + j * 256, 256), 256)
        rows_in = rowh[...].reshape(8 * CAP, D)
        gate = mm(rows_in, wup[:, :, gate_cols].reshape(D, 256))
        lin = mm(rows_in, wup[:, :, lin_cols].reshape(D, 256))
        sigma = jax.nn.sigmoid(gate)
        silu = gate * sigma
        low = (silu * lin).astype(BF)
        act[:, gate_cols] = low
        da[:, gate_cols] = lin * sigma * (1.0 + gate * (1.0 - sigma))
        db[:, gate_cols] = silu
        total[...] += mm(low, wdn[pl.ds(2 * j, 2)].reshape(256, D))

    def give_back(n, ret):
        other = pl.multiple_of((4 - base) * CAP, 4 * CAP)
        part_out[n] = total[pl.ds(other, 4 * CAP), :].astype(BF)
        swap = remote(part_out.at[n], part_in.at[n], ss.at[16 * n + 7], rs.at[16 * n + 8], me.at(c=nc))
        swap.start()
        swap.wait_recv()
        kept = total[pl.ds(pl.multiple_of(base * CAP, 4 * CAP), 4 * CAP), :]
        send[n] = (kept + part_in[n].astype(F32)).astype(BF).reshape(4, CAP, D)
        for k, (cx, cy) in enumerate(chips):
            back_copy(n, ret, k, cx, cy).start()
        ret[mine] = send[n, mine]

    def back_copy(n, ret, k, cx, cy):
        return remote(
            send.at[n, 2 * cx + cy], ret.at[mine], ss.at[16 * n + 8 + k], rs.at[16 * n + 9 + mine], me.at(x=cx, y=cy)
        )

    def back_wait(n, ret, cx, cy):
        slot = 2 * cx + cy
        remote(
            ret.at[slot], ret.at[slot], ss.at[0], rs.at[16 * n + 9 + slot], me.at(x=cx, y=cy)
        ).wait_recv()

    give_back(0, down_ret)
    collect(1, rowg)
    total[...] = jnp.zeros_like(total)

    @pl.loop(0, 4)
    def _(j):
        gate_cols = pl.ds(pl.multiple_of(j * 256, 256), 256)
        lin_cols = pl.ds(pl.multiple_of(1024 + j * 256, 256), 256)
        rows_g = rowg[...].reshape(8 * CAP, D)
        grad_act = mm_nt(rows_g, wdn[pl.ds(2 * j, 2)].reshape(256, D))
        grad_gate = (grad_act * da[:, gate_cols]).astype(BF)
        grad_lin = (grad_act * db[:, gate_cols]).astype(BF)
        gdn[pl.ds(2 * j, 2)] = mm_tn(act[:, gate_cols], rows_g).astype(BF).reshape(2, 128, D)
        gup[:, :, gate_cols] = mm(rowt[...], grad_gate).astype(BF).reshape(8, 96, 256)
        gup[:, :, lin_cols] = mm(rowt[...], grad_lin).astype(BF).reshape(8, 96, 256)
        total[...] += mm_nt(grad_gate, wup[:, :, gate_cols].reshape(D, 256)) + mm_nt(
            grad_lin, wup[:, :, lin_cols].reshape(D, 256)
        )

    give_back(1, gbuf_ret)
    for n, (buf, row, ret) in enumerate(((bufh, rowh, down_ret), (bufg, rowg, gbuf_ret))):
        for k, (cx, cy) in enumerate(chips):
            back_wait(n, ret, cx, cy)
            out_copy(n, buf, row, k, cx, cy).wait_send()
            back_copy(n, ret, k, cx, cy).wait_send()
            core_copy(n, row, base, 1 + k, 2 * cx + cy).wait_send()
        core_copy(n, row, base, 0, mine).wait_send()
        remote(part_out.at[n], part_in.at[n], ss.at[16 * n + 7], rs.at[16 * n + 8], me.at(c=nc)).wait_send()


def expert_call(inner, bufh, bufg, wup, wdn):
    vm = pl.BlockSpec(memory_space=pltpu.VMEM)
    rows = 8 * CAP
    return pl.pallas_call(
        functools.partial(expert_kernel, inner),
        out_shape=[
            jax.ShapeDtypeStruct((NFFN, CAP, D), BF),
            jax.ShapeDtypeStruct((NFFN, CAP, D), BF),
            jax.ShapeDtypeStruct((OUTER, 96, FF), BF),
            jax.ShapeDtypeStruct((OUTER, 128, D), BF),
        ],
        in_specs=[vm] * 4,
        out_specs=[vm] * 4,
        scratch_shapes=[
            pltpu.VMEM((8, CAP, D), BF),
            pltpu.VMEM((8, CAP, D), BF),
            pltpu.VMEM((D, rows), BF),
            pltpu.VMEM((rows, 1024), BF),
            pltpu.VMEM((rows, 1024), F32),
            pltpu.VMEM((rows, 1024), F32),
            pltpu.VMEM((rows, D), F32),
            pltpu.VMEM((2, 4 * CAP, D), BF),
            pltpu.VMEM((2, 4 * CAP, D), BF),
            pltpu.VMEM((2, 4, CAP, D), BF),
            pltpu.SemaphoreType.DMA((32,)),
            pltpu.SemaphoreType.DMA((32,)),
        ],
        compiler_params=pltpu.CompilerParams(
            collective_id=1, has_side_effects=True, vmem_limit_bytes=VMEM_LIMIT
        ),
        name="experts",
    )(bufh, bufg, wup, wdn)


def backward_kernel(
    inner,
    gbranch, attended, wo, qs, ks, vs, ohead, lse, begin, cos, sin, turn, normed, packs, stream, small,
    gup, gdn,
    gnorm_ret, apack, gup_all, gdn_all,
    pk, got, kt, grad, dq, dk, dv, dk_sum, dv_sum, delta, gr, wall, wo_out, wo_in, ap, ap_in, ap_line, gn_out, gn_in, gn_send,
    gn_ret, apall_in, upr, dnr, upf, dnf, ss, rs, ls,
):
    me = Place(inner)
    x, c, l, y, q, own = me.x, me.c, me.l, me.y, me.q, me.own
    nx, nc, ny = 1 - x, 1 - c, 1 - y
    devices = [me.at(c=nc), me.at(x=nx), me.at(x=nx, c=nc), me.at(y=ny), me.at(x=nx, y=ny)]
    greet(me, devices, True)
    S_LINE, S_ATT, S_WO, S_AY, S_AL, S_GN, S_AA, S_GP = 0, 32, 35, 38, 42, 50, 54, 60
    R_LINE, R_ATT, R_WO, R_AY, R_AL, R_GN, R_AA, R_GP = 0, 32, 35, 38, 42, 50, 54, 60
    kinds = ((gup, upr, upf, gup_all), (gdn, dnr, dnf, gdn_all))

    def line_copy(d, z, yy, n, src, device, last):
        k = ((d * 4 + z) * 2 + yy) * 2 + n
        slot = 8 + yy if last and d == 1 else 2 * z + yy
        return remote(src, kinds[n][1].at[slot], ss.at[S_LINE + k], rs.at[R_LINE + k], device)

    def first_sends(d, order, device):
        for z in order:
            for yy in range(2):
                for n in range(2):
                    line_copy(d, z, yy, n, kinds[n][0].at[2 * z + yy], device, z == order[2]).start()

    @pl.when(l == 0)
    def _():
        first_sends(0, (3, 2, 1), me.at(l=l + 1))

    @pl.when(l == LINE - 1)
    def _():
        first_sends(1, (0, 1, 2), me.at(l=l - 1))

    def add_own(n, slot):
        own_ref, ring = kinds[n][0], kinds[n][1]
        rows = own_ref.shape[1]

        @pl.loop(0, rows // 16)
        def _(r):
            part = pl.ds(pl.multiple_of(r * 16, 16), 16)
            total = own_ref[slot, part, :].astype(F32) + ring[slot, part, :].astype(F32)
            ring[slot, part, :] = total.astype(BF)

    def line_step(t):
        for d in range(2):
            far = l if d == 0 else LINE - 1 - l
            z = 3 + l - t if d == 0 else t - 3 + l

            @pl.when((far >= 1) & (far <= t))
            def _():
                device = me.at(l=l + 1) if d == 0 else me.at(l=l - 1)
                for yy in range(2):
                    for n in range(2):
                        slot = 2 * z + yy
                        ring = kinds[n][1]
                        line_copy(d, z, yy, n, ring.at[slot], me.at(y=ny), t == 3).wait_recv()
                        if t < 3:
                            add_own(n, slot)
                            line_copy(d, z, yy, n, ring.at[slot], device, t == 2).start()

    grad_att = mm_nt(gbranch[...], wo[...])
    half = TOK // 2
    for part in range(4):
        cols = grad_att[:, 192 * part:192 * (part + 1)]
        pk[part, 0:TOK, :] = cols[:, :128].astype(BF)
        low = cols[:, 128:]
        pk[part, TOK:ATT, :] = jnp.concatenate([low[:half], low[half:]], axis=1).astype(BF)
    got[q] = pk[q]

    def att_copy(k, to, frm, device):
        return remote(pk.at[to], got.at[frm], ss.at[S_ATT + k], rs.at[R_ATT + k], device)

    others = [(2 * nx + c, me.at(x=nx)), (2 * nx + nc, me.at(x=nx, c=nc)), (2 * x + nc, me.at(c=nc))]
    for k, (other, device) in enumerate(others):
        att_copy(k, other, q, device).start()

    grad_wo = mm_tn(attended[...], gbranch[...]).astype(BF)
    for s in range(OUTER):
        for t in range(6):
            tile = grad_wo[96 * s:96 * (s + 1), 128 * t:128 * (t + 1)]
            wo_out[s, 96 * t:96 * (t + 1), :] = tile

    def wo_rows(part):
        return pl.ds(pl.multiple_of(part * O_ROWS, O_ROWS), O_ROWS)

    def wo_copy(k, to, frm, device):
        return remote(
            wo_out.at[:, wo_rows(to), :], wo_in.at[frm], ss.at[S_WO + k], rs.at[R_WO + k], device
        )

    for k, (other, device) in enumerate(others):
        wo_copy(k, other, q, device).start()

    for h in range(LOCAL_HEADS):
        kt[h] = jnp.transpose(ks[h].astype(F32)).astype(BF)
    for s in range(OUTER):
        for t in range(5):
            wall[96 * s:96 * (s + 1), 128 * t:128 * (t + 1)] = packs[s, 96 * t:96 * (t + 1), :]

    for k, (other, device) in enumerate(others):
        att_copy(k, q, other, device).wait_recv()
    for part in range(4):
        rows = slice(part * TOK, (part + 1) * TOK)
        both = got[part, 0:TOK, :]
        low = got[part, TOK:ATT, :]
        grad[0, rows, :] = both[:, :64]
        grad[1, rows, :] = both[:, 64:]
        grad[2, rows, :] = jnp.concatenate([low[:, :64], low[:, 64:]], axis=0)
    for h in range(LOCAL_HEADS):
        dots = jnp.sum(grad[h].astype(F32) * ohead[h], axis=1, keepdims=True)
        delta[h] = jnp.transpose(jnp.broadcast_to(dots, (STREAM, 128)))[0:8, :]

    block = 256

    def one_head(h):
        dk_sum[...] = jnp.zeros((STREAM, 64), F32)
        dv_sum[...] = jnp.zeros((STREAM, 64), F32)
        for b in range(STREAM // block):
            first, last = b * block, (b + 1) * block
            q_rows, g_rows = qs[h, first:last, :], grad[h, first:last, :]
            scores = mm_nt(ks[h, 0:last, :], q_rows)
            key = lax.broadcasted_iota(jnp.int32, (last, block), 0)
            col = lax.broadcasted_iota(jnp.int32, (last, block), 1) + first
            seen = (key >= begin[0:1, first:last]) & (key <= col)
            probs = jnp.exp(jnp.where(seen, scores, NEGATIVE) - lse[h, 0:1, first:last])
            grad_probs = mm_nt(vs[h, 0:last, :], g_rows)
            grad_scores = (probs * (grad_probs - delta[h, 0:1, first:last])).astype(BF)
            dv_sum[0:last, :] += mm(probs.astype(BF), g_rows)
            dk_sum[0:last, :] += mm(grad_scores, q_rows)
            dq[h, first:last, :] = (jnp.transpose(mm(kt[h, :, 0:last], grad_scores)) * 0.125).astype(BF)
        dk[h] = dk_sum[...].astype(BF)
        dv[h] = dv_sum[...].astype(BF)

    pl.loop(0, 1)(one_head)
    line_step(1)
    pl.loop(1, LOCAL_HEADS)(one_head)
    line_step(2)

    for part in range(4):
        rows = slice(part * TOK, (part + 1) * TOK)
        cosine, sine = cos[rows, :], sin[rows, :]
        for h in range(LOCAL_HEADS):
            turned = jnp.concatenate([dq[h, rows, :], dk[h, rows, :]], axis=1)
            raw = turned.astype(F32) * cosine - mm(turned, turn[...]) * sine
            gr[rows, 128 * h:128 * (h + 1)] = raw.astype(BF)
        gr[rows, 384:512] = jnp.concatenate([dv[0, rows, :], dv[1, rows, :]], axis=1)
        gr[rows, 512:640] = jnp.concatenate([dv[2, rows, :], jnp.zeros((TOK, 64), BF)], axis=1)

    grad_a = mm_tn(normed[...], gr[...]).astype(BF)
    for s in range(OUTER):
        for t in range(5):
            ap[s, 96 * t:96 * (t + 1), :] = grad_a[96 * s:96 * (s + 1), 128 * t:128 * (t + 1)]
    for k, (other, device) in enumerate(others):
        wo_copy(k, q, other, device).wait_recv()
    wo_total = wo_out[:, wo_rows(q), :].astype(F32)
    for other, _ in others:
        wo_total = wo_total + wo_in[other].astype(F32)
    ap[:, A_ROWS:A_ROWS + O_ROWS, :] = wo_total.astype(BF)

    gain_sum = jnp.zeros((1, D), F32)
    for part in range(4):
        rows = slice(part * TOK, (part + 1) * TOK)
        grad_n = mm_nt(gr[rows, :], wall[...])
        values = stream[part].astype(F32)
        scale = lax.rsqrt(jnp.mean(values * values, axis=1, keepdims=True) + NORM_EPSILON)
        gain_sum = gain_sum + jnp.sum(grad_n * (values * scale), axis=0, keepdims=True)
        gn_out[part] = grad_n.astype(BF)

    def gn_swap(a):
        return remote(gn_out.at[2 * a + nc], gn_in.at[a], ss.at[S_GN + a], rs.at[R_GN + a], me.at(c=nc))

    for a in range(2):
        gn_swap(a).start()

    first_row = lax.broadcasted_iota(jnp.int32, (16, 1), 0) == 0
    small_all = small[...] + jnp.where(first_row, gain_sum, 0.0)
    for s in range(OUTER):
        piece = small_all[:, 96 * s:96 * (s + 1)]
        piece = jnp.concatenate([piece, jnp.zeros((16, 32), F32)], axis=1)
        ap[s, A_ROWS + O_ROWS:A_ROWS + O_ROWS + 16, :] = piece.astype(BF)

    def ay_copy(z):
        return remote(ap.at[2 * z + ny], ap_in.at[z], ss.at[S_AY + z], rs.at[R_AY + z], me.at(y=ny))

    for z in range(LINE):
        ay_copy(z).start()

    for a in range(2):
        gn_swap(a).wait_recv()
    for a in range(2):
        gn_send[a] = (gn_out[2 * a + c].astype(F32) + gn_in[a].astype(F32)).astype(BF)
    gn_over = remote(gn_send.at[nx], gn_ret, ss.at[S_GN + 2], rs.at[R_GN + 2], me.at(x=nx))
    gn_over.start()

    for z in range(LINE):
        ay_copy(z).wait_recv()
        ap_in[z] = (ap[2 * z + y].astype(F32) + ap_in[z].astype(F32)).astype(BF)

    def al_copy(d, z, src, device):
        k = 4 * d + z
        return remote(src, ap_line.at[d, z], ss.at[S_AL + k], rs.at[R_AL + k], device)

    @pl.when(l == 0)
    def _():
        for z in (3, 2, 1):
            al_copy(0, z, ap_in.at[z], me.at(l=l + 1)).start()

    @pl.when(l == LINE - 1)
    def _():
        for z in (0, 1, 2):
            al_copy(1, z, ap_in.at[z], me.at(l=l - 1)).start()

    for t in range(1, 4):
        for d in range(2):
            far = l if d == 0 else LINE - 1 - l
            z = 3 + l - t if d == 0 else t - 3 + l

            @pl.when((far >= 1) & (far <= t))
            def _():
                device = me.at(l=l + 1) if d == 0 else me.at(l=l - 1)
                al_copy(d, z, ap_line.at[d, z], me.at(y=ny)).wait_recv()
                if t < 3:
                    ap_line[d, z] = (ap_line[d, z].astype(F32) + ap_in[z].astype(F32)).astype(BF)
                    al_copy(d, z, ap_line.at[d, z], device).start()

    @pl.when(l == 0)
    def _():
        ap_line[0, l] = jnp.zeros((PACKG, 128), BF)

    @pl.when(l == LINE - 1)
    def _():
        ap_line[1, l] = jnp.zeros((PACKG, 128), BF)

    own_sum = ap_in[l].astype(F32) + ap_line[0, l].astype(F32) + ap_line[1, l].astype(F32)
    apack[q] = own_sum.astype(BF)

    def aa_copy(k, part, device):
        return remote(apack.at[part], apack.at[part], ss.at[S_AA + k], rs.at[R_AA + k], device)

    for k, (other, device) in enumerate(others):
        aa_copy(k, q, device).start()

    line_step(3)

    for n in range(2):
        own_ref, ring, fin, _ = kinds[n]
        rows = own_ref.shape[1]
        for yy in range(2):
            slot = 2 * l + yy

            @pl.loop(0, rows // 16)
            def _(r):
                part = pl.ds(pl.multiple_of(r * 16, 16), 16)
                up_sum = jnp.where(l >= 1, ring[slot, part, :].astype(F32), 0.0)
                dn_sum = jnp.where(l <= 2, ring[8 + yy, part, :].astype(F32), 0.0)
                total = own_ref[slot, part, :].astype(F32) + up_sum + dn_sum
                fin[yy, part, :] = total.astype(BF)

    chips = [(nx, y), (x, ny), (nx, ny)]
    mine = 2 * x + y

    def gp_copy(n, k, cx, cy):
        return remote(
            kinds[n][2].at[cy], kinds[n][3].at[2 * mine + c], ss.at[S_GP + 7 * n + k],
            rs.at[R_GP + 8 * n + 2 * mine + c], me.at(x=cx, y=cy)
        )

    def gp_wait(n, slot):
        ref = kinds[n][3]
        remote(ref.at[slot], ref.at[slot], ss.at[0], rs.at[R_GP + 8 * n + slot], me.at(c=nc)).wait_recv()

    def gp_own(n):
        return pltpu.make_async_copy(kinds[n][2].at[y], kinds[n][3].at[2 * mine + c], ls.at[n])

    def gp_core(n, k, slot, src=None):
        ref = kinds[n][3]
        return remote(
            ref.at[slot] if src is None else src, ref.at[slot], ss.at[S_GP + 7 * n + 3 + k], rs.at[R_GP + 8 * n + slot], me.at(c=nc)
        )

    for n in range(2):
        for k, (cx, cy) in enumerate(chips):
            gp_copy(n, k, cx, cy).start()
        gp_own(n).start()
        gp_core(n, 0, 2 * mine + c, kinds[n][2].at[y]).start()
    for n in range(2):
        for k, (cx, cy) in enumerate(chips):
            slot = 2 * (2 * cx + cy) + c
            gp_wait(n, slot)
            gp_core(n, 1 + k, slot).start()

    gn_over.wait_recv()
    gnorm_ret[...] = gn_send[x].astype(F32) + gn_ret[...].astype(F32)

    for n in range(2):
        for slot in range(4):
            gp_wait(n, 2 * slot + nc)
    for k, (other, device) in enumerate(others):
        aa_copy(k, other, device).wait_recv()

    for k, (other, device) in enumerate(others):
        att_copy(k, other, q, device).wait_send()
        wo_copy(k, other, q, device).wait_send()
        aa_copy(k, q, device).wait_send()
    for a in range(2):
        gn_swap(a).wait_send()
    gn_over.wait_send()
    for z in range(LINE):
        ay_copy(z).wait_send()
    for n in range(2):
        for k, (cx, cy) in enumerate(chips):
            gp_copy(n, k, cx, cy).wait_send()
            gp_core(n, 1 + k, 2 * (2 * cx + cy) + c).wait_send()
        gp_core(n, 0, 2 * mine + c, kinds[n][2].at[y]).wait_send()
        gp_own(n).wait()
    for d in range(2):
        for z in range(LINE):
            sent = (z > l) & (l < LINE - 1) if d == 0 else (z < l) & (l > 0)

            @pl.when(sent)
            def _():
                device = me.at(l=l + 1) if d == 0 else me.at(l=l - 1)
                al_copy(d, z, ap_line.at[d, z], device).wait_send()
                for yy in range(2):
                    for n in range(2):
                        line_copy(d, z, yy, n, kinds[n][1].at[2 * z + yy], device, False).wait_send()


PACKG = A_ROWS + O_ROWS + 16


def backward_call(inner, *args):
    vm = pl.BlockSpec(memory_space=pltpu.VMEM)
    heads = (LOCAL_HEADS, STREAM, 64)
    return pl.pallas_call(
        functools.partial(backward_kernel, inner),
        out_shape=[
            jax.ShapeDtypeStruct((TOK, D), F32),
            jax.ShapeDtypeStruct((4, PACKG, 128), BF),
            jax.ShapeDtypeStruct((8, 96, FF), BF),
            jax.ShapeDtypeStruct((8, 128, D), BF),
        ],
        in_specs=[vm] * len(args),
        out_specs=[vm] * 2 + [pl.BlockSpec(memory_space=pl.ANY)] * 2,
        scratch_shapes=[
            pltpu.VMEM((4, ATT, 128), BF),
            pltpu.VMEM((4, ATT, 128), BF),
            pltpu.VMEM((LOCAL_HEADS, 64, STREAM), BF),
            pltpu.VMEM(heads, BF),
            pltpu.VMEM(heads, BF),
            pltpu.VMEM(heads, BF),
            pltpu.VMEM(heads, BF),
            pltpu.VMEM((STREAM, 64), F32),
            pltpu.VMEM((STREAM, 64), F32),
            pltpu.VMEM((LOCAL_HEADS, 8, STREAM), F32),
            pltpu.VMEM((STREAM, 640), BF),
            pltpu.VMEM((D, 640), BF),
            pltpu.VMEM((OUTER, 576, 128), BF),
            pltpu.VMEM((4, OUTER, O_ROWS, 128), BF),
            pltpu.VMEM((OUTER, PACKG, 128), BF),
            pltpu.VMEM((LINE, PACKG, 128), BF),
            pltpu.VMEM((2, LINE, PACKG, 128), BF),
            pltpu.VMEM((4, TOK, D), BF),
            pltpu.VMEM((2, TOK, D), BF),
            pltpu.VMEM((2, TOK, D), BF),
            pltpu.VMEM((TOK, D), BF),
            pltpu.VMEM((8, 128), BF),
            pltpu.VMEM((10, 96, FF), BF),
            pltpu.VMEM((10, 128, D), BF),
            pltpu.VMEM((2, 96, FF), BF),
            pltpu.VMEM((2, 128, D), BF),
            pltpu.SemaphoreType.DMA((74,)),
            pltpu.SemaphoreType.DMA((76,)),
            pltpu.SemaphoreType.DMA((2,)),
        ],
        compiler_params=pltpu.CompilerParams(
            collective_id=2, has_side_effects=True, vmem_limit_bytes=57 * 2**20
        ),
        name="attend_back",
    )(*args)


def scatter_inner(values, axis, inner):
    if inner == 1:
        return values
    count = lax.axis_size("shard")
    groups = [[o * inner + i for i in range(inner)] for o in range(count // inner)]
    return lax.psum_scatter(
        values, "shard", scatter_dimension=axis, axis_index_groups=groups, tiled=True
    )


def norm_rows(values, gain_row):
    scale_rows = lax.rsqrt(jnp.mean(values * values, axis=-1, keepdims=True) + NORM_EPSILON)
    return values * scale_rows * gain_row, scale_rows


def norm_back(grad_rows, values, scale_rows, gain_row):
    normal_rows = values * scale_rows
    inner_term = grad_rows * gain_row
    return scale_rows * (
        inner_term - normal_rows * jnp.mean(inner_term * normal_rows, axis=-1, keepdims=True)
    )


def adam_update(weight, grad, first, second, rate, decay):
    first_new = MOMENT_DECAY * first + (1.0 - MOMENT_DECAY) * grad
    second_new = MOMENT_DECAY * second + (1.0 - MOMENT_DECAY) * grad * grad
    correction = 1.0 - MOMENT_DECAY**STEP
    update = first_new / correction / (jnp.sqrt(second_new / correction) + ADAM_EPSILON)
    return weight - rate * (update + decay * weight), first_new, second_new


def local(
    tokens, route_residual, doc_lengths, routes, priority, grad_out,
    attend_in, attend_in_first, attend_in_second,
    attend_out, attend_out_first, attend_out_second,
    expert_up, expert_up_first, expert_up_second,
    expert_down, expert_down_first, expert_down_second,
    router_mix, router_mix_first, router_mix_second,
    vectors, vectors_first, vectors_second,
):
    inner = lax.axis_size("shard") // OUTER
    q = lax.axis_index("seq")
    outer = lax.axis_index("shard") // inner
    x, c = q // 2, q % 2

    w_in = gather_inner(attend_in.astype(BF), 1, inner)
    w_out = gather_inner(attend_out.astype(BF), 0, inner)
    w_router = gather_inner(router_mix.astype(BF), 0, inner)
    w_vectors = gather_inner(vectors.astype(BF), 1, inner)
    pack = pack_attention(w_in, w_out, w_router, w_vectors, q, outer)
    if inner == 1:
        ups, downs = expert_pieces(expert_up, expert_down, x, c)
    else:
        ups, downs = expert_pieces(
            gather_inner(expert_up.astype(BF), 1, inner), gather_inner(expert_down.astype(BF), 1, inner), x, c
        )
    cosine, sine, turn = rope_constants(STREAM)
    cosine, sine, turn = jnp.asarray(cosine), jnp.asarray(sine), jnp.asarray(turn, BF)
    ids = jnp.arange(STREAM, dtype=jnp.int32)
    starts = jnp.cumsum(doc_lengths[0]) - doc_lengths[0]
    begin = jnp.max(jnp.where(starts[None, :] <= ids[:, None], starts[None, :], 0), axis=1).astype(jnp.int32)

    stream, packs, _, wup, wdn, normed, qs, ks, vs, ohead, lse, attended, branch, wo = forward_call(
        inner, tokens[0], pack, ups, downs, cosine, sine, begin[:, None], turn
    )

    smalls = jnp.sum(packs[:, A_ROWS + O_ROWS:].astype(F32), axis=0)
    smalls = smalls.reshape(6, 16, 128).transpose(1, 0, 2).reshape(16, D)
    vector_rows, router_rows = smalls[:4], smalls[4:]
    residual_in = tokens[0].astype(F32)
    middle = residual_in + branch
    hidden, scale_two = norm_rows(middle, vector_rows[1])
    hidden_low = hidden.astype(BF)
    hidden_val = hidden_low.astype(F32)
    logits = mm_nt(hidden_low, router_rows.astype(BF))
    route_ids = routes[0]
    route_logits = logits[:, :NEXP] + route_residual[0]
    onehot = (route_ids[:, :, None] == jnp.arange(NEXP, dtype=jnp.int32)[None, None, :]).astype(F32)
    picked = jnp.sum(onehot * route_logits[:, None, :], axis=2)
    gates = jax.nn.softmax(picked, axis=-1)
    coefficient = jax.nn.softmax(logits[:, NEXP:].reshape(TOK, 2, 2), axis=-1)
    expert_id = route_ids.T.reshape(-1)
    order_key = (jnp.arange(TOPK, dtype=jnp.int32)[:, None] * STREAM + priority[0][None, :]).reshape(-1)
    earlier = (expert_id[:, None] == expert_id[None, :]) & (order_key[None, :] < order_key[:, None])
    slot_rank = jnp.sum(earlier.astype(jnp.int32), axis=1)
    kept_pair = (expert_id < NFFN) & (slot_rank < CAP)
    flat_slot = jnp.where(kept_pair, expert_id * CAP + slot_rank, -1)
    slots = jnp.arange(NFFN * CAP, dtype=jnp.int32)
    maps = [(slots[:, None] == flat_slot[None, k * TOK:(k + 1) * TOK]).astype(BF) for k in range(TOPK)]
    both_map = maps[0] + maps[1]
    grad_top = grad_out[0].astype(F32)
    bufh = mm(both_map, hidden_low).astype(BF).reshape(NFFN, CAP, D)
    bufg = sum(mm(maps[k], (gates[:, k:k + 1] * grad_top).astype(BF)) for k in range(TOPK))
    bufg = bufg.astype(BF).reshape(NFFN, CAP, D)

    down_ret, gbuf_ret, gup, gdn = expert_call(inner, bufh, bufg, wup, wdn)

    down_rows = down_ret.reshape(NFFN * CAP, D)
    grad_buffer = gbuf_ret.reshape(NFFN * CAP, D)
    consts = [
        coefficient[:, j, 0:1] * hidden_val + coefficient[:, j, 1:2] * vector_rows[2 + j][None, :] for j in range(2)
    ]
    values = []
    for k in range(TOPK):
        column = route_ids[:, k:k + 1]
        value = mm_tn(maps[k], down_rows)
        value = jnp.where(column == NFFN + 1, hidden_val, value)
        for j in range(2):
            value = jnp.where(column == NFFN + 2 + j, consts[j], value)
        values.append(value)
    layer_out = (middle + gates[:, 0:1] * values[0] + gates[:, 1:2] * values[1]).astype(BF)
    grad_gate = jnp.stack([jnp.sum(grad_top * value, axis=1) for value in values], axis=1)
    grad_pick = gates * (grad_gate - jnp.sum(gates * grad_gate, axis=1, keepdims=True))
    grad_route = jnp.sum(onehot * grad_pick[:, :, None], axis=1)
    g_hidden = jnp.sum(grad_top * hidden_val, axis=1)
    direct = jnp.sum(gates * (route_ids == NFFN + 1).astype(F32), axis=1)
    grad_mix = []
    grad_vec = []
    for j in range(2):
        weight = jnp.sum(gates * (route_ids == NFFN + 2 + j).astype(F32), axis=1)
        coef = coefficient[:, j]
        direct = direct + weight * coef[:, 0]
        grad_coef = jnp.stack(
            [weight * g_hidden, weight * jnp.sum(grad_top * vector_rows[2 + j][None, :], axis=1)], axis=1
        )
        grad_mix.append(coef * (grad_coef - jnp.sum(coef * grad_coef, axis=1, keepdims=True)))
        grad_vec.append(jnp.sum((weight * coef[:, 1])[:, None] * grad_top, axis=0))
    grad_logits = jnp.concatenate([grad_route, grad_mix[0], grad_mix[1]], axis=1)
    grad_hidden = direct[:, None] * grad_top + mm_tn(both_map, grad_buffer)
    grad_hidden = grad_hidden + jnp.dot(grad_logits, router_rows, precision=lax.Precision.HIGHEST)
    grad_router = jnp.einsum("te,td->ed", grad_logits, hidden_val, precision=lax.Precision.HIGHEST)
    grad_gain_two = jnp.sum(grad_hidden * (middle * scale_two), axis=0)
    grad_middle = grad_top + norm_back(grad_hidden, middle, scale_two, vector_rows[1])
    small = jnp.concatenate(
        [jnp.stack([jnp.zeros_like(grad_gain_two), grad_gain_two, grad_vec[0], grad_vec[1]]), grad_router], axis=0
    )

    grad_normed, apack, gup_all, gdn_all = backward_call(
        inner,
        grad_middle.astype(BF), attended, wo, qs, ks, vs, ohead, lse, jnp.broadcast_to(begin[None, :], (8, STREAM)),
        cosine, sine, turn, normed, packs, stream, small, gup, gdn,
    )

    scale_one = lax.rsqrt(jnp.mean(residual_in * residual_in, axis=-1, keepdims=True) + NORM_EPSILON)
    grad_tokens = grad_middle + norm_back(grad_normed, residual_in, scale_one, vector_rows[0])

    tiles = apack[:, :A_ROWS].reshape(4, 5, 96, 128)
    heads = [
        tiles[:, 0:3, :, :64].transpose(2, 0, 1, 3),
        tiles[:, 0:3, :, 64:].transpose(2, 0, 1, 3),
        jnp.stack([tiles[:, 3, :, :64], tiles[:, 3, :, 64:], tiles[:, 4, :, :64]], axis=1).transpose(2, 0, 1, 3),
    ]
    g_in = jnp.stack([head.reshape(96, D) for head in heads])
    g_out = apack[:, A_ROWS:A_ROWS + O_ROWS].reshape(6, 96, 128).transpose(1, 0, 2).reshape(96, D)
    g_small = jnp.sum(apack[:, A_ROWS + O_ROWS:, :96].astype(F32), axis=0)
    g_up = gup_all.reshape(NFFN, 2, 96, 2, 8, 128).transpose(0, 2, 3, 4, 1, 5).reshape(NFFN, 96, 2 * FF)
    g_down = gdn_all.reshape(NFFN, 256, D)
    grads = (
        scatter_inner(g_in.astype(F32), 1, inner),
        scatter_inner(g_out.astype(F32), 0, inner),
        scatter_inner(g_up.astype(F32), 1, inner),
        scatter_inner(g_down.astype(F32), 1, inner),
        scatter_inner(g_small[4:].T, 0, inner),
        scatter_inner(g_small[:4], 1, inner),
    )
    states = (
        (attend_in, attend_in_first, attend_in_second),
        (attend_out, attend_out_first, attend_out_second),
        (expert_up, expert_up_first, expert_up_second),
        (expert_down, expert_down_first, expert_down_second),
        (router_mix, router_mix_first, router_mix_second),
        (vectors, vectors_first, vectors_second),
    )
    results = []
    for kind, (weight, first, second) in enumerate(states):
        results.extend(adam_update(weight, grads[kind], first, second, STEP_RATES[kind], STEP_DECAYS[kind]))
    return (layer_out[None], grad_tokens[None], grad_route[None], *results)


def solution(mesh):
    token = P("shard", "seq", None)
    middle = P(None, "shard", None)
    front = P("shard", None)
    back = P(None, "shard")
    weights = (middle,) * 3 + (front,) * 3 + (middle,) * 6 + (front,) * 3 + (back,) * 3
    return jax.shard_map(
        local,
        mesh=mesh,
        in_specs=(token, token, front, token, P("shard", "seq"), token) + weights,
        out_specs=(token, token, token) + weights,
        check_vma=False,
    )
```

time: 2810 us -> 395 us (0.14)
  waiting for transfers between devices: 2260 us -> 0 us
  Pallas kernels: 0 us -> 285 us
  matrix products: 193 us -> 9.08 us
  blocking collectives: 104 us -> 0 us
  other arithmetic: 111 us -> 42.6 us
  local copies, waits for them, and re-layouts: 92.5 us -> 49.3 us
    reduce_scatter x3 -> x0, waiting for transfers between devices: 1270 us -> none  [the longest x1 793 us: local(): lax.psum_scatter(grad_w_up, 'shard', scatter_dimension=1, tiled=True)]
    all_gather x4 -> x0, waiting for transfers between devices: 594 us -> none  [the longest x1 394 us: local(): lax.all_gather(expert_up.astype(jnp.bfloat16), 'shard', axis=1, tiled=True)]
    pallas_call x0 -> x3, Pallas kernels: none -> 285 us  [the longest x1 136 us: backward_call(): pl.pallas_call(functools.partial(backward_kernel, inner), out_shape=[jax....]
    unnamed x14 -> x0, waiting for transfers between devices: 202 us -> none
    dot_general x38 -> x9, matrix products: 192 us -> 9.08 us  [the longest x3 5.09 us: mm_tn(): lax.dot_general(left, right, (((0,), (0,)), ((), ())), preferred_element_...]
    psum x1 -> x0, waiting for transfers between devices: 180 us -> none  [local(): lax.psum((small_shares[0], small_shares[1], up_share, down_share, small_s...]
    all_gather x2 -> x0, blocking collectives: 53.4 us -> none  [the longest x1 30.9 us: local(): lax.all_gather(router_mix.astype(jnp.bfloat16), 'shard', axis=0, tiled=True)]
    all_to_all x1 -> x0, blocking collectives: 40.5 us -> none  [local(): lax.all_to_all(grad_turned, 'seq', split_axis=1, concat_axis=2, tiled=True)]
  transfers between devices with their start and end apart: 14 -> 0, of which waited for: 12 -> 0; matrix products, arithmetic and copies ran while one was open for 5% -> 0% of each run, Pallas kernels for 0% -> 0%
where the time goes in v1:
time: 395 us; the launch traced here: 388 us
  Pallas kernels  285 us (72%)
  local copies, waits for them, and re-layouts  49.3 us (12%)
  other arithmetic  42.6 us (11%)
  matrix products  9.08 us (2%)
    pallas_call x1, Pallas kernels, backward_call(): pl.pallas_call(functools.partial(backward_kernel, inner), out_shape=[jax....  136 us
    pallas_call x1, Pallas kernels, forward_call(): pl.pallas_call(functools.partial(forward_kernel, inner), out_shape=[jax.S...  106 us
    pallas_call x1, Pallas kernels, expert_call(): pl.pallas_call(functools.partial(expert_kernel, inner), out_shape=[jax.Sh...  42.9 us
    sub x6, other arithmetic, adam_update(): return (weight - rate * (update + decay * weight), first_new, second_new)  25.8 us
    convert_element_type x2, local copies, waits for them, and re-layouts, local(): g_up.astype(F32)  16.7 us
    convert_element_type x2, local copies, waits for them, and re-layouts, expert_pieces(): ups = pick(ups, c, 4).reshape(2, 96, FF).astype(BF)  9.32 us

profile of v1, /device:TPU:0, one launch (start us, length us, event | category | flops | bytes accessed | tf_op | source)
XLA Modules:
  0.0 388.1 jit_solution(8330337717278442809)
XLA Ops:
  0.7 0.9 reduce-window_clone.1
  1.6 0.7 subtract_bitcast_fusion
  2.3 0.7 convert_element_type.113
  3.0 0.7 reduce.12
  3.7 1.3 compare_reduce_fusion.5
  5.1 0.7 reshape.315
  5.8 0.5 convert_reduce_fusion
  6.3 0.7 convert_bitcast_fusion
  7.2 0.2 dynamic_update_slice.3
  7.4 0.6 broadcast_in_dim.122.begin
  8.0 1.0 convert_element_type.112
  9.0 0.2 reshape.308
  9.3 1.2 dynamic-slice_convert_fusion.dn
  10.5 0.3 copy.122
  10.8 0.2 copy.123
  11.4 0.3 broadcast_in_dim.125.begin
  11.7 2.1 constant_dynamic-slice_fusion
  13.8 2.3 reshape.312
  16.1 7.1 %convert_reduce_fusion.1 = bf16[2,96,2,8,128]{4,3,2,1,0:T(8,128)(2,1)} fusion(bf16[2,96,2,8,2,128]{5,4,3,2,1,0:T(2,128)(2,1)} %reshape.312, s32[]{:T(128)S(6)} %select_n.64), kind=kLoop, calls=%fused_computation.28 | loop fusion | bytes 1572868 | tf_op jit(solution)/shard_map/convert_element_type | solution.py:451
  23.2 2.3 convert_element_type.116.up
  25.5 1.1 copy-done.3
  26.6 0.8 copy-done.8
  27.3 106.0 %gather_attend.1 = (bf16[4,384,768]{2,1,0:T(8,128)(2,1)}, bf16[8,720,128]{2,1,0:T(8,128)(2,1)}, bf16[8,576,128]{2,1,0:T(8,128)(2,1)}, bf16[8,96,2048]{2,1,0:T(8,...) custom-call(bf16[384,768]{1,0:T(8,128)(2,1)S(1)} %bitcast.150, ...), custom_call_target="tpu_custom_call" | custom-call | tf_op jit(solution)/shard_map/gather_attend/pallas_call | solution.py:404
  133.4 1.9 multiply_reduce_fusion.2
  135.3 0.6 add_rsqrt_fusion
  135.8 1.0 convert_reduce_fusion.2
  136.8 0.6 slice_reduce_fusion
  137.5 0.2 multiply_convert_fusion
  137.7 0.2 fusion.53
  137.9 0.2 copy-done.33
  138.5 0.5 convolution_convert_fusion
  139.0 0.6 fusion.33
  139.6 0.6 fusion.10
  140.2 0.8 copy-done.5
  141.0 42.9 %experts.1 = (bf16[4,96,768]{2,1,0:T(8,128)(2,1)S(1)}, bf16[4,96,768]{2,1,0:T(8,128)(2,1)S(1)}, bf16[8,96,2048]{2,1,0:T(8,128)(2,1)}, bf16[8,128,768]{2,1,0:T(8,128)(2,1)S(1)}) custom-call(bf16[4,96,768]{2,1,0:T(8,128)(2,1)S(1)} %bitcast.152, bf16[4,96,768]{2,1,0:T(8,128)(2,1)S(1)} %bitcast.151, bf16[8,96,2048]{2,1,0:T(8,128)(2,1)} %get-tuple-element.44.wup, ...), custom_call_target="tpu_custom_call" | custom-call | tf_op jit(solution)/shard_map/experts/pallas_call | solution.py:575
  183.9 0.8 fusion.8
  184.8 0.2 copy-done.4
  185.0 2.9 fusion.27
  187.9 0.6 stack.41
  188.5 0.6 stack.40
  189.2 1.0 fusion.55
  190.2 1.1 fusion.56
  191.4 1.4 multiply_reduce_fusion
  192.8 2.9 concatenate.35.small
  195.7 0.7 broadcast_multiply_fusion.1
  196.4 1.8 fusion.71.gbranch
  198.2 136.3 %attend_back.1 = (f32[384,768]{1,0:T(8,128)}, bf16[4,640,128]{2,1,0:T(8,128)(2,1)}, bf16[8,96,2048]{2,1,0:T(8,128)(2,1)}, bf16[8,128,768]{2,1,0:T(8,128)(2,1)}) custom-call(bf16[384,768]{1,0:T(8,128)(2,1)} %fusion.71.gbranch, bf16[384,768]{1,0:T(8,128)(2,1)} %copy-done.6, bf16[768,768]{1,0:T(8,128)(2,1)} %get-tuple-element.49.wo, ...), custom_call_target="tpu_custom_call" | custom-call | tf_op jit(solution)/shard_map/attend_back/pallas_call | solution.py:943
  334.6 1.7 fusion.11
  336.4 1.6 fusion.15
  338.1 0.6 multiply_subtract_fusion.5
  338.7 0.6 multiply_subtract_fusion.4
  339.9 0.8 copy.135
  340.9 0.2 copy.138
  341.0 0.8 copy.133
  342.0 0.8 copy.134
  342.9 2.2 multiply_subtract_fusion.3
  345.1 3.0 multiply_subtract_fusion.2
  348.0 1.0 copy.145
  349.0 7.6 %copy.137 = f32[4,96,2,8,2,128]{5,4,3,2,1,0:T(2,128)} copy(f32[4,96,2,8,2,128]{5,3,2,1,4,0:T(8,128)S(1)} %bitcast.156) | data formatting | bytes 12582912 | tf_op jit(solution)/shard_map/convert_element_type | solution.py:1151
  356.7 9.1 %reshape.323 = f32[4,96,4096]{2,1,0:T(8,128)} reshape(f32[4,96,2,8,2,128]{5,4,3,2,1,0:T(2,128)} %copy.137) | data formatting | bytes 12582912 | tf_op jit(solution)/shard_map/convert_element_type | solution.py:1151
  365.8 8.0 %multiply_subtract_fusion.1 = (f32[4,256,768]{2,1,0:T(8,128)}, f32[4,256,768]{2,1,0:T(8,128)}, f32[4,256,768]{2,1,0:T(8,128)}) fusion(f32[4,256,768]{2,1,0:T(8,128)} %param.42, f32[4,256,768]{2,1,0:T(8,128)} %param.43, f32[4,256,768]{2,1,0:T(8,128)} %param.44, bf16[4,256,768]{2,1,0:T(8,128)(2,1)} %bitcast.162), kind=kLoop, calls=%fused_computation.19 | loop fusion | flops 11796480 | bytes 20447232 | tf_op jit(solution)/shard_map/sub | solution.py:1019
  373.8 1.2 copy-done.9
  375.0 1.2 slice-done.1
  376.3 11.4 %multiply_subtract_fusion = (f32[4,96,4096]{2,1,0:T(8,128)}, f32[4,96,4096]{2,1,0:T(8,128)}, f32[4,96,4096]{2,1,0:T(8,128)}) fusion(f32[4,96,4096]{2,1,0:T(8,128)S(1)} %bitcast.158, f32[4,96,4096]{2,1,0:T(8,128)S(1)} %copy-done.9, f32[4,96,4096]{2,1,0:T(8,128)} %param.40, f32[4,96,4096]{2,1,0:T(8,128)} %param.41), kind=kLoop, calls=%fused_computation.4 | loop fusion | flops 22020096 | bytes 44040192 | tf_op jit(solution)/shard_map/sub | solution.py:1019
  (147 shorter events, 2.2 us)
Async XLA Ops:
  0.7 9.8 %copy-start.12 = (f32[3,96,768]{2,1,0:T(8,128)S(1)}, f32[3,96,768]{2,1,0:T(8,128)}, u32[]{:S(2)}) copy-start(f32[3,96,768]{2,1,0:T(8,128)} %param.33) | copy-start | bytes 2654212
  6.3 177.5 %copy-start.28 = (s32[384]{0:T(512)}, s32[384]{0:T(512)S(1)}, u32[]{:S(2)}) copy-start(s32[384]{0:T(512)S(1)} %get-tuple-element.200) | copy-start | bytes 4612
  6.3 178.4 %copy-start.30 = (s32[384]{0:T(512)}, s32[384]{0:T(512)S(1)}, u32[]{:S(2)}) copy-start(s32[384]{0:T(512)S(1)} %get-tuple-element.201) | copy-start | bytes 4612
  16.1 9.3 %copy-start.2 = (f32[1536,128]{1,0:T(8,128)S(1)}, f32[1536,128]{1,0:T(8,128)}, u32[]{:S(2)}) copy-start(f32[1536,128]{1,0:T(8,128)} %constant.160.clone.cos) | copy-start | bytes 2359300
  23.2 2.3 copy-start
  23.2 2.3 copy-start.1
  25.5 1.1 copy-start.3
  26.6 0.8 copy-start.8
  133.4 1.9 copy-start.6
  133.4 1.9 copy-start.7
  135.8 1.6 copy-start.23
  137.5 0.7 copy-start.33
  137.5 0.7 copy-start.22
  137.7 1.3 copy-start.10
  139.6 1.4 copy-start.5
  141.0 42.9 %copy-start.42 = (pred[384]{0:T(512)(128)(4,1)S(1)}, pred[384]{0:T(512)(128)(4,1)}, u32[]{:S(2)}) copy-start(pred[384]{0:T(512)(128)(4,1)} %get-tuple-element.151) | copy-start | bytes 1156
  141.0 42.9 %copy-start.43 = (pred[384]{0:T(512)(128)(4,1)S(1)}, pred[384]{0:T(512)(128)(4,1)}, u32[]{:S(2)}) copy-start(pred[384]{0:T(512)(128)(4,1)} %get-tuple-element.153) | copy-start | bytes 1156
  141.0 42.9 %copy-start.44 = (pred[384]{0:T(512)(128)(4,1)S(1)}, pred[384]{0:T(512)(128)(4,1)}, u32[]{:S(2)}) copy-start(pred[384]{0:T(512)(128)(4,1)} %get-tuple-element.154) | copy-start | bytes 1156
  183.8 1.1 copy-start.4
  183.9 1.1 copy-start.39
  183.9 1.1 copy-start.40
  183.9 1.1 copy-start.41
  187.9 3.4 copy-start.24
  187.9 3.4 copy-start.29
  187.9 3.5 copy-start.31
  189.2 3.5 copy-start.21
  198.2 136.3 %copy-start.26 = (f32[6,128]{1,0:T(8,128)S(1)}, f32[6,128]{1,0:T(8,128)}, u32[]{:S(2)}) copy-start(f32[6,128]{1,0:T(8,128)} %get-tuple-element.135) | copy-start | bytes 9220
  198.2 136.3 %copy-start.32 = (f32[384]{0:T(512)S(1)}, f32[384]{0:T(512)}, u32[]{:S(2)}) copy-start(f32[384]{0:T(512)} %get-tuple-element.209) | copy-start | bytes 4612
  334.5 1.8 copy-start.11
  334.5 1.8 copy-start.25
  336.3 1.7 copy-start.18
  336.3 1.7 copy-start.36
  336.3 1.7 copy-start.37
  336.3 1.7 copy-start.38
  336.3 2.3 copy-start.27
  336.4 2.3 copy-start.34
  336.4 2.3 copy-start.35
  340.7 2.1 copy-start.15
  341.8 3.2 copy-start.17
  342.0 3.0 copy-start.13
  342.0 3.0 copy-start.16
  342.8 2.2 copy-start.19
  342.8 2.2 copy-start.20
  345.1 3.0 copy-start.14
  356.7 17.1 %slice-start = ((s8[6291456]{0:T(1024)(128)(4,1)}), s8[2097152]{0:T(1024)(128)(4,1)S(1)}, s32[]{:S(2)}) async-start(s8[6291456]{0:T(1024)(128)(4,1)} %bitcast.157), calls=%async_computation | async-start | bytes 4194304
  365.8 9.3 %copy-start.9 = (f32[4,96,4096]{2,1,0:T(8,128)S(1)}, f32[4,96,4096]{2,1,0:T(8,128)}, u32[]{:S(2)}) copy-start(f32[4,96,4096]{2,1,0:T(8,128)} %reshape.323) | copy-start | bytes 18874372
  365.8 10.5 %slice-start.1 = ((s8[6291456]{0:T(1024)(128)(4,1)}), s8[4194304]{0:T(1024)(128)(4,1)S(1)}, s32[]{:S(2)}) async-start(s8[6291456]{0:T(1024)(128)(4,1)} %bitcast.157), calls=%async_computation.1 | async-start | bytes 8388608

commit v2 on v0

v2 whole, which is shorter than its diff:
```python
import functools

import jax
import jax.numpy as jnp
import numpy as np
from jax import lax
from jax.experimental import pallas as pl
from jax.experimental.pallas import tpu as pltpu
from jax.sharding import PartitionSpec as P

D = 768
HEADS = 12
HEAD_DIM = 64
FF = 2048
NFFN = 4
NEXP = 8
TOPK = 2
STEP = 5
CAP = 96
LINE = 4
OUTER = 8
LOCAL_HEADS = 3

NORM_EPSILON = 1e-05
ROPE_BASE = 10000.0
NEGATIVE = -1e30
MOMENT_DECAY = 0.5
ADAM_EPSILON = 1e-08
STEP_RATES = (0.04, 0.1, 0.04, 0.02, 0.02, 0.2)
STEP_DECAYS = (0.1, 0.1, 0.1, 0.1, 0.1, 0.0)
BF = jnp.bfloat16
F32 = jnp.float32
MESH = pl.DeviceIdType.MESH
VMEM_LIMIT = 58 * 2**20


def mm(left, right):
    return jnp.dot(left, right, preferred_element_type=F32)


def mm_nt(left, right):
    return lax.dot_general(left, right, (((1,), (1,)), ((), ())), preferred_element_type=F32)


def mm_tn(left, right):
    return lax.dot_general(left, right, (((0,), (0,)), ((), ())), preferred_element_type=F32)


class Place:
    def __init__(self, inner):
        q = lax.axis_index("seq")
        shard = lax.axis_index("shard")
        self.inner = inner
        self.rest = lax.rem(shard, inner) if inner > 1 else 0
        outer = lax.div(shard, inner) if inner > 1 else shard
        self.q = q
        self.x = lax.div(q, 2)
        self.c = lax.rem(q, 2)
        self.l = lax.div(outer, 2)
        self.y = lax.rem(outer, 2)
        self.own = outer

    def at(self, x=None, c=None, l=None, y=None):
        x = self.x if x is None else x
        c = self.c if c is None else c
        l = self.l if l is None else l
        y = self.y if y is None else y
        return (2 * x + c, (2 * l + y) * self.inner + self.rest)


def greet(me, devices, line):
    barrier = pltpu.get_barrier_semaphore()
    for device in devices:
        pl.semaphore_signal(barrier, inc=1, device_id=device, device_id_type=MESH)
    if not line:
        pl.semaphore_wait(barrier, len(devices))
        return

    @pl.when(me.l > 0)
    def _():
        pl.semaphore_signal(barrier, inc=1, device_id=me.at(l=me.l - 1), device_id_type=MESH)

    @pl.when(me.l < LINE - 1)
    def _():
        pl.semaphore_signal(barrier, inc=1, device_id=me.at(l=me.l + 1), device_id_type=MESH)

    near = jnp.minimum(me.l, 1) + jnp.minimum(LINE - 1 - me.l, 1)
    pl.semaphore_wait(barrier, len(devices) + near)


def remote(src, dst, send, recv, device):
    return pltpu.make_async_remote_copy(
        src_ref=src, dst_ref=dst, send_sem=send, recv_sem=recv, device_id=device, device_id_type=MESH
    )


def rope_constants(stream_len):
    frequency = ROPE_BASE ** (-(np.arange(HEAD_DIM // 2, dtype=np.float64) * 2.0 / HEAD_DIM))
    angles = np.arange(stream_len, dtype=np.float64)[:, None] * frequency[None, :]
    cosine = np.tile(np.cos(angles), (1, 4)).astype(np.float32)
    sine = np.tile(np.sin(angles), (1, 4)).astype(np.float32)
    turn = np.zeros((128, 128), np.float32)
    for j in range(128):
        if j % 64 < 32:
            turn[j + 32, j] = -1.0
        else:
            turn[j - 32, j] = 1.0
    return cosine, sine, turn


A_ROWS = 5 * 96
O_ROWS = 144
S_ROWS = 96
PACK = A_ROWS + O_ROWS + S_ROWS
PACKG = A_ROWS + O_ROWS + 16
TOK = 384
STREAM = 1536
ATT = 576
HALF = TOK // 2
BLOCK = 256
KEYS = 512
ROWS = 128


class Counter:
    def __init__(self):
        self.used = 0

    def take(self, count):
        first = self.used
        self.used += count
        return first


def semaphores():
    s, r = Counter(), Counter()
    send = {
        "tok": s.take(3), "pack": s.take(12), "wo": s.take(3), "ex": s.take(34), "att": s.take(3),
        "row": s.take(6), "core": s.take(8), "part": s.take(2), "back": s.take(6),
        "line": s.take(32), "att2": s.take(3), "wo2": s.take(3), "ay": s.take(4), "al": s.take(8), "gn": s.take(3),
        "aa": s.take(3), "gp": s.take(14),
    }
    recv = {
        "tok": r.take(3), "pack": r.take(8), "wo": r.take(3), "ex": r.take(16), "att": r.take(3),
        "row": r.take(8), "core": r.take(8), "part": r.take(2), "back": r.take(8),
        "line": r.take(32), "att2": r.take(3), "wo2": r.take(3), "ay": r.take(4), "al": r.take(8), "gn": r.take(3),
        "aa": r.take(3), "gp": r.take(16),
    }
    return send, recv, s.used, r.used


def small_rows(packs):
    tiles = []
    for t in range(6):
        first = A_ROWS + O_ROWS + 16 * t
        total = packs[0, first:first + 16, :].astype(F32)
        for s in range(1, OUTER):
            total = total + packs[s, first:first + 16, :].astype(F32)
        tiles.append(total)
    return jnp.concatenate(tiles, axis=1)


def split_low(values):
    high = values.astype(BF)
    return high, (values - high.astype(F32)).astype(BF)


def layer_kernel(
    inner,
    tok, gout_in, w_in, w_out, w_up, w_dn, cos_in, sin_in, turn, lengths, routes, residual, priority, router, vectors,
    layer_out, gtokens, groute, apack, gup_all, gdn_all,
    stream, packs, wo_all, wo, wup, wdn, ringx_up, ringx_dn, gup, gdn, rowh, rowg, part_in, ret, got, wo_in,
    ap_in, ap_line, gn_ret, normed, qk, vo, ks, lse, attended, hidden, cos, sin, gout, bufs, begin,
    cols, facts, ss, rs, ls, ready,
):
    me = Place(inner)
    x, c, l, y, q, own = me.x, me.c, me.l, me.y, me.q, me.own
    nx, nc, ny = 1 - x, 1 - c, 1 - y
    mine = 2 * x + y
    S, R, _, _ = semaphores()
    chips = [(x, ny), (nx, y), (nx, ny)]
    others = [(2 * nx + c, me.at(x=nx)), (2 * nx + nc, me.at(x=nx, c=nc)), (2 * x + nc, me.at(c=nc))]

    def load(src, dst, k):
        return pltpu.make_async_copy(src, dst, ls.at[k])

    def tok_copy(k, part, device):
        return remote(stream.at[part], stream.at[part], ss.at[S["tok"] + k], rs.at[R["tok"] + k], device)

    def pack_copy(kind, z, device):
        slot = 2 * z + y
        return remote(
            packs.at[slot], packs.at[slot], ss.at[S["pack"] + 4 * kind + z], rs.at[R["pack"] + slot], device
        )

    def pack_wait(slot):
        remote(packs.at[slot], packs.at[slot], ss.at[0], rs.at[R["pack"] + slot], me.at(y=ny)).wait_recv()

    def pack_up(z):
        @pl.when(l < LINE - 1)
        def _():
            pack_copy(0, z, me.at(l=l + 1)).start()

    def pack_down(z):
        @pl.when(l > 0)
        def _():
            pack_copy(1, z, me.at(l=l - 1)).start()

    def pack_over(z):
        pack_copy(2, z, me.at(y=ny)).start()

    def pack_step(step):
        @pl.when(l - step >= 0)
        def _():
            pack_wait(2 * (l - step) + y)
            pack_up(l - step)
            pack_over(l - step)

        @pl.when(l + step < LINE)
        def _():
            pack_wait(2 * (l + step) + y)
            pack_down(l + step)
            pack_over(l + step)

    weights = (wup, wdn)

    def ex_copy(kind, n, z, yy, device):
        slot = 2 * z + yy
        k = 2 * (8 * kind + slot) + n
        ref = weights[n]
        return remote(ref.at[slot], ref.at[slot], ss.at[S["ex"] + k], rs.at[R["ex"] + 2 * slot + n], device)

    def ex_wait(slot):
        for n, ref in enumerate(weights):
            remote(ref.at[slot], ref.at[slot], ss.at[0], rs.at[R["ex"] + 2 * slot + n], me.at(y=ny)).wait_recv()

    def ex_forward(z, yy, upward, kinds=(0, 1)):
        if upward:
            @pl.when(l < LINE - 1)
            def _():
                for n in kinds:
                    ex_copy(0, n, z, yy, me.at(l=l + 1)).start()
        else:
            @pl.when(l > 0)
            def _():
                for n in kinds:
                    ex_copy(1, n, z, yy, me.at(l=l - 1)).start()

    def relay(step, yy):
        @pl.when(l - step >= 0)
        def _():
            ex_wait(2 * (l - step) + yy)
            ex_forward(l - step, yy, True)

        @pl.when(l + step < LINE)
        def _():
            ex_wait(2 * (l + step) + yy)
            ex_forward(l + step, yy, False)

    def wo_copy(k, part, device):
        rows = pl.ds(pl.multiple_of(part * O_ROWS, O_ROWS), O_ROWS)
        return remote(
            wo_all.at[:, rows, :], wo_all.at[:, rows, :], ss.at[S["wo"] + k], rs.at[R["wo"] + k], device
        )

    def row_copy(n, k, cx, cy):
        row = (rowh, rowg)[n]
        return remote(
            bufs.at[n, 2 * cx + cy], row.at[4 * c + mine], ss.at[S["row"] + 3 * n + k], rs.at[R["row"] + 4 * n + mine],
            me.at(x=cx, y=cy)
        )

    def row_wait(n, cx, cy):
        row, slot = (rowh, rowg)[n], 2 * cx + cy
        remote(
            row.at[4 * c + slot], row.at[4 * c + slot], ss.at[0], rs.at[R["row"] + 4 * n + slot], me.at(x=cx, y=cy)
        ).wait_recv()

    def core_copy(n, k, first, slot):
        row = (rowh, rowg)[n]
        return remote(
            row.at[first + slot], row.at[first + slot], ss.at[S["core"] + 4 * n + k], rs.at[R["core"] + 4 * n + slot],
            me.at(c=nc)
        )

    def row_send(n):
        for k, (cx, cy) in enumerate(chips):
            row_copy(n, k, cx, cy).start()
        (rowh, rowg)[n][4 * c + mine] = bufs[n, mine]
        core_copy(n, 0, 4 * c, mine).start()

    def row_pass(n):
        for k, (cx, cy) in enumerate(chips):
            row_wait(n, cx, cy)
            core_copy(n, 1 + k, 4 * c, 2 * cx + cy).start()

    def row_collect(n):
        for slot in range(4):
            core_copy(n, 0, 4 * nc, slot).wait_recv()

    def back_copy(n, k, cx, cy):
        return remote(
            bufs.at[n, 2 * cx + cy], ret.at[n, mine], ss.at[S["back"] + 3 * n + k], rs.at[R["back"] + 4 * n + mine],
            me.at(x=cx, y=cy)
        )

    def back_wait(n, cx, cy):
        slot = 2 * cx + cy
        remote(
            ret.at[n, slot], ret.at[n, slot], ss.at[0], rs.at[R["back"] + 4 * n + slot], me.at(x=cx, y=cy)
        ).wait_recv()

    loads = [
        load(tok, stream.at[q], 0), load(cos_in, cos, 1), load(sin_in, sin, 2), load(gout_in, gout, 3),
    ]
    for copy in loads:
        copy.start()

    def forward(st_in, st_out, st_up, st_dn, upx, dnx, wo_tiles, wq, wr, pk, begin_col):
        from_hbm = [load(w_in, st_in, 4), load(w_out, st_out, 5)]
        experts = [2 * x + y, 2 * x + ny]
        from_hbm += [load(w_up.at[e], st_up.at[k], 6 + k) for k, e in enumerate(experts)]
        half_rows = pl.ds(pl.multiple_of(128 * c, 128), 128)
        from_hbm += [load(w_dn.at[e, half_rows, :], st_dn.at[k], 8 + k) for k, e in enumerate(experts)]
        for copy in from_hbm:
            copy.start()
        greet(me, [me.at(c=nc), me.at(x=nx), me.at(x=nx, c=nc), me.at(y=ny), me.at(x=nx, y=ny)], True)
        loads[0].wait()
        tok_copy(1, q, me.at(x=nx)).start()
        tok_copy(0, q, me.at(c=nc)).start()

        from_hbm[0].wait()
        from_hbm[1].wait()
        for t in range(6):
            wo_tiles[96 * t:96 * (t + 1), :] = st_out[:, 128 * t:128 * (t + 1)].astype(BF)
        for part in range(4):

            @pl.when(q == part)
            def _():
                def head(kind, h):
                    first = 192 * part + 64 * h
                    return st_in[kind, :, first:first + 64]

                tiles = [(head(0, h), head(1, h)) for h in range(LOCAL_HEADS)]
                tiles += [(head(2, 0), head(2, 1)), (head(2, 2), jnp.zeros((96, 64), F32))]
                for t, pair in enumerate(tiles):
                    packs[own, 96 * t:96 * (t + 1), :] = jnp.concatenate(pair, axis=1).astype(BF)

        rows = pl.ds(pl.multiple_of(q * O_ROWS, O_ROWS), O_ROWS)
        packs[own, A_ROWS:A_ROWS + O_ROWS, :] = wo_tiles[rows, :]
        small = jnp.concatenate([router[...], vectors[...]], axis=0)
        small = jnp.concatenate([small, jnp.zeros((16, 32), F32)], axis=1).astype(BF)
        to_col = lax.broadcasted_iota(jnp.int32, (128, D), 1) - 96 * own
        from_row = lax.broadcasted_iota(jnp.int32, (128, D), 0)
        place = ((to_col == from_row) & (from_row < 96)).astype(F32).astype(BF)
        placed = mm(small, place).astype(BF)
        for t in range(6):
            first = A_ROWS + O_ROWS + 16 * t
            packs[own, first:first + 16, :] = placed[:, 128 * t:128 * (t + 1)]
        pack_up(l)
        pack_down(l)
        pack_over(l)

        for k in range(2):
            from_hbm[4 + k].wait()
        wdn[own] = st_dn[0].astype(BF)
        ex_forward(l, y, True, (1,))
        ex_forward(l, y, False, (1,))
        dnx[...] = st_dn[1].astype(BF)
        for k in range(2):
            from_hbm[2 + k].wait()
        for j in range(16):
            part = pl.ds(pl.multiple_of(256 * j + 128 * c, 128), 128)
            wup[own, :, 128 * j:128 * (j + 1)] = st_up[0, :, part].astype(BF)
            upx[:, 128 * j:128 * (j + 1)] = st_up[1, :, part].astype(BF)

        pack_step(1)
        pack_step(2)
        tok_copy(1, 2 * nx + c, me.at(x=nx)).wait_recv()
        tok_copy(2, 2 * nx + c, me.at(c=nc)).start()
        pack_step(3)
        ex_forward(l, y, True, (0,))
        ex_forward(l, y, False, (0,))

        def ex_over(n):
            return remote(
                (upx, dnx)[n], weights[n].at[own], ss.at[S["ex"] + 32 + n], rs.at[R["ex"] + 2 * own + n], me.at(y=ny)
            )

        for n in range(2):
            ex_over(n).start()

        ids = lax.broadcasted_iota(jnp.int32, (8, STREAM), 1)
        first = lengths[0, 0] * 0
        at = jnp.zeros((8, STREAM), jnp.int32)
        for k in range(8):
            at = jnp.maximum(at, jnp.where(ids >= first, first, 0))
            first = first + lengths[0, k]
        begin[...] = at
        begin_col[...] = jnp.transpose(jnp.broadcast_to(at[0:1].astype(F32), (128, STREAM)))

        for z in range(LINE):
            pack_wait(2 * z + ny)
        wo_all[:, rows, :] = packs[:, A_ROWS:A_ROWS + O_ROWS, :]
        wo_copy(1, q, me.at(x=nx)).start()
        wo_copy(0, q, me.at(c=nc)).start()
        for s in range(OUTER):
            for t in range(5):
                wq[t, 96 * s:96 * (s + 1), :] = packs[s, 96 * t:96 * (t + 1), :]
        for t in range(LOCAL_HEADS):
            wr[t] = mm(wq[t], turn[...]).astype(BF)
        gain = small_rows(packs)[12:13]
        tok_copy(0, 2 * x + nc, me.at(c=nc)).wait_recv()
        tok_copy(2, 2 * nx + nc, me.at(c=nc)).wait_recv()
        loads[1].wait()
        loads[2].wait()

        halves = jnp.where(lax.broadcasted_iota(jnp.int32, (1, 128), 1) < 64, 0.125, 1.0)

        @pl.loop(0, 4)
        def _(part):
            values = stream[part].astype(F32)
            scale = lax.rsqrt(jnp.mean(values * values, axis=1, keepdims=True) + NORM_EPSILON)
            rows = pl.ds(pl.multiple_of(part * TOK, TOK), TOK)
            low = (values * scale * gain).astype(BF)
            normed[rows, :] = low
            cosine, sine = cos[rows, :], sin[rows, :]
            for h in range(LOCAL_HEADS):
                turned = mm(low, wq[h]) * cosine + mm(low, wr[h]) * sine
                qk[h, rows, :] = (turned * halves).astype(BF)
            both = mm(low, wq[3]).astype(BF)
            vo[0, rows, 0:64] = both[:, :64]
            vo[1, rows, 0:64] = both[:, 64:]
            vo[2, rows, 0:64] = mm(low, wq[4])[:, :64].astype(BF)

        ex_wait(2 * l + ny)
        ex_forward(l, ny, True)
        ex_forward(l, ny, False)

        def one_head(h):
            ks[...] = qk[h, :, 64:128]
            for b in range(STREAM // BLOCK):
                first, last = b * BLOCK, (b + 1) * BLOCK
                scores = mm_nt(qk[h, first:last, 0:64], ks[0:last, :])
                col = lax.broadcasted_iota(jnp.int32, (BLOCK, last), 1)
                row = lax.broadcasted_iota(jnp.int32, (BLOCK, last), 0) + first
                starts = begin_col[first:last, 0:1].astype(jnp.int32)
                scores = jnp.where((col >= starts) & (col <= row), scores, NEGATIVE)
                top = jnp.max(scores, axis=1, keepdims=True)
                weight = jnp.exp(scores - top)
                total = jnp.sum(weight, axis=1, keepdims=True)
                vo[h, first:last, 64:128] = (mm(weight.astype(BF), vo[h, 0:last, 0:64]) / total).astype(BF)
                logs = jnp.broadcast_to(top + jnp.log(total), (BLOCK, 128))
                lse[h, :, first:last] = jnp.transpose(logs)[0:8, :]

        pl.loop(0, 1)(one_head)
        wo_copy(1, 2 * nx + c, me.at(x=nx)).wait_recv()
        wo_copy(2, 2 * nx + c, me.at(c=nc)).start()
        relay(1, y)
        pl.loop(1, LOCAL_HEADS)(one_head)

        for part in range(4):
            rows = slice(part * TOK, (part + 1) * TOK)
            pk[part, 0:TOK, :] = jnp.concatenate([vo[0, rows, 64:128], vo[1, rows, 64:128]], axis=1)
            third = [vo[2, part * TOK + k * HALF:part * TOK + (k + 1) * HALF, 64:128] for k in range(2)]
            pk[part, TOK:ATT, :] = jnp.concatenate(third, axis=1)
        got[q] = pk[q]

        def att_copy(k, to, frm, device):
            return remote(pk.at[to], got.at[frm], ss.at[S["att"] + k], rs.at[R["att"] + k], device)

        for k, (other, device) in enumerate(others):
            att_copy(k, other, q, device).start()
        relay(1, ny)

        wo_copy(0, 2 * x + nc, me.at(c=nc)).wait_recv()
        wo_copy(2, 2 * nx + nc, me.at(c=nc)).wait_recv()
        for s in range(OUTER):
            for t in range(6):
                wo[96 * s:96 * (s + 1), 128 * t:128 * (t + 1)] = wo_all[s, 96 * t:96 * (t + 1), :]
        for k, (other, device) in enumerate(others):
            att_copy(k, q, other, device).wait_recv()
        pieces = []
        for part in range(4):
            low = got[part, TOK:ATT, :]
            pieces.append(got[part, 0:TOK, :])
            pieces.append(jnp.concatenate([low[:, :64], low[:, 64:]], axis=0))
        whole = jnp.concatenate(pieces, axis=1)
        attended[...] = whole
        middle = stream[q].astype(F32) + mm(whole, wo[...])
        gtokens[...] = middle

        smalls = small_rows(packs)
        scale = lax.rsqrt(jnp.mean(middle * middle, axis=1, keepdims=True) + NORM_EPSILON)
        low = (middle * scale * smalls[13:14]).astype(BF)
        hidden[...] = low
        logits = mm_nt(smalls.astype(BF), low)
        route_logits = logits[0:8] + residual[...]
        expert_row = lax.broadcasted_iota(jnp.int32, (8, TOK), 0)
        picks = [routes[k:k + 1, :] for k in range(TOPK)]
        picked = [
            jnp.sum(jnp.where(expert_row == pick, route_logits, 0.0), axis=0, keepdims=True) for pick in picks
        ]

        def pair_softmax(first, second):
            top = jnp.maximum(first, second)
            one, two = jnp.exp(first - top), jnp.exp(second - top)
            return [one / (one + two), two / (one + two)]

        gates = pair_softmax(*picked)
        coefs = pair_softmax(logits[8:9], logits[9:10]) + pair_softmax(logits[10:11], logits[11:12])
        expert = jnp.concatenate(picks, axis=1).astype(F32)
        order = jnp.concatenate([priority[...], priority[...] + STREAM], axis=1).astype(F32)
        base = expert * 4096.0
        rank_key = base + order
        key_rows = jnp.transpose(jnp.broadcast_to(rank_key, (128, 2 * TOK)))[:, 0:1]
        ahead = jnp.where((key_rows < rank_key) & (key_rows >= base), 1.0, 0.0)
        rank = jnp.sum(ahead, axis=0, keepdims=True)
        slot = jnp.where((expert < NFFN) & (rank < CAP), expert * CAP + rank, -1.0)
        slots = [slot[:, :TOK], slot[:, TOK:]]
        lanes = gates + coefs + slots + [pick.astype(F32) for pick in picks]
        lanes = jnp.concatenate(lanes + [jnp.zeros((128 - len(lanes), TOK), F32)], axis=0)
        cols[...] = jnp.transpose(lanes)
        slot_row = lax.broadcasted_iota(jnp.int32, (NFFN * CAP, TOK), 0).astype(F32)
        maps = [(slot_row == slots[k]).astype(F32).astype(BF) for k in range(TOPK)]
        bufs[0] = mm(maps[0] + maps[1], low).astype(BF).reshape(NFFN, CAP, D)
        row_send(0)
        loads[3].wait()
        grad_top = gout[...].astype(F32)
        grad_rows = sum(mm(maps[k], (cols[:, k:k + 1] * grad_top).astype(BF)) for k in range(TOPK))
        bufs[1] = grad_rows.astype(BF).reshape(NFFN, CAP, D)
        row_send(1)

        for n in range(2):
            ex_over(n).wait_send()
        for k, (other, device) in enumerate(others):
            att_copy(k, other, q, device).wait_send()

    pl.run_scoped(
        forward,
        pltpu.VMEM((3, 96, D), F32),
        pltpu.VMEM((96, D), F32),
        pltpu.VMEM((2, 96, 2 * FF), F32),
        pltpu.VMEM((2, 128, D), F32),
        pltpu.VMEM((96, FF), BF),
        pltpu.VMEM((128, D), BF),
        pltpu.VMEM((576, 128), BF),
        pltpu.VMEM((5, D, 128), BF),
        pltpu.VMEM((3, D, 128), BF),
        pltpu.VMEM((4, ATT, 128), BF),
        pltpu.VMEM((STREAM, 128), F32),
    )
    relay(2, y)
    row_pass(0)
    relay(2, ny)
    row_pass(1)
    row_collect(0)
    row_collect(1)

    def experts(rowt, down_sum, back_sum, part_out):
        rowt[...] = jnp.transpose(rowh[...].reshape(8 * CAP, D).astype(F32)).astype(BF)
        down_sum[...] = jnp.zeros_like(down_sum)
        back_sum[...] = jnp.zeros_like(back_sum)
        relay(3, y)
        relay(3, ny)

        @pl.loop(0, 4)
        def _(j):
            gate_cols = pl.ds(pl.multiple_of(j * 256, 256), 256)
            lin_cols = pl.ds(pl.multiple_of(1024 + j * 256, 256), 256)
            rows_h = rowh[...].reshape(8 * CAP, D)
            rows_g = rowg[...].reshape(8 * CAP, D)
            w_gate = wup[:, :, gate_cols].reshape(D, 256)
            w_lin = wup[:, :, lin_cols].reshape(D, 256)
            w_down = wdn[pl.ds(2 * j, 2)].reshape(256, D)
            gate = mm(rows_h, w_gate)
            lin = mm(rows_h, w_lin)
            grad_act = mm_nt(rows_g, w_down)
            sigma = jax.nn.sigmoid(gate)
            silu = gate * sigma
            low = (silu * lin).astype(BF)
            down_sum[...] += mm(low, w_down)
            grad_gate = (grad_act * lin * sigma * (1.0 + gate * (1.0 - sigma))).astype(BF)
            grad_lin = (grad_act * silu).astype(BF)
            back_sum[...] += mm_nt(grad_gate, w_gate) + mm_nt(grad_lin, w_lin)
            gdn[pl.ds(2 * j, 2)] = mm_tn(low, rows_g).astype(BF).reshape(2, 128, D)
            gup[:, :, gate_cols] = mm(rowt[...], grad_gate).astype(BF).reshape(8, 96, 256)
            gup[:, :, lin_cols] = mm(rowt[...], grad_lin).astype(BF).reshape(8, 96, 256)

        for z in range(LINE):
            for yy in range(2):
                for n in range(2):

                    @pl.when((l >= z) & (l < LINE - 1))
                    def _():
                        ex_copy(0, n, z, yy, me.at(l=l + 1)).wait_send()

                    @pl.when((l <= z) & (l > 0))
                    def _():
                        ex_copy(1, n, z, yy, me.at(l=l - 1)).wait_send()

        @pl.when(l < LINE - 1)
        def _():
            pl.semaphore_signal(ready.at[0], inc=1, device_id=me.at(l=l + 1), device_id_type=MESH)

        @pl.when(l > 0)
        def _():
            pl.semaphore_signal(ready.at[1], inc=1, device_id=me.at(l=l - 1), device_id_type=MESH)

        for n in range(2):
            for k, (cx, cy) in enumerate(chips):
                row_copy(n, k, cx, cy).wait_send()

        def swap(n):
            return remote(
                part_out.at[n], part_in.at[n], ss.at[S["part"] + n], rs.at[R["part"] + n], me.at(c=nc)
            )

        sums = (down_sum, back_sum)
        away = pl.ds(pl.multiple_of(nc * 4 * CAP, 4 * CAP), 4 * CAP)
        here = pl.ds(pl.multiple_of(c * 4 * CAP, 4 * CAP), 4 * CAP)
        for n in range(2):
            part_out[n] = sums[n][away, :].astype(BF).reshape(4, CAP, D)
            swap(n).start()
        for n in range(2):
            swap(n).wait_recv()
            kept = sums[n][here, :].reshape(4, CAP, D)
            bufs[n] = (kept + part_in[n].astype(F32)).astype(BF)
            for k, (cx, cy) in enumerate(chips):
                back_copy(n, k, cx, cy).start()
            ret[n, mine] = bufs[n, mine]
        for n in range(2):
            swap(n).wait_send()

    pl.run_scoped(
        experts,
        pltpu.VMEM((D, 8 * CAP), BF),
        pltpu.VMEM((8 * CAP, D), F32),
        pltpu.VMEM((8 * CAP, D), F32),
        pltpu.VMEM((2, 4, CAP, D), BF),
    )

    kinds = ((gup, wup, ringx_up, gup_all), (gdn, wdn, ringx_dn, gdn_all))

    def line_copy(d, z, yy, n, src, device, last):
        k = ((d * 4 + z) * 2 + yy) * 2 + n
        dst = kinds[n][2].at[yy] if last and d == 1 else kinds[n][1].at[2 * z + yy]
        return remote(src, dst, ss.at[S["line"] + k], rs.at[R["line"] + k], device)

    def first_sends(d, order, device):
        for z in order:
            for yy in range(2):
                for n in range(2):
                    line_copy(d, z, yy, n, kinds[n][0].at[2 * z + yy], device, z == order[2]).start()

    @pl.when(l < LINE - 1)
    def _():
        pl.semaphore_wait(ready.at[1], 1)

    @pl.when(l > 0)
    def _():
        pl.semaphore_wait(ready.at[0], 1)

    @pl.when(l == 0)
    def _():
        first_sends(0, (3, 2, 1), me.at(l=l + 1))

    @pl.when(l == LINE - 1)
    def _():
        first_sends(1, (0, 1, 2), me.at(l=l - 1))

    def add_own(n, slot):
        own_ref, ring = kinds[n][0], kinds[n][1]

        @pl.loop(0, own_ref.shape[1] // 16)
        def _(r):
            part = pl.ds(pl.multiple_of(r * 16, 16), 16)
            total = own_ref[slot, part, :].astype(F32) + ring[slot, part, :].astype(F32)
            ring[slot, part, :] = total.astype(BF)

    def line_step(t, yy):
        for d in range(2):
            far = l if d == 0 else LINE - 1 - l
            z = 3 + l - t if d == 0 else t - 3 + l

            @pl.when((far >= 1) & (far <= t))
            def _():
                device = me.at(l=l + 1) if d == 0 else me.at(l=l - 1)
                for n in range(2):
                    slot = 2 * z + yy
                    ring = kinds[n][1]
                    line_copy(d, z, yy, n, ring.at[slot], me.at(y=ny), t == 3).wait_recv()
                    if t < 3:
                        add_own(n, slot)
                        line_copy(d, z, yy, n, ring.at[slot], device, t == 2).start()

    for n in range(2):
        for cx, cy in chips:
            back_wait(n, cx, cy)
    smalls = small_rows(packs)
    down_rows = ret[0].reshape(NFFN * CAP, D)
    back_rows = ret[1].reshape(NFFN * CAP, D)
    vector = [smalls[14 + j:15 + j] for j in range(2)]
    router_row = lax.broadcasted_iota(jnp.int32, (16, 1), 0)
    router_low = jnp.where(router_row < 12, smalls, 0.0)
    router_low = jnp.concatenate([router_low, jnp.zeros((112, D), F32)], axis=0).astype(BF)
    facts[...] = jnp.zeros_like(facts)

    @pl.loop(0, TOK // ROWS)
    def _(i):
        rows = pl.ds(pl.multiple_of(i * ROWS, ROWS), ROWS)
        middle = gtokens[rows, :]
        low = hidden[rows, :]
        grad_low = gout[rows, :]
        info = cols[rows, :]
        token_lane = lax.broadcasted_iota(jnp.int32, (ROWS, NFFN * CAP), 1).astype(F32)
        gates = [info[:, k:k + 1] for k in range(TOPK)]
        coefs = [[info[:, 2 + 2 * j:3 + 2 * j], info[:, 3 + 2 * j:4 + 2 * j]] for j in range(2)]
        spread = [(token_lane == info[:, 6 + k:7 + k]).astype(F32).astype(BF) for k in range(TOPK)]
        picks = [info[:, 8 + k:9 + k] for k in range(TOPK)]
        chosen = [[(pick == e).astype(F32) for e in (5.0, 6.0, 7.0)] for pick in picks]
        grad_top = grad_low.astype(F32)
        value_hidden = low.astype(F32)
        grad_gate, mixture = [], middle
        for k in range(TOPK):
            copy, one, two = chosen[k]
            value = mm(spread[k], down_rows)
            value = value + (copy + one * coefs[0][0] + two * coefs[1][0]) * value_hidden
            value = value + (one * coefs[0][1]) * vector[0] + (two * coefs[1][1]) * vector[1]
            mixture = mixture + gates[k] * value
            grad_gate.append(jnp.sum(grad_top * value, axis=1, keepdims=True))
        layer_out[rows, :] = mixture.astype(BF)
        mean_gate = gates[0] * grad_gate[0] + gates[1] * grad_gate[1]
        grad_pick = [gates[k] * (grad_gate[k] - mean_gate) for k in range(TOPK)]
        lane = lax.broadcasted_iota(jnp.int32, (ROWS, 128), 1).astype(F32)
        grad_logits = sum(jnp.where(lane == picks[k], grad_pick[k], 0.0) for k in range(TOPK))
        groute[rows, :] = grad_logits[:, :NEXP]
        on_hidden = jnp.sum(grad_top * value_hidden, axis=1, keepdims=True)
        direct = gates[0] * chosen[0][0] + gates[1] * chosen[1][0]
        on_vectors = jnp.zeros((ROWS, 128), F32)
        for j in range(2):
            weight = gates[0] * chosen[0][1 + j] + gates[1] * chosen[1][1 + j]
            direct = direct + weight * coefs[j][0]
            grad_coef = [weight * on_hidden, weight * jnp.sum(grad_top * vector[j], axis=1, keepdims=True)]
            mean_coef = coefs[j][0] * grad_coef[0] + coefs[j][1] * grad_coef[1]
            for n in range(2):
                grad_logits = grad_logits + jnp.where(
                    lane == 8.0 + 2 * j + n, coefs[j][n] * (grad_coef[n] - mean_coef), 0.0
                )
            on_vectors = on_vectors + jnp.where(lane == 14.0 + j, weight * coefs[j][1], 0.0)
        logit_parts = split_low(grad_logits)
        vector_parts = split_low(on_vectors)
        grad_hidden = direct * grad_top + mm(spread[0] + spread[1], back_rows)
        grad_hidden = grad_hidden + mm(logit_parts[0], router_low) + mm(logit_parts[1], router_low)
        small_sum = mm_tn(logit_parts[0], low) + mm_tn(logit_parts[1], low)
        small_sum = small_sum + mm_tn(vector_parts[0], grad_low) + mm_tn(vector_parts[1], grad_low)
        scale = lax.rsqrt(jnp.mean(middle * middle, axis=1, keepdims=True) + NORM_EPSILON)
        normal = middle * scale
        gain_sum = jnp.sum(grad_hidden * normal, axis=0, keepdims=True)
        facts[...] += small_sum[0:16] + jnp.where(router_row == 13, gain_sum, 0.0)
        inner_term = grad_hidden * smalls[13:14]
        gtokens[rows, :] = grad_top + scale * (
            inner_term - normal * jnp.mean(inner_term * normal, axis=1, keepdims=True)
        )

    def backward(pk, kt, grad, dq, dv, dk_sum, dv_sum, delta, gr, wall, ap):
        grad_att = mm_nt(gtokens[...].astype(BF), wo[...])
        for part in range(4):
            wide = grad_att[:, 192 * part:192 * (part + 1)]
            pk[part, 0:TOK, :] = wide[:, :128].astype(BF)
            third = wide[:, 128:]
            pk[part, TOK:ATT, :] = jnp.concatenate([third[:HALF], third[HALF:]], axis=1).astype(BF)
        got[q] = pk[q]

        def att_copy(k, to, frm, device):
            return remote(pk.at[to], got.at[frm], ss.at[S["att2"] + k], rs.at[R["att2"] + k], device)

        for k, (other, device) in enumerate(others):
            att_copy(k, other, q, device).start()

        wo_copy(1, q, me.at(x=nx)).wait_send()
        wo_copy(0, q, me.at(c=nc)).wait_send()
        wo_copy(2, 2 * nx + c, me.at(c=nc)).wait_send()

        @pl.loop(0, 2)
        def _(i):
            wide = pl.ds(pl.multiple_of(i * 384, 384), 384)
            grad_wo = mm_tn(attended[:, wide], gtokens[...].astype(BF)).astype(BF)
            for s in range(4):
                for t in range(6):
                    tile = grad_wo[96 * s:96 * (s + 1), 128 * t:128 * (t + 1)]
                    wo_all[4 * i + s, 96 * t:96 * (t + 1), :] = tile

        def wo_rows(part):
            return pl.ds(pl.multiple_of(part * O_ROWS, O_ROWS), O_ROWS)

        def wo_share(k, to, device):
            return remote(
                wo_all.at[:, wo_rows(to), :], wo_in.at[k], ss.at[S["wo2"] + k], rs.at[R["wo2"] + k], device
            )

        for s in range(OUTER):
            for t in range(5):
                wall[96 * s:96 * (s + 1), 128 * t:128 * (t + 1)] = packs[s, 96 * t:96 * (t + 1), :]

        for k, (other, device) in enumerate(others):
            att_copy(k, q, other, device).wait_recv()
        for k, (other, device) in enumerate(others):
            wo_share(k, other, device).start()
        for part in range(4):
            rows = slice(part * TOK, (part + 1) * TOK)
            both = got[part, 0:TOK, :]
            third = got[part, TOK:ATT, :]
            grad[0, rows, :] = both[:, :64]
            grad[1, rows, :] = both[:, 64:]
            grad[2, rows, :] = jnp.concatenate([third[:, :64], third[:, 64:]], axis=0)
        for h in range(LOCAL_HEADS):
            dots = jnp.sum(grad[h].astype(F32) * vo[h, :, 64:128].astype(F32), axis=1, keepdims=True)
            delta[h] = jnp.transpose(jnp.broadcast_to(dots, (STREAM, 128)))[0:8, :]

        def one_head(h):
            ks[...] = qk[h, :, 64:128]
            kt[...] = jnp.transpose(ks[...].astype(F32)).astype(BF)
            dk_sum[...] = jnp.zeros((STREAM, 64), F32)
            dv_sum[...] = jnp.zeros((STREAM, 64), F32)
            for b in range(STREAM // BLOCK):
                first, last = b * BLOCK, (b + 1) * BLOCK
                q_rows, g_rows = qk[h, first:last, 0:64], grad[h, first:last, :]
                grad_q = jnp.zeros((64, BLOCK), F32)
                for start in range(0, last, KEYS):
                    keys = slice(start, min(start + KEYS, last))
                    size = keys.stop - start
                    scores = mm_nt(ks[keys, :], q_rows)
                    key = lax.broadcasted_iota(jnp.int32, (size, BLOCK), 0) + start
                    col = lax.broadcasted_iota(jnp.int32, (size, BLOCK), 1) + first
                    seen = (key >= begin[0:1, first:last]) & (key <= col)
                    probs = jnp.exp(jnp.where(seen, scores, NEGATIVE) - lse[h, 0:1, first:last])
                    grad_probs = mm_nt(vo[h, keys, 0:64], g_rows)
                    grad_scores = (probs * (grad_probs - delta[h, 0:1, first:last])).astype(BF)
                    dv_sum[keys, :] += mm(probs.astype(BF), g_rows)
                    dk_sum[keys, :] += mm(grad_scores, q_rows)
                    grad_q = grad_q + mm(kt[:, keys], grad_scores)
                dq[first:last, :] = (jnp.transpose(grad_q) * 0.125).astype(BF)
            dv[h] = dv_sum[...].astype(BF)
            for part in range(4):
                rows = slice(part * TOK, (part + 1) * TOK)
                turned = jnp.concatenate([dq[rows, :], dk_sum[rows, :].astype(BF)], axis=1)
                raw = turned.astype(F32) * cos[rows, :] - mm(turned, turn[...]) * sin[rows, :]
                gr[rows, pl.ds(pl.multiple_of(h * 128, 128), 128)] = raw.astype(BF)

        line_step(1, 0)
        pl.loop(0, LOCAL_HEADS)(one_head)
        line_step(1, 1)
        for part in range(4):
            rows = slice(part * TOK, (part + 1) * TOK)
            gr[rows, 384:512] = jnp.concatenate([dv[0, rows, :], dv[1, rows, :]], axis=1)
            gr[rows, 512:640] = jnp.concatenate([dv[2, rows, :], jnp.zeros((TOK, 64), BF)], axis=1)

        @pl.loop(0, 2)
        def _(i):
            wide = pl.ds(pl.multiple_of(i * 384, 384), 384)
            grad_a = mm_tn(normed[:, wide], gr[...]).astype(BF)
            for s in range(4):
                for t in range(5):
                    ap[4 * i + s, 96 * t:96 * (t + 1), :] = grad_a[96 * s:96 * (s + 1), 128 * t:128 * (t + 1)]

        for k, (other, device) in enumerate(others):
            wo_share(k, q, device).wait_recv()
        wo_total = wo_all[:, wo_rows(q), :].astype(F32)
        for k in range(3):
            wo_total = wo_total + wo_in[k].astype(F32)
        ap[:, A_ROWS:A_ROWS + O_ROWS, :] = wo_total.astype(BF)

        for n in range(2):
            core_copy(n, 0, 4 * c, mine).wait_send()
            for k, (cx, cy) in enumerate(chips):
                core_copy(n, 1 + k, 4 * c, 2 * cx + cy).wait_send()
                back_copy(n, k, cx, cy).wait_send()
        gain_sum = jnp.zeros((1, D), F32)
        for part in range(4):
            rows = slice(part * TOK, (part + 1) * TOK)
            grad_n = mm_nt(gr[rows, :], wall[...])
            values = stream[part].astype(F32)
            scale = lax.rsqrt(jnp.mean(values * values, axis=1, keepdims=True) + NORM_EPSILON)
            gain_sum = gain_sum + jnp.sum(grad_n * (values * scale), axis=0, keepdims=True)
            first = 4 * (part % 2)
            (rowh, rowg)[part // 2][first:first + 4] = grad_n.astype(BF).reshape(4, CAP, D)

        def gn_swap(a):
            row = (rowh, rowg)[a]
            return remote(
                row.at[pl.ds(4 * nc, 4)], part_in.at[a], ss.at[S["gn"] + a], rs.at[R["gn"] + a], me.at(c=nc)
            )

        for a in range(2):
            gn_swap(a).start()
        small_all = facts[...] + jnp.where(router_row == 12, gain_sum, 0.0)
        for s in range(OUTER):
            piece = jnp.concatenate([small_all[:, 96 * s:96 * (s + 1)], jnp.zeros((16, 32), F32)], axis=1)
            ap[s, A_ROWS + O_ROWS:PACKG, :] = piece.astype(BF)

        def ay_copy(z):
            return remote(ap.at[2 * z + ny], ap_in.at[z], ss.at[S["ay"] + z], rs.at[R["ay"] + z], me.at(y=ny))

        for z in range(LINE):
            ay_copy(z).start()
        line_step(2, 0)
        for a in range(2):
            gn_swap(a).wait_recv()
            bufs[a] = ((rowh, rowg)[a][pl.ds(4 * c, 4)].astype(F32) + part_in[a].astype(F32)).astype(BF)
        gn_over = remote(bufs.at[nx], gn_ret, ss.at[S["gn"] + 2], rs.at[R["gn"] + 2], me.at(x=nx))
        gn_over.start()
        line_step(2, 1)
        for z in range(LINE):
            ay_copy(z).wait_recv()
            ap_in[z] = (ap[2 * z + y].astype(F32) + ap_in[z].astype(F32)).astype(BF)

        for k, (other, device) in enumerate(others):
            att_copy(k, other, q, device).wait_send()
            wo_share(k, other, device).wait_send()
        for a in range(2):
            gn_swap(a).wait_send()
        for z in range(LINE):
            ay_copy(z).wait_send()

    heads = (LOCAL_HEADS, STREAM, 64)
    pl.run_scoped(
        backward,
        pltpu.VMEM((4, ATT, 128), BF),
        pltpu.VMEM((64, STREAM), BF),
        pltpu.VMEM(heads, BF),
        pltpu.VMEM((STREAM, 64), BF),
        pltpu.VMEM(heads, BF),
        pltpu.VMEM((STREAM, 64), F32),
        pltpu.VMEM((STREAM, 64), F32),
        pltpu.VMEM((LOCAL_HEADS, 8, STREAM), F32),
        pltpu.VMEM((STREAM, 640), BF),
        pltpu.VMEM((D, 640), BF),
        pltpu.VMEM((OUTER, PACKG, 128), BF),
    )

    def al_copy(d, z, src, device):
        k = 4 * d + z
        return remote(src, ap_line.at[d, z], ss.at[S["al"] + k], rs.at[R["al"] + k], device)

    @pl.when(l == 0)
    def _():
        for z in (3, 2, 1):
            al_copy(0, z, ap_in.at[z], me.at(l=l + 1)).start()

    @pl.when(l == LINE - 1)
    def _():
        for z in (0, 1, 2):
            al_copy(1, z, ap_in.at[z], me.at(l=l - 1)).start()

    def al_step(t):
        for d in range(2):
            far = l if d == 0 else LINE - 1 - l
            z = 3 + l - t if d == 0 else t - 3 + l

            @pl.when((far >= 1) & (far <= t))
            def _():
                device = me.at(l=l + 1) if d == 0 else me.at(l=l - 1)
                al_copy(d, z, ap_line.at[d, z], me.at(y=ny)).wait_recv()
                if t < 3:
                    ap_line[d, z] = (ap_line[d, z].astype(F32) + ap_in[z].astype(F32)).astype(BF)
                    al_copy(d, z, ap_line.at[d, z], device).start()

    def gp_over(n, k, cx, cy):
        return remote(
            kinds[n][2].at[cy], kinds[n][3].at[2 * mine + c], ss.at[S["gp"] + 7 * n + k],
            rs.at[R["gp"] + 8 * n + 2 * mine + c], me.at(x=cx, y=cy)
        )

    def gp_wait(n, slot):
        ref = kinds[n][3]
        remote(ref.at[slot], ref.at[slot], ss.at[0], rs.at[R["gp"] + 8 * n + slot], me.at(c=nc)).wait_recv()

    def gp_own(n):
        return pltpu.make_async_copy(kinds[n][2].at[y], kinds[n][3].at[2 * mine + c], ls.at[10 + n])

    def gp_core(n, k, slot, src=None):
        ref = kinds[n][3]
        return remote(
            ref.at[slot] if src is None else src, ref.at[slot], ss.at[S["gp"] + 7 * n + 3 + k],
            rs.at[R["gp"] + 8 * n + slot], me.at(c=nc)
        )

    def line_end(yy):
        line_step(3, yy)
        for n in range(2):
            own_ref, ring, fin, _ = kinds[n]
            slot = 2 * l + yy

            @pl.loop(0, own_ref.shape[1] // 16)
            def _(r):
                part = pl.ds(pl.multiple_of(r * 16, 16), 16)
                up_sum = jnp.where(l >= 1, ring[slot, part, :].astype(F32), 0.0)
                dn_sum = jnp.where(l <= 2, fin[yy, part, :].astype(F32), 0.0)
                total = own_ref[slot, part, :].astype(F32) + up_sum + dn_sum
                fin[yy, part, :] = total.astype(BF)

            @pl.when(y == yy)
            def _():
                gp_over(n, 1, nx, y).start()
                gp_own(n).start()
                gp_core(n, 0, 2 * mine + c, fin.at[yy]).start()

            @pl.when(y != yy)
            def _():
                gp_over(n, 0, x, ny).start()
                gp_over(n, 2, nx, ny).start()

    al_step(1)

    gn_over = remote(bufs.at[nx], gn_ret, ss.at[S["gn"] + 2], rs.at[R["gn"] + 2], me.at(x=nx))
    gn_over.wait_recv()
    values = stream[q].astype(F32)
    scale = lax.rsqrt(jnp.mean(values * values, axis=1, keepdims=True) + NORM_EPSILON)
    normal = values * scale
    grad_n = (bufs[x].astype(F32) + gn_ret[...].astype(F32)).reshape(TOK, D)
    inner_term = grad_n * small_rows(packs)[12:13]
    gtokens[...] = gtokens[...] + scale * (
        inner_term - normal * jnp.mean(inner_term * normal, axis=1, keepdims=True)
    )

    line_end(0)
    al_step(2)
    line_end(1)
    al_step(3)

    @pl.when(l == 0)
    def _():
        ap_line[0, l] = jnp.zeros((PACKG, 128), BF)

    @pl.when(l == LINE - 1)
    def _():
        ap_line[1, l] = jnp.zeros((PACKG, 128), BF)

    own_sum = ap_in[l].astype(F32) + ap_line[0, l].astype(F32) + ap_line[1, l].astype(F32)
    apack[q] = own_sum.astype(BF)

    def aa_copy(k, part, device):
        return remote(apack.at[part], apack.at[part], ss.at[S["aa"] + k], rs.at[R["aa"] + k], device)

    for k, (other, device) in enumerate(others):
        aa_copy(k, q, device).start()

    for k, (cx, cy) in enumerate(chips):
        for n in range(2):
            slot = 2 * (2 * cx + cy) + c
            gp_wait(n, slot)
            gp_core(n, 1 + k, slot).start()
    for n in range(2):
        for slot in range(4):
            gp_wait(n, 2 * slot + nc)
    for k, (other, device) in enumerate(others):
        aa_copy(k, other, device).wait_recv()

    tok_copy(1, q, me.at(x=nx)).wait_send()
    tok_copy(0, q, me.at(c=nc)).wait_send()
    tok_copy(2, 2 * nx + c, me.at(c=nc)).wait_send()
    gn_over.wait_send()
    for k, (other, device) in enumerate(others):
        aa_copy(k, q, device).wait_send()
    for n in range(2):
        for k, (cx, cy) in enumerate(chips):
            gp_over(n, k, cx, cy).wait_send()
            gp_core(n, 1 + k, 2 * (2 * cx + cy) + c).wait_send()
        gp_core(n, 0, 2 * mine + c, kinds[n][2].at[y]).wait_send()
        gp_own(n).wait()
    for z in range(LINE):
        pack_copy(2, z, me.at(y=ny)).wait_send()

        @pl.when((l >= z) & (l < LINE - 1))
        def _():
            pack_copy(0, z, me.at(l=l + 1)).wait_send()

        @pl.when((l <= z) & (l > 0))
        def _():
            pack_copy(1, z, me.at(l=l - 1)).wait_send()
    for d in range(2):
        for z in range(LINE):
            sent = (z > l) & (l < LINE - 1) if d == 0 else (z < l) & (l > 0)

            @pl.when(sent)
            def _():
                device = me.at(l=l + 1) if d == 0 else me.at(l=l - 1)
                al_copy(d, z, ap_line.at[d, z], device).wait_send()
                for yy in range(2):
                    for n in range(2):
                        line_copy(d, z, yy, n, kinds[n][1].at[2 * z + yy], device, False).wait_send()


def layer_call(inner, *args):
    vm = pl.BlockSpec(memory_space=pltpu.VMEM)
    hbm = pl.BlockSpec(memory_space=pl.ANY)
    smem = pl.BlockSpec(memory_space=pltpu.SMEM)
    heads = (LOCAL_HEADS, STREAM, 64)
    wide = (LOCAL_HEADS, STREAM, 128)
    _, _, sends, recvs = semaphores()
    scratch = [
        ((4, TOK, D), BF), ((OUTER, PACK, 128), BF), ((OUTER, 576, 128), BF), ((D, D), BF),
        ((OUTER, 96, FF), BF), ((OUTER, 128, D), BF), ((2, 96, FF), BF), ((2, 128, D), BF),
        ((OUTER, 96, FF), BF), ((OUTER, 128, D), BF),
        ((8, CAP, D), BF), ((8, CAP, D), BF), ((2, 4, CAP, D), BF), ((2, 4, CAP, D), BF),
        ((4, ATT, 128), BF), ((3, OUTER, O_ROWS, 128), BF),
        ((LINE, PACKG, 128), BF), ((2, LINE, PACKG, 128), BF), ((4, CAP, D), BF),
        ((STREAM, D), BF), (wide, BF), (wide, BF), ((STREAM, 64), BF), ((LOCAL_HEADS, 8, STREAM), F32),
        ((TOK, D), BF), ((TOK, D), BF), ((STREAM, 128), F32), ((STREAM, 128), F32), ((TOK, D), BF),
        ((2, 4, CAP, D), BF), ((8, STREAM), jnp.int32), ((TOK, 128), F32), ((16, D), F32),
    ]
    return pl.pallas_call(
        functools.partial(layer_kernel, inner),
        out_shape=[
            jax.ShapeDtypeStruct((TOK, D), BF),
            jax.ShapeDtypeStruct((TOK, D), F32),
            jax.ShapeDtypeStruct((TOK, NEXP), F32),
            jax.ShapeDtypeStruct((4, PACKG, 128), BF),
            jax.ShapeDtypeStruct((8, 96, FF), BF),
            jax.ShapeDtypeStruct((8, 128, D), BF),
        ],
        in_specs=[hbm] * 8 + [vm, smem] + [vm] * 5,
        out_specs=[vm] * 4 + [hbm] * 2,
        scratch_shapes=[pltpu.VMEM(s, t) for s, t in scratch]
        + [
            pltpu.SemaphoreType.DMA((sends,)),
            pltpu.SemaphoreType.DMA((recvs,)),
            pltpu.SemaphoreType.DMA((12,)),
            pltpu.SemaphoreType.REGULAR((2,)),
        ],
        compiler_params=pltpu.CompilerParams(
            collective_id=0, has_side_effects=True, vmem_limit_bytes=VMEM_LIMIT
        ),
        name="layer",
    )(*args)


def adam(weight, grad, first, second, rate, decay):
    first_new = MOMENT_DECAY * first + (1.0 - MOMENT_DECAY) * grad
    second_new = MOMENT_DECAY * second + (1.0 - MOMENT_DECAY) * grad * grad
    correction = 1.0 - MOMENT_DECAY**STEP
    update = first_new / correction / (jnp.sqrt(second_new / correction) + ADAM_EPSILON)
    return weight - rate * (update + decay * weight), first_new, second_new


UP_PARTS = 2


def update_kernel(
    apack, gu, gd,
    in_w, in_m, in_v, out_w, out_m, out_v, rt_w, rt_m, rt_v, vec_w, vec_m, vec_v,
    up_w, up_m, up_v, dn_w, dn_m, dn_v,
    in_w2, in_m2, in_v2, out_w2, out_m2, out_v2, rt_w2, rt_m2, rt_v2, vec_w2, vec_m2, vec_v2,
    up_w2, up_m2, up_v2, dn_w2, dn_m2, dn_v2,
):
    step = pl.program_id(0)

    for j in range(16):
        cols, part = slice(256 * j, 256 * (j + 1)), slice(128 * j, 128 * (j + 1))
        grad = jnp.concatenate([gu[0, :, part], gu[1, :, part]], axis=1).astype(F32)
        new = adam(up_w[0, :, cols], grad, up_m[0, :, cols], up_v[0, :, cols], STEP_RATES[2], STEP_DECAYS[2])
        up_w2[0, :, cols], up_m2[0, :, cols], up_v2[0, :, cols] = new
    for half in range(2):
        rows = slice(128 * half, 128 * (half + 1))
        grad = gd[half].astype(F32)
        new = adam(dn_w[0, rows, :], grad, dn_m[0, rows, :], dn_v[0, rows, :], STEP_RATES[3], STEP_DECAYS[3])
        dn_w2[0, rows, :], dn_m2[0, rows, :], dn_v2[0, rows, :] = new

    @pl.when(step == 0)
    def _():
        tiles = [[apack[p, 96 * t:96 * (t + 1), :].astype(F32) for t in range(5)] for p in range(4)]
        for kind in range(3):
            pieces = []
            for p in range(4):
                if kind < 2:
                    pieces += [tiles[p][h][:, 64 * kind:64 * kind + 64] for h in range(LOCAL_HEADS)]
                else:
                    pieces += [tiles[p][3][:, :64], tiles[p][3][:, 64:], tiles[p][4][:, :64]]
            grad = jnp.concatenate(pieces, axis=1)
            new = adam(in_w[kind], grad, in_m[kind], in_v[kind], STEP_RATES[0], STEP_DECAYS[0])
            in_w2[kind], in_m2[kind], in_v2[kind] = new
        rows = jnp.concatenate([apack[p, A_ROWS:A_ROWS + O_ROWS, :] for p in range(4)], axis=0)
        for t in range(6):
            cols = slice(128 * t, 128 * (t + 1))
            grad = rows[96 * t:96 * (t + 1), :].astype(F32)
            new = adam(out_w[:, cols], grad, out_m[:, cols], out_v[:, cols], STEP_RATES[1], STEP_DECAYS[1])
            out_w2[:, cols], out_m2[:, cols], out_v2[:, cols] = new
        small = jnp.zeros((16, 128), F32)
        for p in range(4):
            small = small + apack[p, A_ROWS + O_ROWS:A_ROWS + O_ROWS + 16, :].astype(F32)
        new = adam(vec_w[...], small[12:, :96], vec_m[...], vec_v[...], STEP_RATES[5], STEP_DECAYS[5])
        vec_w2[...], vec_m2[...], vec_v2[...] = new
        new = adam(rt_w[...], small[:12, :96], rt_m[...], rt_v[...], STEP_RATES[4], STEP_DECAYS[4])
        rt_w2[...], rt_m2[...], rt_v2[...] = new


def update_call(apack, gu, gd, states):
    flat = [a for group in states for a in group]

    def whole(a):
        return pl.BlockSpec(a.shape, lambda e: (0,) * a.ndim)

    def by_expert(a):
        return pl.BlockSpec((1,) + a.shape[1:], lambda e: (e, 0, 0))

    specs = [whole(a) for a in flat[:12]] + [by_expert(a) for a in flat[12:]]
    pairs = [pl.BlockSpec((2,) + a.shape[1:], lambda e: (e, 0, 0)) for a in (gu, gd)]
    return pl.pallas_call(
        update_kernel,
        grid=(NFFN,),
        out_shape=[jax.ShapeDtypeStruct(a.shape, a.dtype) for a in flat],
        in_specs=[whole(apack)] + pairs + specs,
        out_specs=specs,
        compiler_params=pltpu.CompilerParams(vmem_limit_bytes=56 * 2**20),
        name="update",
    )(apack, gu, gd, *flat)


def gather_inner(values, axis, inner):
    if inner == 1:
        return values
    count = lax.axis_size("shard")
    groups = [[o * inner + i for i in range(inner)] for o in range(count // inner)]
    return lax.all_gather(values, "shard", axis=axis, tiled=True, axis_index_groups=groups)


def scatter_inner(values, axis, inner):
    count = lax.axis_size("shard")
    groups = [[o * inner + i for i in range(inner)] for o in range(count // inner)]
    return lax.psum_scatter(
        values, "shard", scatter_dimension=axis, axis_index_groups=groups, tiled=True
    )


def whole_gradients(apack, gup_all, gdn_all):
    tiles = apack[:, :A_ROWS].reshape(4, 5, 96, 128)
    heads = [
        tiles[:, 0:3, :, :64].transpose(2, 0, 1, 3),
        tiles[:, 0:3, :, 64:].transpose(2, 0, 1, 3),
        jnp.stack([tiles[:, 3, :, :64], tiles[:, 3, :, 64:], tiles[:, 4, :, :64]], axis=1).transpose(2, 0, 1, 3),
    ]
    g_in = jnp.stack([head.reshape(96, D) for head in heads])
    g_out = apack[:, A_ROWS:A_ROWS + O_ROWS].reshape(6, 96, 128).transpose(1, 0, 2).reshape(96, D)
    g_small = jnp.sum(apack[:, A_ROWS + O_ROWS:, :96].astype(F32), axis=0)
    g_up = gup_all.reshape(NFFN, 2, 96, 2, 8, 128).transpose(0, 2, 3, 4, 1, 5).reshape(NFFN, 96, 2 * FF)
    g_down = gdn_all.reshape(NFFN, 256, D)
    grads = (g_in, g_out, g_small[:12].T, g_small[12:], g_up, g_down)
    return [grad.astype(F32) for grad in grads]


def local(
    tokens, route_residual, doc_lengths, routes, priority, grad_out,
    attend_in, attend_in_first, attend_in_second,
    attend_out, attend_out_first, attend_out_second,
    expert_up, expert_up_first, expert_up_second,
    expert_down, expert_down_first, expert_down_second,
    router_mix, router_mix_first, router_mix_second,
    vectors, vectors_first, vectors_second,
):
    inner = lax.axis_size("shard") // OUTER
    cosine, sine, turn = rope_constants(STREAM)
    layer_out, grad_tokens, grad_route, apack, gup_all, gdn_all = layer_call(
        inner,
        tokens[0], grad_out[0],
        gather_inner(attend_in, 1, inner), gather_inner(attend_out, 0, inner),
        gather_inner(expert_up, 1, inner), gather_inner(expert_down, 1, inner),
        jnp.asarray(cosine), jnp.asarray(sine), jnp.asarray(turn, BF), doc_lengths,
        routes[0].T, route_residual[0].T, priority,
        gather_inner(router_mix, 0, inner).T, gather_inner(vectors, 1, inner),
    )
    states = (
        (attend_in, attend_in_first, attend_in_second),
        (attend_out, attend_out_first, attend_out_second),
        (router_mix, router_mix_first, router_mix_second),
        (vectors, vectors_first, vectors_second),
        (expert_up, expert_up_first, expert_up_second),
        (expert_down, expert_down_first, expert_down_second),
    )
    if inner == 1:
        turned = [a.T for a in states[2]]
        updated = update_call(apack, gup_all, gdn_all, (states[0], states[1], turned, *states[3:]))
        router = [a.T for a in updated[6:9]]
        results = (*updated[0:6], *updated[12:18], *router, *updated[9:12])
        return (layer_out[None], grad_tokens[None], grad_route[None], *results)

    grads = whole_gradients(apack, gup_all, gdn_all)
    axes = (1, 0, 0, 1, 1, 1)
    rates = [STEP_RATES[k] for k in (0, 1, 4, 5, 2, 3)]
    decays = [STEP_DECAYS[k] for k in (0, 1, 4, 5, 2, 3)]
    updated = [
        adam(weight, scatter_inner(grad, axis, inner), first, second, rate, decay)
        for (weight, first, second), grad, axis, rate, decay in zip(states, grads, axes, rates, decays)
    ]
    results = [a for k in (0, 1, 4, 5, 2, 3) for a in updated[k]]
    return (layer_out[None], grad_tokens[None], grad_route[None], *results)


def solution(mesh):
    token = P("shard", "seq", None)
    middle = P(None, "shard", None)
    front = P("shard", None)
    back = P(None, "shard")
    weights = (middle,) * 3 + (front,) * 3 + (middle,) * 6 + (front,) * 3 + (back,) * 3
    return jax.shard_map(
        local,
        mesh=mesh,
        in_specs=(token, token, front, token, P("shard", "seq"), token) + weights,
        out_specs=(token, token, token) + weights,
        check_vma=False,
    )
```

time: 2810 us -> 265 us (0.09)
  the two profiles are of different devices: /device:TPU:0 before, /device:TPU:9 now
where the time goes in v2:
time: 265 us
  Pallas kernels  261 us (98%)
  local copies, waits for them, and re-layouts  3.47 us (1%)
    pallas_call x1, Pallas kernels, layer_call(): pl.pallas_call(functools.partial(layer_kernel, inner), out_shape=[jax.Sha...  236 us
    pallas_call x1, Pallas kernels, update_call(): pl.pallas_call(update_kernel, grid=(NFFN,), out_shape=[jax.ShapeDtypeStru...  25.1 us

profile of v2, /device:TPU:9, one launch (start us, length us, event | category | flops | bytes accessed | tf_op | source)
XLA Modules:
  0.0 265.2 jit_solution(16999675914403720530)
XLA Ops:
  0.7 236.0 %layer.1 = (bf16[384,768]{1,0:T(8,128)(2,1)}, f32[384,768]{1,0:T(8,128)}, f32[384,8]{1,0:T(8,128)}, bf16[4,640,128]{2,1,0:T(8,128)(2,1)}, bf16[8,96,2048]{2,1,0:T(8,128)(2,1)}, /*index=5*/bf16[8,128,768]{2,1,0:T(8,128)(2,1)}) custom-call(bf16[384,768]{1,0:T(8,128)(2,1)} %bitcast.19, bf16[384,768]{1,0:T(8,128)(2,1)} %bitcast.20, f32[3,96,768]{2,1,0:T(8,128)} %in_w.1, ...), custom_call_target="tpu_custom_call" | custom-call | tf_op jit(solution)/shard_map/layer/pallas_call | solution.py:1113
  236.6 1.6 copy.48
  238.3 0.0 copy-start.1
  238.3 0.0 copy-start
  238.3 25.1 %update.1 = (f32[3,96,768]{2,1,0:T(8,128)}, f32[3,96,768]{2,1,0:T(8,128)}, f32[3,96,768]{2,1,0:T(8,128)}, f32[96,768]{1,0:T(8,128)}, f32[96,768]{1,0:T(8,128)}, ...) custom-call(bf16[4,640,128]{2,1,0:T(8,128)(2,1)} %get-tuple-element., ...), custom_call_target="tpu_custom_call" | custom-call | tf_op jit(solution)/shard_map/update/pallas_call | solution.py:1209
  263.4 0.0 copy-done.1
  263.4 0.8 copy.51
  264.2 0.0 copy-done
  264.2 1.0 copy.52
Async XLA Ops:
  238.3 25.1 %copy-start.1 = (bf16[384,768]{1,0:T(8,128)(2,1)S(1)}, bf16[384,768]{1,0:T(8,128)(2,1)}, u32[]{:S(2)}) copy-start(bf16[384,768]{1,0:T(8,128)(2,1)} %get-tuple-element.45) | copy-start | bytes 1769476
  238.3 26.0 %copy-start = (f32[384,768]{1,0:T(8,128)S(1)}, f32[384,768]{1,0:T(8,128)}, u32[]{:S(2)}) copy-start(f32[384,768]{1,0:T(8,128)} %get-tuple-element.46) | copy-start | bytes 3538948

commit v3 on v2

--- a/solution.py
+++ b/solution.py
@@ -68,24 +68,11 @@
         return (2 * x + c, (2 * l + y) * self.inner + self.rest)
 
 
-def greet(me, devices, line):
+def greet(devices):
     barrier = pltpu.get_barrier_semaphore()
     for device in devices:
         pl.semaphore_signal(barrier, inc=1, device_id=device, device_id_type=MESH)
-    if not line:
-        pl.semaphore_wait(barrier, len(devices))
-        return
-
-    @pl.when(me.l > 0)
-    def _():
-        pl.semaphore_signal(barrier, inc=1, device_id=me.at(l=me.l - 1), device_id_type=MESH)
-
-    @pl.when(me.l < LINE - 1)
-    def _():
-        pl.semaphore_signal(barrier, inc=1, device_id=me.at(l=me.l + 1), device_id_type=MESH)
-
-    near = jnp.minimum(me.l, 1) + jnp.minimum(LINE - 1 - me.l, 1)
-    pl.semaphore_wait(barrier, len(devices) + near)
+    pl.semaphore_wait(barrier, len(devices))
 
 
 def remote(src, dst, send, recv, device):
@@ -111,8 +98,9 @@
 A_ROWS = 5 * 96
 O_ROWS = 144
 S_ROWS = 96
-PACK = A_ROWS + O_ROWS + S_ROWS
+PACK = A_ROWS + S_ROWS
 PACKG = A_ROWS + O_ROWS + 16
+A_PARTS = (slice(0, 192), slice(192, A_ROWS + O_ROWS), slice(A_ROWS + O_ROWS, PACKG))
 TOK = 384
 STREAM = 1536
 ATT = 576
@@ -134,25 +122,20 @@
 
 def semaphores():
     s, r = Counter(), Counter()
-    send = {
-        "tok": s.take(3), "pack": s.take(12), "wo": s.take(3), "ex": s.take(34), "att": s.take(3),
-        "row": s.take(6), "core": s.take(8), "part": s.take(2), "back": s.take(6),
-        "line": s.take(32), "att2": s.take(3), "wo2": s.take(3), "ay": s.take(4), "al": s.take(8), "gn": s.take(3),
-        "aa": s.take(3), "gp": s.take(14),
+    counts = {
+        "tok": (3, 3), "pack": (7, 8), "wo8": (7, 8), "wo": (3, 3), "ex": (8, 18), "over": (8, 0), "last": (2, 0),
+        "att": (6, 6), "row": (9, 12), "core": (12, 12), "part": (2, 2), "back": (6, 8), "pair": (8, 8), "line": (8, 10),
+        "att2": (3, 3), "wo2": (3, 3), "ay": (12, 12), "al": (9, 12), "gn": (3, 3), "aa": (9, 9), "gp": (12, 16),
     }
-    recv = {
-        "tok": r.take(3), "pack": r.take(8), "wo": r.take(3), "ex": r.take(16), "att": r.take(3),
-        "row": r.take(8), "core": r.take(8), "part": r.take(2), "back": r.take(8),
-        "line": r.take(32), "att2": r.take(3), "wo2": r.take(3), "ay": r.take(4), "al": r.take(8), "gn": r.take(3),
-        "aa": r.take(3), "gp": r.take(16),
-    }
+    send = {name: s.take(count[0]) for name, count in counts.items()}
+    recv = {name: r.take(count[1]) for name, count in counts.items()}
     return send, recv, s.used, r.used
 
 
 def small_rows(packs):
     tiles = []
     for t in range(6):
-        first = A_ROWS + O_ROWS + 16 * t
+        first = A_ROWS + 16 * t
         total = packs[0, first:first + 16, :].astype(F32)
         for s in range(1, OUTER):
             total = total + packs[s, first:first + 16, :].astype(F32)
@@ -171,14 +154,20 @@
     layer_out, gtokens, groute, apack, gup_all, gdn_all,
     stream, packs, wo_all, wo, wup, wdn, ringx_up, ringx_dn, gup, gdn, rowh, rowg, part_in, ret, got, wo_in,
     ap_in, ap_line, gn_ret, normed, qk, vo, ks, lse, attended, hidden, cos, sin, gout, bufs, begin,
-    cols, facts, ss, rs, ls, ready,
+    cols, facts, gate_out, gate_in, ss, rs, ls, ready,
 ):
     me = Place(inner)
     x, c, l, y, q, own = me.x, me.c, me.l, me.y, me.q, me.own
     nx, nc, ny = 1 - x, 1 - c, 1 - y
-    mine = 2 * x + y
+    side = lax.div(l, 2)
+    far = 1 - side
+    outer = (l == 0) | (l == LINE - 1)
+    inside = (l == 1) | (l == 2)
+    out, near, far_near, far_out = 3 * side, 1 + side, 2 - side, 3 - 3 * side
+    mate = 1 - l + 4 * side
+    mine = 2 * side + x
     S, R, _, _ = semaphores()
-    chips = [(x, ny), (nx, y), (nx, ny)]
+    chips = [(nx, side), (x, far), (nx, far)]
     others = [(2 * nx + c, me.at(x=nx)), (2 * nx + nc, me.at(x=nx, c=nc)), (2 * x + nc, me.at(c=nc))]
 
     def load(src, dst, k):
@@ -187,75 +176,105 @@
     def tok_copy(k, part, device):
         return remote(stream.at[part], stream.at[part], ss.at[S["tok"] + k], rs.at[R["tok"] + k], device)
 
-    def pack_copy(kind, z, device):
+    turns = [lax.rem(l + dl, LINE) for dl in range(LINE)]
+    shards = [me.at(l=turns[dl]) for dl in (1, 3, 2)] + [me.at(l=turns[dl], y=ny) for dl in (0, 1, 3, 2)]
+
+    def pack_copy(k, z, device):
         slot = 2 * z + y
-        return remote(
-            packs.at[slot], packs.at[slot], ss.at[S["pack"] + 4 * kind + z], rs.at[R["pack"] + slot], device
-        )
+        return remote(packs.at[slot], packs.at[slot], ss.at[S["pack"] + k], rs.at[R["pack"] + slot], device)
 
     def pack_wait(slot):
         remote(packs.at[slot], packs.at[slot], ss.at[0], rs.at[R["pack"] + slot], me.at(y=ny)).wait_recv()
 
-    def pack_up(z):
-        @pl.when(l < LINE - 1)
-        def _():
-            pack_copy(0, z, me.at(l=l + 1)).start()
-
-    def pack_down(z):
-        @pl.when(l > 0)
-        def _():
-            pack_copy(1, z, me.at(l=l - 1)).start()
-
     def pack_over(z):
-        pack_copy(2, z, me.at(y=ny)).start()
+        return pack_copy(3 + z, z, me.at(y=ny))
 
     def pack_step(step):
         @pl.when(l - step >= 0)
         def _():
             pack_wait(2 * (l - step) + y)
-            pack_up(l - step)
-            pack_over(l - step)
+            pack_over(l - step).start()
 
         @pl.when(l + step < LINE)
         def _():
             pack_wait(2 * (l + step) + y)
-            pack_down(l + step)
-            pack_over(l + step)
+            pack_over(l + step).start()
 
     weights = (wup, wdn)
 
-    def ex_copy(kind, n, z, yy, device):
-        slot = 2 * z + yy
-        k = 2 * (8 * kind + slot) + n
-        ref = weights[n]
-        return remote(ref.at[slot], ref.at[slot], ss.at[S["ex"] + k], rs.at[R["ex"] + 2 * slot + n], device)
-
-    def ex_wait(slot):
-        for n, ref in enumerate(weights):
-            remote(ref.at[slot], ref.at[slot], ss.at[0], rs.at[R["ex"] + 2 * slot + n], me.at(y=ny)).wait_recv()
-
-    def ex_forward(z, yy, upward, kinds=(0, 1)):
-        if upward:
-            @pl.when(l < LINE - 1)
-            def _():
-                for n in kinds:
-                    ex_copy(0, n, z, yy, me.at(l=l + 1)).start()
-        else:
-            @pl.when(l > 0)
-            def _():
-                for n in kinds:
-                    ex_copy(1, n, z, yy, me.at(l=l - 1)).start()
-
-    def relay(step, yy):
-        @pl.when(l - step >= 0)
+    def ex_ref(n, z, yy):
+        return weights[n].at[2 * z + yy]
+
+    def ex_send(n, k, src, dst, recv, device):
+        return remote(src, dst, ss.at[S["ex"] + 2 * k + n], rs.at[R["ex"] + recv], device)
+
+    def ex_recv(n, z, yy):
+        ref = ex_ref(n, z, yy)
+        remote(ref, ref, ss.at[0], rs.at[R["ex"] + 2 * (2 * z + yy) + n], me.at(y=ny)).wait_recv()
+
+    def ex_line(n, k, z, node, src=None):
+        ref = ex_ref(n, z, y)
+        return ex_send(n, k, ref if src is None else src, ref, 2 * (2 * z + y) + n, me.at(l=node))
+
+    def ex_through(n, src):
+        return ex_send(n, 0, src, ring_extra[n].at[0], 16 + n, me.at(l=near))
+
+    def ex_through_wait(n):
+        ref = ring_extra[n].at[0]
+        remote(ref, ref, ss.at[0], rs.at[R["ex"] + 16 + n], me.at(l=out)).wait_recv()
+
+    def ex_over(n, z):
+        ref = ex_ref(n, z, y)
+        return remote(ref, ref, ss.at[S["over"] + 2 * z + n], rs.at[R["ex"] + 2 * (2 * z + y) + n], me.at(y=ny))
+
+    def ex_first(n, other):
+        @pl.when(outer)
         def _():
-            ex_wait(2 * (l - step) + yy)
-            ex_forward(l - step, yy, True)
-
-        @pl.when(l + step < LINE)
+            ex_through(n, other).start()
+            ex_line(n, 1, l, near).start()
+
+        @pl.when(inside)
         def _():
-            ex_wait(2 * (l + step) + yy)
-            ex_forward(l + step, yy, False)
+            ex_line(n, 0, l, far_near, other).start()
+            ex_line(n, 1, l, out).start()
+
+        ex_over(n, l).start()
+
+    def relay(step):
+        for n in range(2):
+            if step == 1:
+                @pl.when(inside)
+                def _():
+                    ex_through_wait(n)
+                    ex_line(n, 2, out, far_near, ring_extra[n].at[0]).start()
+                    ex_recv(n, far_near, y)
+                    ex_line(n, 3, far_near, out).start()
+                    ex_over(n, far_near).start()
+
+                @pl.when(outer)
+                def _():
+                    ex_recv(n, near, y)
+                    ex_over(n, near).start()
+            elif step == 2:
+                @pl.when(inside)
+                def _():
+                    ex_recv(n, out, y)
+                    ex_over(n, out).start()
+
+                @pl.when(outer)
+                def _():
+                    ex_recv(n, far_near, y)
+                    ex_over(n, far_near).start()
+            else:
+                @pl.when(inside)
+                def _():
+                    ex_recv(n, far_out, y)
+                    ex_line_last(n).start()
+                    ex_over(n, far_out).start()
+
+    def ex_line_last(n):
+        ref = ex_ref(n, far_out, y)
+        return remote(ref, ref, ss.at[S["last"] + n], rs.at[R["ex"] + 2 * (2 * far_out + y) + n], me.at(l=out))
 
     def wo_copy(k, part, device):
         rows = pl.ds(pl.multiple_of(part * O_ROWS, O_ROWS), O_ROWS)
@@ -263,21 +282,24 @@
             wo_all.at[:, rows, :], wo_all.at[:, rows, :], ss.at[S["wo"] + k], rs.at[R["wo"] + k], device
         )
 
+    row_src = (bufs.at[0], bufs.at[1], gate_out)
+    row_dst = (rowh, rowg, gate_in)
+
     def row_copy(n, k, cx, cy):
-        row = (rowh, rowg)[n]
         return remote(
-            bufs.at[n, 2 * cx + cy], row.at[4 * c + mine], ss.at[S["row"] + 3 * n + k], rs.at[R["row"] + 4 * n + mine],
-            me.at(x=cx, y=cy)
+            row_src[n].at[2 * cy + cx], row_dst[n].at[4 * c + mine], ss.at[S["row"] + 3 * n + k],
+            rs.at[R["row"] + 4 * n + mine], me.at(x=cx, l=l + 2 * (cy - side))
         )
 
     def row_wait(n, cx, cy):
-        row, slot = (rowh, rowg)[n], 2 * cx + cy
+        row, slot = row_dst[n], 2 * cy + cx
         remote(
-            row.at[4 * c + slot], row.at[4 * c + slot], ss.at[0], rs.at[R["row"] + 4 * n + slot], me.at(x=cx, y=cy)
+            row.at[4 * c + slot], row.at[4 * c + slot], ss.at[0], rs.at[R["row"] + 4 * n + slot],
+            me.at(x=cx, l=l + 2 * (cy - side))
         ).wait_recv()
 
     def core_copy(n, k, first, slot):
-        row = (rowh, rowg)[n]
+        row = row_dst[n]
         return remote(
             row.at[first + slot], row.at[first + slot], ss.at[S["core"] + 4 * n + k], rs.at[R["core"] + 4 * n + slot],
             me.at(c=nc)
@@ -286,13 +308,13 @@
     def row_send(n):
         for k, (cx, cy) in enumerate(chips):
             row_copy(n, k, cx, cy).start()
-        (rowh, rowg)[n][4 * c + mine] = bufs[n, mine]
+        row_dst[n][4 * c + mine] = row_src[n][mine]
         core_copy(n, 0, 4 * c, mine).start()
 
     def row_pass(n):
         for k, (cx, cy) in enumerate(chips):
             row_wait(n, cx, cy)
-            core_copy(n, 1 + k, 4 * c, 2 * cx + cy).start()
+            core_copy(n, 1 + k, 4 * c, 2 * cy + cx).start()
 
     def row_collect(n):
         for slot in range(4):
@@ -300,14 +322,14 @@
 
     def back_copy(n, k, cx, cy):
         return remote(
-            bufs.at[n, 2 * cx + cy], ret.at[n, mine], ss.at[S["back"] + 3 * n + k], rs.at[R["back"] + 4 * n + mine],
-            me.at(x=cx, y=cy)
+            bufs.at[n, 2 * cy + cx], ret.at[n, mine], ss.at[S["back"] + 3 * n + k], rs.at[R["back"] + 4 * n + mine],
+            me.at(x=cx, l=l + 2 * (cy - side))
         )
 
     def back_wait(n, cx, cy):
-        slot = 2 * cx + cy
+        slot = 2 * cy + cx
         remote(
-            ret.at[n, slot], ret.at[n, slot], ss.at[0], rs.at[R["back"] + 4 * n + slot], me.at(x=cx, y=cy)
+            ret.at[n, slot], ret.at[n, slot], ss.at[0], rs.at[R["back"] + 4 * n + slot], me.at(x=cx, l=l + 2 * (cy - side))
         ).wait_recv()
 
     loads = [
@@ -316,15 +338,18 @@
     for copy in loads:
         copy.start()
 
-    def forward(st_in, st_out, st_up, st_dn, upx, dnx, wo_tiles, wq, wr, pk, begin_col):
+    ring_extra = (ringx_up, ringx_dn)
+
+    def forward(st_in, st_out, st_up, st_dn, upx, dnx, wo_tiles, wo_mine, wq, wr, pk, begin_col, maps, slot_lanes):
         from_hbm = [load(w_in, st_in, 4), load(w_out, st_out, 5)]
-        experts = [2 * x + y, 2 * x + ny]
+        experts = [2 * side + x, 2 * far + x]
         from_hbm += [load(w_up.at[e], st_up.at[k], 6 + k) for k, e in enumerate(experts)]
         half_rows = pl.ds(pl.multiple_of(128 * c, 128), 128)
         from_hbm += [load(w_dn.at[e, half_rows, :], st_dn.at[k], 8 + k) for k, e in enumerate(experts)]
         for copy in from_hbm:
             copy.start()
-        greet(me, [me.at(c=nc), me.at(x=nx), me.at(x=nx, c=nc), me.at(y=ny), me.at(x=nx, y=ny)], True)
+        away = l + 2 * (far - side)
+        greet([me.at(c=nc), me.at(x=nx), me.at(x=nx, c=nc), me.at(x=nx, l=away)] + shards)
         loads[0].wait()
         tok_copy(1, q, me.at(x=nx)).start()
         tok_copy(0, q, me.at(c=nc)).start()
@@ -347,7 +372,8 @@
                     packs[own, 96 * t:96 * (t + 1), :] = jnp.concatenate(pair, axis=1).astype(BF)
 
         rows = pl.ds(pl.multiple_of(q * O_ROWS, O_ROWS), O_ROWS)
-        packs[own, A_ROWS:A_ROWS + O_ROWS, :] = wo_tiles[rows, :]
+        wo_mine[...] = wo_tiles[rows, :]
+        wo_all[own, rows, :] = wo_tiles[rows, :]
         small = jnp.concatenate([router[...], vectors[...]], axis=0)
         small = jnp.concatenate([small, jnp.zeros((16, 32), F32)], axis=1).astype(BF)
         to_col = lax.broadcasted_iota(jnp.int32, (128, D), 1) - 96 * own
@@ -355,17 +381,15 @@
         place = ((to_col == from_row) & (from_row < 96)).astype(F32).astype(BF)
         placed = mm(small, place).astype(BF)
         for t in range(6):
-            first = A_ROWS + O_ROWS + 16 * t
+            first = A_ROWS + 16 * t
             packs[own, first:first + 16, :] = placed[:, 128 * t:128 * (t + 1)]
-        pack_up(l)
-        pack_down(l)
-        pack_over(l)
+        for k in range(3):
+            pack_copy(k, l, shards[k]).start()
+        pack_over(l).start()
 
         for k in range(2):
             from_hbm[4 + k].wait()
         wdn[own] = st_dn[0].astype(BF)
-        ex_forward(l, y, True, (1,))
-        ex_forward(l, y, False, (1,))
         dnx[...] = st_dn[1].astype(BF)
         for k in range(2):
             from_hbm[2 + k].wait()
@@ -374,21 +398,43 @@
             wup[own, :, 128 * j:128 * (j + 1)] = st_up[0, :, part].astype(BF)
             upx[:, 128 * j:128 * (j + 1)] = st_up[1, :, part].astype(BF)
 
+        expert = jnp.concatenate([routes[k:k + 1, :] for k in range(TOPK)], axis=1).astype(F32)
+        order = jnp.concatenate([priority[...], priority[...] + STREAM], axis=1).astype(F32)
+        base = expert * 4096.0
+        rank_key = base + order
+        key_rows = jnp.transpose(jnp.broadcast_to(rank_key, (128, 2 * TOK)))[:, 0:1]
+        ahead = jnp.where((key_rows < rank_key) & (key_rows >= base), 1.0, 0.0)
+        rank = jnp.sum(ahead, axis=0, keepdims=True)
+        slot = jnp.where((expert < NFFN) & (rank < CAP), expert * CAP + rank, -1.0)
+        slots = [slot[:, :TOK], slot[:, TOK:]]
+        slot_row = lax.broadcasted_iota(jnp.int32, (NFFN * CAP, TOK), 0).astype(F32)
+        for k in range(TOPK):
+            slot_lanes[k:k + 1, :] = slots[k]
+            maps[k] = (slot_row == slots[k]).astype(F32).astype(BF)
+        loads[3].wait()
+        bufs[1] = mm(maps[0] + maps[1], gout[...]).astype(BF).reshape(NFFN, CAP, D)
+
         pack_step(1)
         pack_step(2)
         tok_copy(1, 2 * nx + c, me.at(x=nx)).wait_recv()
         tok_copy(2, 2 * nx + c, me.at(c=nc)).start()
         pack_step(3)
-        ex_forward(l, y, True, (0,))
-        ex_forward(l, y, False, (0,))
-
-        def ex_over(n):
+        def wo_send(k):
             return remote(
-                (upx, dnx)[n], weights[n].at[own], ss.at[S["ex"] + 32 + n], rs.at[R["ex"] + 2 * own + n], me.at(y=ny)
+                wo_mine, wo_all.at[own, rows, :], ss.at[S["wo8"] + k], rs.at[R["wo8"] + own], shards[k]
             )
 
-        for n in range(2):
-            ex_over(n).start()
+        def wo_arrive(k):
+            slot = 2 * turns[(1, 3, 2, 0, 1, 3, 2)[k]] + (y if k < 3 else ny)
+            remote(
+                wo_all.at[slot, rows, :], wo_all.at[slot, rows, :], ss.at[0], rs.at[R["wo8"] + slot], shards[k]
+            ).wait_recv()
+
+        for k in range(7):
+            wo_send(k).start()
+        for n, other in enumerate((upx, dnx)):
+            ex_first(n, other)
+        row_send(1)
 
         ids = lax.broadcasted_iota(jnp.int32, (8, STREAM), 1)
         first = lengths[0, 0] * 0
@@ -401,9 +447,6 @@
 
         for z in range(LINE):
             pack_wait(2 * z + ny)
-        wo_all[:, rows, :] = packs[:, A_ROWS:A_ROWS + O_ROWS, :]
-        wo_copy(1, q, me.at(x=nx)).start()
-        wo_copy(0, q, me.at(c=nc)).start()
         for s in range(OUTER):
             for t in range(5):
                 wq[t, 96 * s:96 * (s + 1), :] = packs[s, 96 * t:96 * (t + 1), :]
@@ -433,10 +476,6 @@
             vo[1, rows, 0:64] = both[:, 64:]
             vo[2, rows, 0:64] = mm(low, wq[4])[:, :64].astype(BF)
 
-        ex_wait(2 * l + ny)
-        ex_forward(l, ny, True)
-        ex_forward(l, ny, False)
-
         def one_head(h):
             ks[...] = qk[h, :, 64:128]
             for b in range(STREAM // BLOCK):
@@ -453,33 +492,47 @@
                 logs = jnp.broadcast_to(top + jnp.log(total), (BLOCK, 128))
                 lse[h, :, first:last] = jnp.transpose(logs)[0:8, :]
 
+        att_rows = (slice(0, TOK), slice(TOK, ATT))
+
+        def att_copy(k, piece, to, frm, device):
+            part = att_rows[piece]
+            return remote(
+                pk.at[to, part, :], got.at[frm, part, :], ss.at[S["att"] + 2 * k + piece],
+                rs.at[R["att"] + 2 * k + piece], device
+            )
+
         pl.loop(0, 1)(one_head)
+        for k in range(7):
+            wo_arrive(k)
+        wo_copy(1, q, me.at(x=nx)).start()
+        wo_copy(0, q, me.at(c=nc)).start()
+        relay(1)
+        pl.loop(1, 2)(one_head)
+        for part in range(4):
+            here = slice(part * TOK, (part + 1) * TOK)
+            pk[part, 0:TOK, :] = jnp.concatenate([vo[0, here, 64:128], vo[1, here, 64:128]], axis=1)
+        for k, (other, device) in enumerate(others):
+            att_copy(k, 0, other, q, device).start()
+        pl.loop(2, LOCAL_HEADS)(one_head)
         wo_copy(1, 2 * nx + c, me.at(x=nx)).wait_recv()
         wo_copy(2, 2 * nx + c, me.at(c=nc)).start()
-        relay(1, y)
-        pl.loop(1, LOCAL_HEADS)(one_head)
-
         for part in range(4):
-            rows = slice(part * TOK, (part + 1) * TOK)
-            pk[part, 0:TOK, :] = jnp.concatenate([vo[0, rows, 64:128], vo[1, rows, 64:128]], axis=1)
             third = [vo[2, part * TOK + k * HALF:part * TOK + (k + 1) * HALF, 64:128] for k in range(2)]
             pk[part, TOK:ATT, :] = jnp.concatenate(third, axis=1)
+        for k, (other, device) in enumerate(others):
+            att_copy(k, 1, other, q, device).start()
         got[q] = pk[q]
-
-        def att_copy(k, to, frm, device):
-            return remote(pk.at[to], got.at[frm], ss.at[S["att"] + k], rs.at[R["att"] + k], device)
-
-        for k, (other, device) in enumerate(others):
-            att_copy(k, other, q, device).start()
-        relay(1, ny)
+        relay(2)
 
         wo_copy(0, 2 * x + nc, me.at(c=nc)).wait_recv()
         wo_copy(2, 2 * nx + nc, me.at(c=nc)).wait_recv()
         for s in range(OUTER):
             for t in range(6):
                 wo[96 * s:96 * (s + 1), 128 * t:128 * (t + 1)] = wo_all[s, 96 * t:96 * (t + 1), :]
+        row_pass(1)
         for k, (other, device) in enumerate(others):
-            att_copy(k, q, other, device).wait_recv()
+            for piece in range(2):
+                att_copy(k, piece, q, other, device).wait_recv()
         pieces = []
         for part in range(4):
             low = got[part, TOK:ATT, :]
@@ -509,32 +562,35 @@
 
         gates = pair_softmax(*picked)
         coefs = pair_softmax(logits[8:9], logits[9:10]) + pair_softmax(logits[10:11], logits[11:12])
-        expert = jnp.concatenate(picks, axis=1).astype(F32)
-        order = jnp.concatenate([priority[...], priority[...] + STREAM], axis=1).astype(F32)
-        base = expert * 4096.0
-        rank_key = base + order
-        key_rows = jnp.transpose(jnp.broadcast_to(rank_key, (128, 2 * TOK)))[:, 0:1]
-        ahead = jnp.where((key_rows < rank_key) & (key_rows >= base), 1.0, 0.0)
-        rank = jnp.sum(ahead, axis=0, keepdims=True)
-        slot = jnp.where((expert < NFFN) & (rank < CAP), expert * CAP + rank, -1.0)
-        slots = [slot[:, :TOK], slot[:, TOK:]]
+        slots = [slot_lanes[k:k + 1, :] for k in range(TOPK)]
         lanes = gates + coefs + slots + [pick.astype(F32) for pick in picks]
         lanes = jnp.concatenate(lanes + [jnp.zeros((128 - len(lanes), TOK), F32)], axis=0)
         cols[...] = jnp.transpose(lanes)
-        slot_row = lax.broadcasted_iota(jnp.int32, (NFFN * CAP, TOK), 0).astype(F32)
-        maps = [(slot_row == slots[k]).astype(F32).astype(BF) for k in range(TOPK)]
         bufs[0] = mm(maps[0] + maps[1], low).astype(BF).reshape(NFFN, CAP, D)
         row_send(0)
-        loads[3].wait()
-        grad_top = gout[...].astype(F32)
-        grad_rows = sum(mm(maps[k], (cols[:, k:k + 1] * grad_top).astype(BF)) for k in range(TOPK))
-        bufs[1] = grad_rows.astype(BF).reshape(NFFN, CAP, D)
-        row_send(1)
-
-        for n in range(2):
-            ex_over(n).wait_send()
+        slot_gate = jnp.zeros((NFFN * CAP, 1), F32)
+        for k in range(TOPK):
+            slot_gate = slot_gate + jnp.sum(maps[k].astype(F32) * gates[k], axis=1, keepdims=True)
+        high, rest = split_low(slot_gate)
+        lane = lax.broadcasted_iota(jnp.int32, (NFFN * CAP, 128), 1)
+        packed = jnp.where(lane == 0, high.astype(F32), jnp.where(lane == 1, rest.astype(F32), 0.0))
+        gate_out[...] = packed.astype(BF).reshape(NFFN, CAP, 128)
+        row_send(2)
+
+        for n, other in enumerate((upx, dnx)):
+            @pl.when(outer)
+            def _():
+                ex_through(n, other).wait_send()
+
+            @pl.when(inside)
+            def _():
+                ex_line(n, 0, l, far_near, other).wait_send()
+
         for k, (other, device) in enumerate(others):
-            att_copy(k, other, q, device).wait_send()
+            for piece in range(2):
+                att_copy(k, piece, other, q, device).wait_send()
+        for k in range(7):
+            wo_send(k).wait_send()
 
     pl.run_scoped(
         forward,
@@ -545,90 +601,129 @@
         pltpu.VMEM((96, FF), BF),
         pltpu.VMEM((128, D), BF),
         pltpu.VMEM((576, 128), BF),
+        pltpu.VMEM((O_ROWS, 128), BF),
         pltpu.VMEM((5, D, 128), BF),
         pltpu.VMEM((3, D, 128), BF),
         pltpu.VMEM((4, ATT, 128), BF),
         pltpu.VMEM((STREAM, 128), F32),
+        pltpu.VMEM((TOPK, NFFN * CAP, TOK), BF),
+        pltpu.VMEM((8, TOK), F32),
     )
-    relay(2, y)
+    relay(3)
     row_pass(0)
-    relay(2, ny)
-    row_pass(1)
+    row_pass(2)
+    row_collect(1)
     row_collect(0)
-    row_collect(1)
-
-    def experts(rowt, down_sum, back_sum, part_out):
+
+    def experts(rowt, total, part_out, act, slope_gate, slope_lin):
         rowt[...] = jnp.transpose(rowh[...].reshape(8 * CAP, D).astype(F32)).astype(BF)
-        down_sum[...] = jnp.zeros_like(down_sum)
-        back_sum[...] = jnp.zeros_like(back_sum)
-        relay(3, y)
-        relay(3, ny)
-
-        @pl.loop(0, 4)
-        def _(j):
-            gate_cols = pl.ds(pl.multiple_of(j * 256, 256), 256)
-            lin_cols = pl.ds(pl.multiple_of(1024 + j * 256, 256), 256)
-            rows_h = rowh[...].reshape(8 * CAP, D)
-            rows_g = rowg[...].reshape(8 * CAP, D)
-            w_gate = wup[:, :, gate_cols].reshape(D, 256)
-            w_lin = wup[:, :, lin_cols].reshape(D, 256)
-            w_down = wdn[pl.ds(2 * j, 2)].reshape(256, D)
-            gate = mm(rows_h, w_gate)
-            lin = mm(rows_h, w_lin)
-            grad_act = mm_nt(rows_g, w_down)
-            sigma = jax.nn.sigmoid(gate)
-            silu = gate * sigma
-            low = (silu * lin).astype(BF)
-            down_sum[...] += mm(low, w_down)
-            grad_gate = (grad_act * lin * sigma * (1.0 + gate * (1.0 - sigma))).astype(BF)
-            grad_lin = (grad_act * silu).astype(BF)
-            back_sum[...] += mm_nt(grad_gate, w_gate) + mm_nt(grad_lin, w_lin)
-            gdn[pl.ds(2 * j, 2)] = mm_tn(low, rows_g).astype(BF).reshape(2, 128, D)
-            gup[:, :, gate_cols] = mm(rowt[...], grad_gate).astype(BF).reshape(8, 96, 256)
-            gup[:, :, lin_cols] = mm(rowt[...], grad_lin).astype(BF).reshape(8, 96, 256)
-
-        for z in range(LINE):
-            for yy in range(2):
-                for n in range(2):
-
-                    @pl.when((l >= z) & (l < LINE - 1))
-                    def _():
-                        ex_copy(0, n, z, yy, me.at(l=l + 1)).wait_send()
-
-                    @pl.when((l <= z) & (l > 0))
-                    def _():
-                        ex_copy(1, n, z, yy, me.at(l=l - 1)).wait_send()
-
-        @pl.when(l < LINE - 1)
-        def _():
-            pl.semaphore_signal(ready.at[0], inc=1, device_id=me.at(l=l + 1), device_id_type=MESH)
-
-        @pl.when(l > 0)
-        def _():
-            pl.semaphore_signal(ready.at[1], inc=1, device_id=me.at(l=l - 1), device_id_type=MESH)
-
+        total[...] = jnp.zeros_like(total)
         for n in range(2):
-            for k, (cx, cy) in enumerate(chips):
-                row_copy(n, k, cx, cy).wait_send()
+            @pl.when(outer)
+            def _():
+                ex_recv(n, far_out, y)
+                ex_over(n, far_out).start()
+
+            for z in range(LINE):
+                ex_recv(n, z, ny)
 
         def swap(n):
             return remote(
                 part_out.at[n], part_in.at[n], ss.at[S["part"] + n], rs.at[R["part"] + n], me.at(c=nc)
             )
 
-        sums = (down_sum, back_sum)
         away = pl.ds(pl.multiple_of(nc * 4 * CAP, 4 * CAP), 4 * CAP)
         here = pl.ds(pl.multiple_of(c * 4 * CAP, 4 * CAP), 4 * CAP)
-        for n in range(2):
-            part_out[n] = sums[n][away, :].astype(BF).reshape(4, CAP, D)
+
+        def swap_start(n):
+            part_out[n] = total[away, :].astype(BF).reshape(4, CAP, D)
             swap(n).start()
-        for n in range(2):
+
+        def give_back(n):
             swap(n).wait_recv()
-            kept = sums[n][here, :].reshape(4, CAP, D)
-            bufs[n] = (kept + part_in[n].astype(F32)).astype(BF)
+            bufs[n] = (total[here, :].reshape(4, CAP, D) + part_in[n].astype(F32)).astype(BF)
             for k, (cx, cy) in enumerate(chips):
                 back_copy(n, k, cx, cy).start()
             ret[n, mine] = bufs[n, mine]
+
+        def columns(j):
+            gate_cols = pl.ds(pl.multiple_of(j * 256, 256), 256)
+            return gate_cols, pl.ds(pl.multiple_of(1024 + j * 256, 256), 256)
+
+        @pl.loop(0, 4)
+        def _(j):
+            gate_cols, lin_cols = columns(j)
+            rows_h = rowh[...].reshape(8 * CAP, D)
+            gate = mm(rows_h, wup[:, :, gate_cols].reshape(D, 256))
+            lin = mm(rows_h, wup[:, :, lin_cols].reshape(D, 256))
+            sigma = jax.nn.sigmoid(gate)
+            silu = gate * sigma
+            low = (silu * lin).astype(BF)
+            act[:, gate_cols] = low
+            slope_gate[:, gate_cols] = (lin * sigma * (1.0 + gate * (1.0 - sigma))).astype(BF)
+            slope_lin[:, gate_cols] = silu.astype(BF)
+            total[...] += mm(low, wdn[pl.ds(2 * j, 2)].reshape(256, D))
+
+        for n in range(3):
+            for k, (cx, cy) in enumerate(chips):
+                row_copy(n, k, cx, cy).wait_send()
+        swap_start(0)
+        row_collect(2)
+        for n in range(3):
+            core_copy(n, 0, 4 * c, mine).wait_send()
+            for k, (cx, cy) in enumerate(chips):
+                core_copy(n, 1 + k, 4 * c, 2 * cy + cx).wait_send()
+        for slot in range(8):
+            gate = gate_in[slot].astype(F32)
+            rowg[slot] = ((gate[:, 0:1] + gate[:, 1:2]) * rowg[slot].astype(F32)).astype(BF)
+        give_back(0)
+        total[...] = jnp.zeros_like(total)
+
+        @pl.loop(0, 4)
+        def _(j):
+            gate_cols, lin_cols = columns(j)
+            rows_g = rowg[...].reshape(8 * CAP, D)
+            grad_act = mm_nt(rows_g, wdn[pl.ds(2 * j, 2)].reshape(256, D))
+            grad_gate = (grad_act * slope_gate[:, gate_cols].astype(F32)).astype(BF)
+            grad_lin = (grad_act * slope_lin[:, gate_cols].astype(F32)).astype(BF)
+            total[...] += mm_nt(grad_gate, wup[:, :, gate_cols].reshape(D, 256))
+            total[...] += mm_nt(grad_lin, wup[:, :, lin_cols].reshape(D, 256))
+            gdn[pl.ds(2 * j, 2)] = mm_tn(act[:, gate_cols], rows_g).astype(BF).reshape(2, 128, D)
+            gup[:, :, gate_cols] = mm(rowt[...], grad_gate).astype(BF).reshape(8, 96, 256)
+            gup[:, :, lin_cols] = mm(rowt[...], grad_lin).astype(BF).reshape(8, 96, 256)
+
+        swap_start(1)
+        for n in range(2):
+            @pl.when(outer)
+            def _():
+                ex_line(n, 1, l, near).wait_send()
+
+            @pl.when(inside)
+            def _():
+                ex_line(n, 1, l, out).wait_send()
+                ex_line(n, 2, out, far_near, ring_extra[n].at[0]).wait_send()
+                ex_line(n, 3, far_near, out).wait_send()
+                ex_line_last(n).wait_send()
+
+            for z in range(LINE):
+                ex_over(n, z).wait_send()
+
+        @pl.when(l < LINE - 1)
+        def _():
+            pl.semaphore_signal(ready.at[0], inc=1, device_id=me.at(l=l + 1), device_id_type=MESH)
+
+        @pl.when(l > 0)
+        def _():
+            pl.semaphore_signal(ready.at[1], inc=1, device_id=me.at(l=l - 1), device_id_type=MESH)
+
+        pl.semaphore_signal(ready.at[2], inc=1, device_id=me.at(y=ny), device_id_type=MESH)
+
+        @pl.when(outer)
+        def _():
+            pl.semaphore_signal(ready.at[3], inc=1, device_id=me.at(l=far_near), device_id_type=MESH)
+
+
+        give_back(1)
         for n in range(2):
             swap(n).wait_send()
 
@@ -636,22 +731,66 @@
         experts,
         pltpu.VMEM((D, 8 * CAP), BF),
         pltpu.VMEM((8 * CAP, D), F32),
-        pltpu.VMEM((8 * CAP, D), F32),
         pltpu.VMEM((2, 4, CAP, D), BF),
+        pltpu.VMEM((8 * CAP, 1024), BF),
+        pltpu.VMEM((8 * CAP, 1024), BF),
+        pltpu.VMEM((8 * CAP, 1024), BF),
     )
 
-    kinds = ((gup, wup, ringx_up, gup_all), (gdn, wdn, ringx_dn, gdn_all))
-
-    def line_copy(d, z, yy, n, src, device, last):
-        k = ((d * 4 + z) * 2 + yy) * 2 + n
-        dst = kinds[n][2].at[yy] if last and d == 1 else kinds[n][1].at[2 * z + yy]
-        return remote(src, dst, ss.at[S["line"] + k], rs.at[R["line"] + k], device)
-
-    def first_sends(d, order, device):
-        for z in order:
-            for yy in range(2):
-                for n in range(2):
-                    line_copy(d, z, yy, n, kinds[n][0].at[2 * z + yy], device, z == order[2]).start()
+    grads = (gup, gdn)
+
+    def room(n, i):
+        return weights[n].at[i] if isinstance(i, jax.Array) or i < 8 else ring_extra[n].at[0]
+
+    pieces = [far_out, far_near, mate, l]
+
+    def pair_copy(n, j):
+        z = pieces[j]
+        return remote(
+            grads[n].at[2 * z + ny], weights[n].at[z], ss.at[S["pair"] + 2 * j + n], rs.at[R["pair"] + 2 * j + n],
+            me.at(y=ny)
+        )
+
+    def line_copy(n, k, src, to, node):
+        return remote(
+            src, room(n, to), ss.at[S["line"] + 2 * k + n], rs.at[R["line"] + 2 * (to - 4) + n], me.at(l=node)
+        )
+
+    def line_wait(n, to):
+        remote(room(n, to), room(n, to), ss.at[0], rs.at[R["line"] + 2 * (to - 4) + n], me.at(y=ny)).wait_recv()
+
+    def add(n, into, other):
+        rows = grads[n].shape[1]
+
+        @pl.loop(0, rows // 16)
+        def _(r):
+            part = pl.ds(pl.multiple_of(r * 16, 16), 16)
+            into[part, :] = (into[part, :].astype(F32) + other[part, :].astype(F32)).astype(BF)
+
+    def pair_end(n, j):
+        pair_copy(n, j).wait_recv()
+        add(n, weights[n].at[pieces[j]], grads[n].at[2 * pieces[j] + y])
+
+    def line_step(j):
+        for n in range(2):
+            pair_end(n, j)
+            if j == 2:
+                line_copy(n, 2, weights[n].at[mate], 8, mate).start()
+                continue
+
+            @pl.when(outer)
+            def _():
+                line_copy(n, j, weights[n].at[pieces[j]], 4 + j, near).start()
+
+    def line_cross(j):
+        for n in range(2):
+            @pl.when(inside)
+            def _():
+                if j == 0 and n == 0:
+                    pl.semaphore_wait(ready.at[3], 1)
+                line_wait(n, 4 + j)
+                add(n, weights[n].at[4 + j], weights[n].at[pieces[j]])
+                line_copy(n, j, weights[n].at[4 + j], 7, (far_out, far_near)[j]).start()
 
     @pl.when(l < LINE - 1)
     def _():
@@ -661,38 +800,13 @@
     def _():
         pl.semaphore_wait(ready.at[0], 1)
 
-    @pl.when(l == 0)
-    def _():
-        first_sends(0, (3, 2, 1), me.at(l=l + 1))
-
-    @pl.when(l == LINE - 1)
-    def _():
-        first_sends(1, (0, 1, 2), me.at(l=l - 1))
-
-    def add_own(n, slot):
-        own_ref, ring = kinds[n][0], kinds[n][1]
-
-        @pl.loop(0, own_ref.shape[1] // 16)
-        def _(r):
-            part = pl.ds(pl.multiple_of(r * 16, 16), 16)
-            total = own_ref[slot, part, :].astype(F32) + ring[slot, part, :].astype(F32)
-            ring[slot, part, :] = total.astype(BF)
-
-    def line_step(t, yy):
-        for d in range(2):
-            far = l if d == 0 else LINE - 1 - l
-            z = 3 + l - t if d == 0 else t - 3 + l
-
-            @pl.when((far >= 1) & (far <= t))
-            def _():
-                device = me.at(l=l + 1) if d == 0 else me.at(l=l - 1)
-                for n in range(2):
-                    slot = 2 * z + yy
-                    ring = kinds[n][1]
-                    line_copy(d, z, yy, n, ring.at[slot], me.at(y=ny), t == 3).wait_recv()
-                    if t < 3:
-                        add_own(n, slot)
-                        line_copy(d, z, yy, n, ring.at[slot], device, t == 2).start()
+    pl.semaphore_wait(ready.at[2], 1)
+    def pair_start(j):
+        for n in range(2):
+            pair_copy(n, j).start()
+
+    pair_start(0)
+    pair_start(1)
 
     for n in range(2):
         for cx, cy in chips:
@@ -763,7 +877,15 @@
             inner_term - normal * jnp.mean(inner_term * normal, axis=1, keepdims=True)
         )
 
+    def al_copy(p, k):
+        z, rows = turns[(1, 3, 2)[k]], A_PARTS[p]
+        return remote(
+            ap_in.at[z, rows, :], ap_line.at[l, rows, :], ss.at[S["al"] + 3 * p + k], rs.at[R["al"] + 4 * p + l], shards[k]
+        )
+
     def backward(pk, kt, grad, dq, dv, dk_sum, dv_sum, delta, gr, wall, ap):
+        line_step(0)
+        pair_start(2)
         grad_att = mm_nt(gtokens[...].astype(BF), wo[...])
         for part in range(4):
             wide = grad_att[:, 192 * part:192 * (part + 1)]
@@ -848,33 +970,60 @@
                 raw = turned.astype(F32) * cos[rows, :] - mm(turned, turn[...]) * sin[rows, :]
                 gr[rows, pl.ds(pl.multiple_of(h * 128, 128), 128)] = raw.astype(BF)
 
-        line_step(1, 0)
-        pl.loop(0, LOCAL_HEADS)(one_head)
-        line_step(1, 1)
+        def grad_tiles(first, last):
+            @pl.loop(0, 2)
+            def _(i):
+                wide = pl.ds(pl.multiple_of(i * 384, 384), 384)
+                grad_a = mm_tn(normed[:, wide], gr[:, 128 * first:128 * last]).astype(BF)
+                for s in range(4):
+                    for t in range(first, last):
+                        tile = grad_a[96 * s:96 * (s + 1), 128 * (t - first):128 * (t - first + 1)]
+                        ap[4 * i + s, 96 * t:96 * (t + 1), :] = tile
+
+        def ay_copy(p, z):
+            rows = A_PARTS[p]
+            return remote(
+                ap.at[2 * z + ny, rows, :], ap_in.at[z, rows, :], ss.at[S["ay"] + 4 * p + z],
+                rs.at[R["ay"] + 4 * p + z], me.at(y=ny)
+            )
+
+        def ay_start(p):
+            for z in range(LINE):
+                ay_copy(p, z).start()
+
+        def ay_end(p):
+            rows = A_PARTS[p]
+            for z in range(LINE):
+                ay_copy(p, z).wait_recv()
+                ap_in[z, rows, :] = (ap[2 * z + y, rows, :].astype(F32) + ap_in[z, rows, :].astype(F32)).astype(BF)
+            for k in range(3):
+                al_copy(p, k).start()
+
+        pl.loop(0, 1)(one_head)
+        line_step(1)
+        line_cross(0)
+        pl.loop(1, 2)(one_head)
+        grad_tiles(0, 2)
+        ay_start(0)
+        pair_start(3)
+        pl.loop(2, LOCAL_HEADS)(one_head)
+        line_cross(1)
         for part in range(4):
             rows = slice(part * TOK, (part + 1) * TOK)
             gr[rows, 384:512] = jnp.concatenate([dv[0, rows, :], dv[1, rows, :]], axis=1)
             gr[rows, 512:640] = jnp.concatenate([dv[2, rows, :], jnp.zeros((TOK, 64), BF)], axis=1)
 
-        @pl.loop(0, 2)
-        def _(i):
-            wide = pl.ds(pl.multiple_of(i * 384, 384), 384)
-            grad_a = mm_tn(normed[:, wide], gr[...]).astype(BF)
-            for s in range(4):
-                for t in range(5):
-                    ap[4 * i + s, 96 * t:96 * (t + 1), :] = grad_a[96 * s:96 * (s + 1), 128 * t:128 * (t + 1)]
-
+        grad_tiles(2, 5)
         for k, (other, device) in enumerate(others):
             wo_share(k, q, device).wait_recv()
         wo_total = wo_all[:, wo_rows(q), :].astype(F32)
         for k in range(3):
             wo_total = wo_total + wo_in[k].astype(F32)
         ap[:, A_ROWS:A_ROWS + O_ROWS, :] = wo_total.astype(BF)
+        ay_start(1)
 
         for n in range(2):
-            core_copy(n, 0, 4 * c, mine).wait_send()
             for k, (cx, cy) in enumerate(chips):
-                core_copy(n, 1 + k, 4 * c, 2 * cx + cy).wait_send()
                 back_copy(n, k, cx, cy).wait_send()
         gain_sum = jnp.zeros((1, D), F32)
         for part in range(4):
@@ -899,29 +1048,24 @@
             piece = jnp.concatenate([small_all[:, 96 * s:96 * (s + 1)], jnp.zeros((16, 32), F32)], axis=1)
             ap[s, A_ROWS + O_ROWS:PACKG, :] = piece.astype(BF)
 
-        def ay_copy(z):
-            return remote(ap.at[2 * z + ny], ap_in.at[z], ss.at[S["ay"] + z], rs.at[R["ay"] + z], me.at(y=ny))
-
-        for z in range(LINE):
-            ay_copy(z).start()
-        line_step(2, 0)
+        ay_start(2)
+        ay_end(0)
+        line_step(2)
         for a in range(2):
             gn_swap(a).wait_recv()
             bufs[a] = ((rowh, rowg)[a][pl.ds(4 * c, 4)].astype(F32) + part_in[a].astype(F32)).astype(BF)
         gn_over = remote(bufs.at[nx], gn_ret, ss.at[S["gn"] + 2], rs.at[R["gn"] + 2], me.at(x=nx))
         gn_over.start()
-        line_step(2, 1)
-        for z in range(LINE):
-            ay_copy(z).wait_recv()
-            ap_in[z] = (ap[2 * z + y].astype(F32) + ap_in[z].astype(F32)).astype(BF)
-
+        ay_end(1)
+        ay_end(2)
         for k, (other, device) in enumerate(others):
             att_copy(k, other, q, device).wait_send()
             wo_share(k, other, device).wait_send()
         for a in range(2):
             gn_swap(a).wait_send()
-        for z in range(LINE):
-            ay_copy(z).wait_send()
+        for p in range(3):
+            for z in range(LINE):
+                ay_copy(p, z).wait_send()
 
     heads = (LOCAL_HEADS, STREAM, 64)
     pl.run_scoped(
@@ -939,79 +1083,75 @@
         pltpu.VMEM((OUTER, PACKG, 128), BF),
     )
 
-    def al_copy(d, z, src, device):
-        k = 4 * d + z
-        return remote(src, ap_line.at[d, z], ss.at[S["al"] + k], rs.at[R["al"] + k], device)
-
-    @pl.when(l == 0)
-    def _():
-        for z in (3, 2, 1):
-            al_copy(0, z, ap_in.at[z], me.at(l=l + 1)).start()
-
-    @pl.when(l == LINE - 1)
-    def _():
-        for z in (0, 1, 2):
-            al_copy(1, z, ap_in.at[z], me.at(l=l - 1)).start()
-
-    def al_step(t):
-        for d in range(2):
-            far = l if d == 0 else LINE - 1 - l
-            z = 3 + l - t if d == 0 else t - 3 + l
-
-            @pl.when((far >= 1) & (far <= t))
-            def _():
-                device = me.at(l=l + 1) if d == 0 else me.at(l=l - 1)
-                al_copy(d, z, ap_line.at[d, z], me.at(y=ny)).wait_recv()
-                if t < 3:
-                    ap_line[d, z] = (ap_line[d, z].astype(F32) + ap_in[z].astype(F32)).astype(BF)
-                    al_copy(d, z, ap_line.at[d, z], device).start()
-
-    def gp_over(n, k, cx, cy):
+    def aa_copy(p, k, part, device):
+        rows = A_PARTS[p]
         return remote(
-            kinds[n][2].at[cy], kinds[n][3].at[2 * mine + c], ss.at[S["gp"] + 7 * n + k],
-            rs.at[R["gp"] + 8 * n + 2 * mine + c], me.at(x=cx, y=cy)
+            apack.at[part, rows, :], apack.at[part, rows, :], ss.at[S["aa"] + 3 * p + k], rs.at[R["aa"] + 3 * p + k], device
         )
 
+    def al_end(p):
+        rows = A_PARTS[p]
+        total = ap_in[l, rows, :].astype(F32)
+        for k in range(3):
+            z = turns[(1, 3, 2)[k]]
+            ref = ap_line.at[z, rows, :]
+            remote(ref, ref, ss.at[0], rs.at[R["al"] + 4 * p + z], shards[k]).wait_recv()
+            total = total + ap_line[z, rows, :].astype(F32)
+        apack[q, rows, :] = total.astype(BF)
+        for k, (other, device) in enumerate(others):
+            aa_copy(p, k, q, device).start()
+
+    spread_out = (gup_all, gdn_all)
+
+    def gp_slot(k, cx, cc):
+        return 2 * (2 * (side if k == 0 else far) + cx) + cc
+
+    def gp_src(n, k):
+        return ring_extra[n].at[0] if k == 0 else weights[n].at[7]
+
+    def gp_over(n, k):
+        slot = gp_slot(k, x, c)
+        return remote(
+            gp_src(n, k), spread_out[n].at[slot], ss.at[S["gp"] + 6 * n + k], rs.at[R["gp"] + 8 * n + slot], me.at(x=nx)
+        )
+
     def gp_wait(n, slot):
-        ref = kinds[n][3]
-        remote(ref.at[slot], ref.at[slot], ss.at[0], rs.at[R["gp"] + 8 * n + slot], me.at(c=nc)).wait_recv()
-
-    def gp_own(n):
-        return pltpu.make_async_copy(kinds[n][2].at[y], kinds[n][3].at[2 * mine + c], ls.at[10 + n])
-
-    def gp_core(n, k, slot, src=None):
-        ref = kinds[n][3]
+        ref = spread_out[n].at[slot]
+        remote(ref, ref, ss.at[0], rs.at[R["gp"] + 8 * n + slot], me.at(c=nc)).wait_recv()
+
+    def gp_own(n, k):
+        return pltpu.make_async_copy(gp_src(n, k), spread_out[n].at[gp_slot(k, x, c)], ls.at[10 + 2 * n + k])
+
+    def gp_core(n, k):
+        slot = gp_slot(k, x, c)
         return remote(
-            ref.at[slot] if src is None else src, ref.at[slot], ss.at[S["gp"] + 7 * n + 3 + k],
-            rs.at[R["gp"] + 8 * n + slot], me.at(c=nc)
+            gp_src(n, k), spread_out[n].at[slot], ss.at[S["gp"] + 6 * n + 2 + k], rs.at[R["gp"] + 8 * n + slot],
+            me.at(c=nc)
         )
 
-    def line_end(yy):
-        line_step(3, yy)
+    def gp_pass(n, k):
+        slot = gp_slot(k, nx, c)
+        ref = spread_out[n].at[slot]
+        return remote(ref, ref, ss.at[S["gp"] + 6 * n + 4 + k], rs.at[R["gp"] + 8 * n + slot], me.at(c=nc))
+
+    def gp_start(n, k):
+        gp_over(n, k).start()
+        gp_own(n, k).start()
+        gp_core(n, k).start()
+
+    def line_other():
         for n in range(2):
-            own_ref, ring, fin, _ = kinds[n]
-            slot = 2 * l + yy
-
-            @pl.loop(0, own_ref.shape[1] // 16)
-            def _(r):
-                part = pl.ds(pl.multiple_of(r * 16, 16), 16)
-                up_sum = jnp.where(l >= 1, ring[slot, part, :].astype(F32), 0.0)
-                dn_sum = jnp.where(l <= 2, fin[yy, part, :].astype(F32), 0.0)
-                total = own_ref[slot, part, :].astype(F32) + up_sum + dn_sum
-                fin[yy, part, :] = total.astype(BF)
-
-            @pl.when(y == yy)
-            def _():
-                gp_over(n, 1, nx, y).start()
-                gp_own(n).start()
-                gp_core(n, 0, 2 * mine + c, fin.at[yy]).start()
-
-            @pl.when(y != yy)
-            def _():
-                gp_over(n, 0, x, ny).start()
-                gp_over(n, 2, nx, ny).start()
-
-    al_step(1)
+            line_wait(n, 7)
+            gp_start(n, 1)
+
+    def line_own():
+        for n in range(2):
+            pair_end(n, 3)
+            line_wait(n, 8)
+            add(n, ring_extra[n].at[0], weights[n].at[l])
+            gp_start(n, 0)
+
+    al_end(0)
 
     gn_over = remote(bufs.at[nx], gn_ret, ss.at[S["gn"] + 2], rs.at[R["gn"] + 2], me.at(x=nx))
     gn_over.wait_recv()
@@ -1024,72 +1164,55 @@
         inner_term - normal * jnp.mean(inner_term * normal, axis=1, keepdims=True)
     )
 
-    line_end(0)
-    al_step(2)
-    line_end(1)
-    al_step(3)
-
-    @pl.when(l == 0)
-    def _():
-        ap_line[0, l] = jnp.zeros((PACKG, 128), BF)
-
-    @pl.when(l == LINE - 1)
-    def _():
-        ap_line[1, l] = jnp.zeros((PACKG, 128), BF)
-
-    own_sum = ap_in[l].astype(F32) + ap_line[0, l].astype(F32) + ap_line[1, l].astype(F32)
-    apack[q] = own_sum.astype(BF)
-
-    def aa_copy(k, part, device):
-        return remote(apack.at[part], apack.at[part], ss.at[S["aa"] + k], rs.at[R["aa"] + k], device)
-
-    for k, (other, device) in enumerate(others):
-        aa_copy(k, q, device).start()
-
-    for k, (cx, cy) in enumerate(chips):
+    line_other()
+    al_end(1)
+    al_end(2)
+    line_own()
+
+    for k in (1, 0):
         for n in range(2):
-            slot = 2 * (2 * cx + cy) + c
-            gp_wait(n, slot)
-            gp_core(n, 1 + k, slot).start()
-    for n in range(2):
-        for slot in range(4):
-            gp_wait(n, 2 * slot + nc)
-    for k, (other, device) in enumerate(others):
-        aa_copy(k, other, device).wait_recv()
+            gp_wait(n, gp_slot(k, nx, c))
+            gp_pass(n, k).start()
+    for k in range(2):
+        for n in range(2):
+            gp_wait(n, gp_slot(k, x, nc))
+            gp_wait(n, gp_slot(k, nx, nc))
+    for p in range(3):
+        for k, (other, device) in enumerate(others):
+            aa_copy(p, k, other, device).wait_recv()
 
     tok_copy(1, q, me.at(x=nx)).wait_send()
     tok_copy(0, q, me.at(c=nc)).wait_send()
     tok_copy(2, 2 * nx + c, me.at(c=nc)).wait_send()
     gn_over.wait_send()
-    for k, (other, device) in enumerate(others):
-        aa_copy(k, q, device).wait_send()
+    for p in range(3):
+        for k, (other, device) in enumerate(others):
+            aa_copy(p, k, q, device).wait_send()
+            al_copy(p, k).wait_send()
     for n in range(2):
-        for k, (cx, cy) in enumerate(chips):
-            gp_over(n, k, cx, cy).wait_send()
-            gp_core(n, 1 + k, 2 * (2 * cx + cy) + c).wait_send()
-        gp_core(n, 0, 2 * mine + c, kinds[n][2].at[y]).wait_send()
-        gp_own(n).wait()
+        for k in range(2):
+            gp_over(n, k).wait_send()
+            gp_core(n, k).wait_send()
+            gp_pass(n, k).wait_send()
+            gp_own(n, k).wait()
+        for j in range(4):
+            pair_copy(n, j).wait_send()
+        line_copy(n, 2, weights[n].at[mate], 8, mate).wait_send()
+
+        @pl.when(outer)
+        def _():
+            for j in range(2):
+                line_copy(n, j, weights[n].at[pieces[j]], 4 + j, near).wait_send()
+
+        @pl.when(inside)
+        def _():
+            for j in range(2):
+                line_copy(n, j, weights[n].at[4 + j], 7, (far_out, far_near)[j]).wait_send()
+
+    for k in range(3):
+        pack_copy(k, l, shards[k]).wait_send()
     for z in range(LINE):
-        pack_copy(2, z, me.at(y=ny)).wait_send()
-
-        @pl.when((l >= z) & (l < LINE - 1))
-        def _():
-            pack_copy(0, z, me.at(l=l + 1)).wait_send()
-
-        @pl.when((l <= z) & (l > 0))
-        def _():
-            pack_copy(1, z, me.at(l=l - 1)).wait_send()
-    for d in range(2):
-        for z in range(LINE):
-            sent = (z > l) & (l < LINE - 1) if d == 0 else (z < l) & (l > 0)
-
-            @pl.when(sent)
-            def _():
-                device = me.at(l=l + 1) if d == 0 else me.at(l=l - 1)
-                al_copy(d, z, ap_line.at[d, z], device).wait_send()
-                for yy in range(2):
-                    for n in range(2):
-                        line_copy(d, z, yy, n, kinds[n][1].at[2 * z + yy], device, False).wait_send()
+        pack_over(z).wait_send()
 
 
 def layer_call(inner, *args):
@@ -1101,14 +1224,15 @@
     _, _, sends, recvs = semaphores()
     scratch = [
         ((4, TOK, D), BF), ((OUTER, PACK, 128), BF), ((OUTER, 576, 128), BF), ((D, D), BF),
-        ((OUTER, 96, FF), BF), ((OUTER, 128, D), BF), ((2, 96, FF), BF), ((2, 128, D), BF),
+        ((OUTER, 96, FF), BF), ((OUTER, 128, D), BF), ((1, 96, FF), BF), ((1, 128, D), BF),
         ((OUTER, 96, FF), BF), ((OUTER, 128, D), BF),
         ((8, CAP, D), BF), ((8, CAP, D), BF), ((2, 4, CAP, D), BF), ((2, 4, CAP, D), BF),
         ((4, ATT, 128), BF), ((3, OUTER, O_ROWS, 128), BF),
-        ((LINE, PACKG, 128), BF), ((2, LINE, PACKG, 128), BF), ((4, CAP, D), BF),
+        ((LINE, PACKG, 128), BF), ((LINE, PACKG, 128), BF), ((4, CAP, D), BF),
         ((STREAM, D), BF), (wide, BF), (wide, BF), ((STREAM, 64), BF), ((LOCAL_HEADS, 8, STREAM), F32),
         ((TOK, D), BF), ((TOK, D), BF), ((STREAM, 128), F32), ((STREAM, 128), F32), ((TOK, D), BF),
         ((2, 4, CAP, D), BF), ((8, STREAM), jnp.int32), ((TOK, 128), F32), ((16, D), F32),
+        ((4, CAP, 128), BF), ((8, CAP, 128), BF),
     ]
     return pl.pallas_call(
         functools.partial(layer_kernel, inner),
@@ -1126,8 +1250,8 @@
         + [
             pltpu.SemaphoreType.DMA((sends,)),
             pltpu.SemaphoreType.DMA((recvs,)),
-            pltpu.SemaphoreType.DMA((12,)),
-            pltpu.SemaphoreType.REGULAR((2,)),
+            pltpu.SemaphoreType.DMA((14,)),
+            pltpu.SemaphoreType.REGULAR((4,)),
         ],
         compiler_params=pltpu.CompilerParams(
             collective_id=0, has_side_effects=True, vmem_limit_bytes=VMEM_LIMIT

time: 265 us -> 257 us (0.970)
  the two profiles are of different devices: /device:TPU:9 before, /device:TPU:0 now
where the time goes in v3:
time: 257 us; the launch traced here: 254 us
  Pallas kernels  250 us (97%)
  local copies, waits for them, and re-layouts  3.47 us (1%)
    pallas_call x1, Pallas kernels, layer_call(): pl.pallas_call(functools.partial(layer_kernel, inner), out_shape=[jax.Sha...  225 us
    pallas_call x1, Pallas kernels, update_call(): pl.pallas_call(update_kernel, grid=(NFFN,), out_shape=[jax.ShapeDtypeStru...  24.9 us

profile of v3, /device:TPU:0, one launch (start us, length us, event | category | flops | bytes accessed | tf_op | source)
XLA Modules:
  0.0 254.1 jit_solution(13280545068582316414)
XLA Ops:
  0.7 224.8 %layer.1 = (bf16[384,768]{1,0:T(8,128)(2,1)}, f32[384,768]{1,0:T(8,128)}, f32[384,8]{1,0:T(8,128)}, bf16[4,640,128]{2,1,0:T(8,128)(2,1)}, bf16[8,96,2048]{2,1,0:T(8,128)(2,1)}, /*index=5*/bf16[8,128,768]{2,1,0:T(8,128)(2,1)}) custom-call(bf16[384,768]{1,0:T(8,128)(2,1)} %bitcast.19, bf16[384,768]{1,0:T(8,128)(2,1)} %bitcast.20, f32[3,96,768]{2,1,0:T(8,128)} %in_w.1, ...), custom_call_target="tpu_custom_call" | custom-call | tf_op jit(solution)/shard_map/layer/pallas_call | solution.py:1237
  225.5 1.6 copy.48
  227.1 0.0 copy-start.1
  227.1 0.0 copy-start
  227.1 24.9 %update.1 = (f32[3,96,768]{2,1,0:T(8,128)}, f32[3,96,768]{2,1,0:T(8,128)}, f32[3,96,768]{2,1,0:T(8,128)}, f32[96,768]{1,0:T(8,128)}, f32[96,768]{1,0:T(8,128)}, ...) custom-call(bf16[4,640,128]{2,1,0:T(8,128)(2,1)} %get-tuple-element., ...), custom_call_target="tpu_custom_call" | custom-call | tf_op jit(solution)/shard_map/update/pallas_call | solution.py:1333
  252.0 0.0 copy-done.1
  252.0 0.8 copy.51
  252.8 0.0 copy-done
  252.8 1.0 copy.52
Async XLA Ops:
  227.1 24.9 %copy-start.1 = (bf16[384,768]{1,0:T(8,128)(2,1)S(1)}, bf16[384,768]{1,0:T(8,128)(2,1)}, u32[]{:S(2)}) copy-start(bf16[384,768]{1,0:T(8,128)(2,1)} %get-tuple-element.45) | copy-start | bytes 1769476
  227.1 25.7 %copy-start = (f32[384,768]{1,0:T(8,128)S(1)}, f32[384,768]{1,0:T(8,128)}, u32[]{:S(2)}) copy-start(f32[384,768]{1,0:T(8,128)} %get-tuple-element.46) | copy-start | bytes 3538948

commit v4 on v3

--- a/solution.py
+++ b/solution.py
@@ -999,20 +999,21 @@
             for k in range(3):
                 al_copy(p, k).start()
 
+        line_step(1)
         pl.loop(0, 1)(one_head)
-        line_step(1)
         line_cross(0)
         pl.loop(1, 2)(one_head)
         grad_tiles(0, 2)
         ay_start(0)
         pair_start(3)
+        line_cross(1)
         pl.loop(2, LOCAL_HEADS)(one_head)
-        line_cross(1)
         for part in range(4):
             rows = slice(part * TOK, (part + 1) * TOK)
             gr[rows, 384:512] = jnp.concatenate([dv[0, rows, :], dv[1, rows, :]], axis=1)
             gr[rows, 512:640] = jnp.concatenate([dv[2, rows, :], jnp.zeros((TOK, 64), BF)], axis=1)
 
+        line_step(2)
         grad_tiles(2, 5)
         for k, (other, device) in enumerate(others):
             wo_share(k, q, device).wait_recv()
@@ -1050,7 +1051,6 @@
 
         ay_start(2)
         ay_end(0)
-        line_step(2)
         for a in range(2):
             gn_swap(a).wait_recv()
             bufs[a] = ((rowh, rowg)[a][pl.ds(4 * c, 4)].astype(F32) + part_in[a].astype(F32)).astype(BF)
@@ -1165,9 +1165,9 @@
     )
 
     line_other()
+    line_own()
     al_end(1)
     al_end(2)
-    line_own()
 
     for k in (1, 0):
         for n in range(2):
@@ -1263,8 +1263,8 @@
 def adam(weight, grad, first, second, rate, decay):
     first_new = MOMENT_DECAY * first + (1.0 - MOMENT_DECAY) * grad
     second_new = MOMENT_DECAY * second + (1.0 - MOMENT_DECAY) * grad * grad
-    correction = 1.0 - MOMENT_DECAY**STEP
-    update = first_new / correction / (jnp.sqrt(second_new / correction) + ADAM_EPSILON)
+    scale = 1.0 / (1.0 - MOMENT_DECAY**STEP)
+    update = (first_new * scale) / (jnp.sqrt(second_new * scale) + ADAM_EPSILON)
     return weight - rate * (update + decay * weight), first_new, second_new
 
 

time: 257 us -> 255 us (level)
  Pallas kernels: 250 us -> 247 us
where the time goes in v4:
time: 255 us; the launch traced here: 252 us
  Pallas kernels  247 us (97%)
  local copies, waits for them, and re-layouts  3.47 us (1%)
    pallas_call x1, Pallas kernels, layer_call(): pl.pallas_call(functools.partial(layer_kernel, inner), out_shape=[jax.Sha...  222 us
    pallas_call x1, Pallas kernels, update_call(): pl.pallas_call(update_kernel, grid=(NFFN,), out_shape=[jax.ShapeDtypeStru...  24.9 us

profile of v4, /device:TPU:0, one launch (start us, length us, event | category | flops | bytes accessed | tf_op | source)
XLA Modules:
  0.0 251.6 jit_solution(7289383522464296762)
XLA Ops:
  0.7 222.4 %layer.1 = (bf16[384,768]{1,0:T(8,128)(2,1)}, f32[384,768]{1,0:T(8,128)}, f32[384,8]{1,0:T(8,128)}, bf16[4,640,128]{2,1,0:T(8,128)(2,1)}, bf16[8,96,2048]{2,1,0:T(8,128)(2,1)}, /*index=5*/bf16[8,128,768]{2,1,0:T(8,128)(2,1)}) custom-call(bf16[384,768]{1,0:T(8,128)(2,1)} %bitcast.19, bf16[384,768]{1,0:T(8,128)(2,1)} %bitcast.20, f32[3,96,768]{2,1,0:T(8,128)} %in_w.1, ...), custom_call_target="tpu_custom_call" | custom-call | tf_op jit(solution)/shard_map/layer/pallas_call | solution.py:1237
  223.0 1.6 copy.48
  224.7 0.0 copy-start.1
  224.7 0.0 copy-start
  224.7 24.9 %update.1 = (f32[3,96,768]{2,1,0:T(8,128)}, f32[3,96,768]{2,1,0:T(8,128)}, f32[3,96,768]{2,1,0:T(8,128)}, f32[96,768]{1,0:T(8,128)}, f32[96,768]{1,0:T(8,128)}, ...) custom-call(bf16[4,640,128]{2,1,0:T(8,128)(2,1)} %get-tuple-element., ...), custom_call_target="tpu_custom_call" | custom-call | tf_op jit(solution)/shard_map/update/pallas_call | solution.py:1333
  249.5 0.0 copy-done.1
  249.5 0.8 copy.51
  250.4 0.0 copy-done
  250.4 1.0 copy.52
Async XLA Ops:
  224.7 24.9 %copy-start.1 = (bf16[384,768]{1,0:T(8,128)(2,1)S(1)}, bf16[384,768]{1,0:T(8,128)(2,1)}, u32[]{:S(2)}) copy-start(bf16[384,768]{1,0:T(8,128)(2,1)} %get-tuple-element.45) | copy-start | bytes 1769476
  224.7 25.7 %copy-start = (f32[384,768]{1,0:T(8,128)S(1)}, f32[384,768]{1,0:T(8,128)}, u32[]{:S(2)}) copy-start(f32[384,768]{1,0:T(8,128)} %get-tuple-element.46) | copy-start | bytes 3538948
